TPU v7x, 512 devices: a whole 4x4x16 slice. The times are simulated.
512 devices in a mesh: dp: 16 (over z), fsdp: 8 (over y, x_hi), tensor: 4 (over x_lo, core).
Axes of the slice: x: 4 (x_hi: 2, x_lo: 2; x = x_hi * 2 + x_lo), y: 4, z: 16, core: 2. Of those that a mesh axis runs over, the one named last changes fastest.
Arguments:
- tokens: bfloat16 [32768, 2560], P(('dp', 'fsdp')), may hold values from -6 to 6
- cotangent: bfloat16 [32768, 7168], P(('dp', 'fsdp'), 'tensor'), may hold values from -6 to 6
- weight: bfloat16 [2560, 7168], P(('dp', 'fsdp'), 'tensor'), may hold values from -0.125 to 0.125
- basis: bfloat16 [2560, 256], P(('dp', 'fsdp')), may hold values from -0.125 to 0.125
- first_moment: float32 [256, 7168], P(('dp', 'fsdp'), 'tensor'), may hold values from -0.0016572815 to 0.0016572815
- second_moment: float32 [256, 7168], P(('dp', 'fsdp'), 'tensor'), may hold values from 3.0517578e-07 to 6.1035156e-06
Outputs:
- token_grad: bfloat16 [32768, 2560], P(('dp', 'fsdp'))
- new_weight: bfloat16 [2560, 7168], P(('dp', 'fsdp'), 'tensor')
- new_first_moment: float32 [256, 7168], P(('dp', 'fsdp'), 'tensor')
- new_second_moment: float32 [256, 7168], P(('dp', 'fsdp'), 'tensor')
All inputs are finite; a program needn't handle non-finite values.
Results may differ from a plain program's by a relative error of at most 0.015.
Values may be sent and summed in bfloat16 or wider, within the bound.
No kernel may reach another device: no remote copies, remote signals or barrier semaphores. Data moves between devices by JAX's collectives and lax.ppermute only.
A program may use at most 64 MiB of HBM per device.

v0:
```python
import jax
import jax.numpy as jnp
from jax import lax
from jax.sharding import PartitionSpec as P

ADAM_STEP = 10


BETA_ONE = 0.9
BETA_TWO = 0.95
EPSILON = 1e-08
LEARN_RATE = 0.01


def silu_slope(preact):
    logistic = jax.nn.sigmoid(preact)
    return logistic * (1.0 + preact * (1.0 - logistic))


def local(tokens, cotangent, weight, basis, first_moment, second_moment):
    full_weight, full_basis = (
        lax.all_gather(weight, ("dp", "fsdp"), axis=0, tiled=True),
        lax.all_gather(basis, ("dp", "fsdp"), axis=0, tiled=True),
    )
    preact = jnp.dot(tokens, full_weight, preferred_element_type=jnp.float32)
    grad_pre = (cotangent.astype(jnp.float32) * silu_slope(preact)).astype(jnp.bfloat16)
    partial_rows = lax.dot_general(
        grad_pre, full_weight, (((1,), (1,)), ((), ())), preferred_element_type=jnp.float32
    )
    token_grad = lax.psum(partial_rows.astype(jnp.bfloat16), "tensor")
    projected = jnp.dot(tokens, full_basis, preferred_element_type=jnp.float32).astype(jnp.bfloat16)
    grad_part = lax.dot_general(
        projected, grad_pre, (((0,), (0,)), ((), ())), preferred_element_type=jnp.float32
    )
    outer_count = lax.axis_size("dp")
    inner_count = lax.axis_size("fsdp")
    reduced = lax.psum_scatter(grad_part, ("dp", "fsdp"), scatter_dimension=0, tiled=True)
    token_count = tokens.shape[0] * outer_count * inner_count
    grad_low = reduced / float(token_count)
    new_first_moment = BETA_ONE * first_moment + (1.0 - BETA_ONE) * grad_low
    new_second_moment = BETA_TWO * second_moment + (1.0 - BETA_TWO) * grad_low * grad_low
    first_hat = new_first_moment / (1.0 - BETA_ONE**ADAM_STEP)
    second_hat = new_second_moment / (1.0 - BETA_TWO**ADAM_STEP)
    direction = (first_hat / (jnp.sqrt(second_hat) + EPSILON)).astype(jnp.bfloat16)
    full_direction = lax.all_gather(direction, ("dp", "fsdp"), axis=0, tiled=True)
    update = jnp.dot(basis, full_direction, preferred_element_type=jnp.float32)
    new_weight = (weight.astype(jnp.float32) - LEARN_RATE * update).astype(jnp.bfloat16)
    return (token_grad, new_weight, new_first_moment, new_second_moment)


def solution(mesh):
    in_specs = (
        P(("dp", "fsdp"), None),
        P(("dp", "fsdp"), "tensor"),
        P(("dp", "fsdp"), "tensor"),
        P(("dp", "fsdp"), None),
        P(("dp", "fsdp"), "tensor"),
        P(("dp", "fsdp"), "tensor"),
    )
    out_specs = (
        P(("dp", "fsdp"), None),
        P(("dp", "fsdp"), "tensor"),
        P(("dp", "fsdp"), "tensor"),
        P(("dp", "fsdp"), "tensor"),
    )
    return jax.shard_map(local, mesh=mesh, in_specs=in_specs, out_specs=out_specs, check_vma=False)
```

profile of v0, /device:TPU:2, one launch (start us, length us, event | category | flops | bytes accessed | tf_op | source)
XLA Modules:
  0.0 2225.4 jit_solution(3341464761759724895)
XLA Ops:
  7.2 0.0 copy-start
  7.2 0.0 all-gather.8.cloned.1.call-start
  7.2 0.7 all-gather.8.cloned.1.call-update
  7.9 0.0 all-gather.6.cloned.1.call-start
  8.0 0.7 all-gather.6.cloned.1.call-update
  8.7 0.0 all-reduce.6.cloned.1.call-start
  8.7 205.9 %all-gather.8.cloned.1.call-done = bf16[128,20,256]{2,1,0:T(8,128)(2,1)} async-done(((bf16[1,20,256]{2,1,0:T(8,128)(2,1)}), bf16[128,20,256]{2,1,0:T(8,128)(2,1)}) %all-gather.8.cloned.1.call-update) | async-done | bytes 1310736 | tf_op jit(solution)/shard_map/all_gather | solution.py:23
  214.6 2.3 reshape.11
  216.9 257.5 %all-gather.6.cloned.1.call-done = bf16[128,20,1792]{2,1,0:T(8,128)(2,1)} async-done(((bf16[1,20,1792]{2,1,0:T(8,128)(2,1)}), bf16[128,20,1792]{2,1,0:T(8,128)(2,1)}) %all-gather.6.cloned.1.call-update) | async-done | bytes 9175056 | tf_op jit(solution)/shard_map/all_gather | solution.py:22
  474.4 13.2 reshape.9
  487.6 0.0 copy-done
  487.6 0.0 copy-start.5
  487.6 7.5 fusion.12
  495.1 0.0 copy-done.5
  495.1 4.3 fusion.3
  499.4 0.0 all-reduce.6.cloned.1.call-update
  499.4 0.0 copy-start.3
  499.5 0.0 copy-start.4
  499.5 0.0 all-reduce.4.cloned.1.call-start
  499.5 8.0 convolution_convert_fusion
  507.5 0.0 all-reduce.4.cloned.1.call-update
  507.6 1.3 dynamic-slice
  509.5 1347.9 %all-reduce.6.cloned.1.call-done = f32[256,1792]{1,0:T(8,128)} async-done(((f32[256,1792]{1,0:T(8,128)}), f32[256,1792]{1,0:T(8,128)}) %all-reduce.6.cloned.1.call-update) | async-done | bytes 1835024
  1857.4 0.0 copy-done.3
  1857.4 0.0 copy-done.4
  1857.4 1.5 fusion.9
  1858.9 356.3 %all-gather.2 = bf16[128,2,1792]{2,1,0:T(2,128)(2,1)S(1)} all-gather(bf16[1,2,1792]{2,1,0:T(2,128)(2,1)S(1)} %get-tuple-element.4), channel_id=1, replica_groups=mesh['dp'=16,'fsdp'=8,'tensor'=4] {'dp','fsdp'}, dimensions={0}, use_global_device_ids=true | all-gather | bytes 924672 | tf_op jit(solution)/shard_map/all_gather | solution.py:45
  2215.2 0.3 reshape.13
  2215.5 0.0 copy-done.1
  2215.5 0.0 copy-done.2
  2215.5 0.9 fusion.2
  2216.4 2.5 copy.12
  (3 shorter events, 0.0 us)
Async XLA Ops:
  7.2 480.4 %copy-start = (bf16[256,2560]{1,0:T(8,128)(2,1)S(1)}, bf16[256,2560]{1,0:T(8,128)(2,1)}, u32[]{:S(2)}) copy-start(bf16[256,2560]{1,0:T(8,128)(2,1)} %param.6) | copy-start | bytes 3932164
  7.2 207.5 %all-gather.8.cloned.1.call-start = ((), (), s32[]{:S(2)}) async-start(), calls=%async_computation.2 | async-start | bytes 1585152 | tf_op jit(solution)/shard_map/all_gather | solution.py:23
  7.9 466.5 %all-gather.6.cloned.1.call-start = ((), (), s32[]{:S(2)}) async-start(), calls=%async_computation.1 | async-start | bytes 11096064 | tf_op jit(solution)/shard_map/all_gather | solution.py:22
  8.7 1848.8 %all-reduce.6.cloned.1.call-start = ((), (), s32[]{:S(2)}) async-start(), calls=%async_computation.3 | async-start | bytes 3670016
  487.6 7.5 copy-start.5
  499.4 1358.0 %copy-start.3 = (f32[2,1792]{1,0:T(2,128)S(1)}, f32[2,1792]{1,0:T(2,128)}, u32[]{:S(2)}) copy-start(f32[2,1792]{1,0:T(2,128)} %param.10) | copy-start | bytes 43012
  499.5 1358.0 %copy-start.4 = (f32[2,1792]{1,0:T(2,128)S(1)}, f32[2,1792]{1,0:T(2,128)}, u32[]{:S(2)}) copy-start(f32[2,1792]{1,0:T(2,128)} %param.11) | copy-start | bytes 43012
  499.5 1717.0 %all-reduce.4.cloned.1.call-start = ((), (), s32[]{:S(2)}) async-start(), calls=%async_computation | async-start | bytes 2621440 | tf_op jit(solution)/shard_map/psum | solution.py:30
  507.5 1708.0 %copy-start.1 = (bf16[20,1792]{1,0:T(8,128)(2,1)S(1)}, bf16[20,1792]{1,0:T(8,128)(2,1)}, u32[]{:S(2)}) copy-start(bf16[20,1792]{1,0:T(8,128)(2,1)} %param.8) | copy-start | bytes 215044
  507.5 1708.0 %copy-start.2 = (bf16[20,256]{1,0:T(8,128)(2,1)S(1)}, bf16[20,256]{1,0:T(8,128)(2,1)}, u32[]{:S(2)}) copy-start(bf16[20,256]{1,0:T(8,128)(2,1)} %param.9) | copy-start | bytes 30724
Sparse Core Ops, SparseCore 0:
  12.3 202.3 all-gather.7
  219.2 255.1 all-gather.5
  499.6 1357.8 all-reduce.5
  1861.1 57.8 all-reduce.3
where the time goes:
time: 2230 us
  waiting for transfers between devices  1810 us (81%)
  blocking collectives  356 us (16%)
    unnamed x5, waiting for transfers between devices  1350 us
    all_gather x1, blocking collectives, local(): lax.all_gather(direction, ('dp', 'fsdp'), axis=0, tiled=True)  356 us
    all_gather x1, waiting for transfers between devices, local(): lax.all_gather(weight, ('dp', 'fsdp'), axis=0, tiled=True)  257 us
    all_gather x1, waiting for transfers between devices, local(): lax.all_gather(basis, ('dp', 'fsdp'), axis=0, tiled=True)  206 us
  transfers between devices with their start and end apart: 4, of which 3 were waited for; matrix products, arithmetic and copies ran while one was open for 1% of the time, Pallas kernels for 0%

commit v1 on v0

v1 whole, which is shorter than its diff:
```python
import jax
import jax.numpy as jnp
from jax import lax
from jax.sharding import PartitionSpec as P

ADAM_STEP = 10


BETA_ONE = 0.9
BETA_TWO = 0.95
EPSILON = 1e-08
LEARN_RATE = 0.01


def silu_slope(preact):
    logistic = jax.nn.sigmoid(preact)
    return logistic * (1.0 + preact * (1.0 - logistic))


def spread(block, axis):
    count = lax.axis_size(axis)
    copies = jnp.broadcast_to(block[None], (count,) + block.shape)
    return lax.all_to_all(copies, axis, 0, 0, tiled=True)


def local(tokens, cotangent, weight, basis, first_moment, second_moment):
    f32, bf16 = jnp.float32, jnp.bfloat16
    outer, inner, quarters = lax.axis_size("dp"), lax.axis_size("fsdp"), lax.axis_size("tensor")
    rows, width = weight.shape
    rank = basis.shape[1]
    share = rank // (outer * inner)
    basis_perm = basis.reshape(rows, outer, inner, share).transpose(0, 2, 1, 3).reshape(rows, rank)
    part = rank // quarters
    basis_part = lax.dynamic_slice_in_dim(basis_perm, lax.axis_index("tensor") * part, part, 1)

    weight_plane = spread(weight, "fsdp").reshape(inner * rows, width)
    full_weight = lax.all_gather(weight_plane, "dp", axis=0, tiled=True)
    basis_plane = spread(basis_part, "fsdp").reshape(inner * rows, part)
    full_basis = spread(basis_plane, "dp").reshape(outer * inner * rows, part)
    projected_part = lax.dot_general(
        full_basis, tokens, (((0,), (1,)), ((), ())), preferred_element_type=f32
    ).astype(bf16)
    projected = spread(projected_part, "tensor").reshape(rank, tokens.shape[0])

    preact = jnp.dot(tokens, full_weight, preferred_element_type=f32)
    grad_pre = (cotangent.astype(f32) * silu_slope(preact)).astype(bf16)
    grad_part = jnp.dot(projected, grad_pre, preferred_element_type=f32).astype(bf16)
    partial_rows = lax.dot_general(
        grad_pre, full_weight, (((1,), (1,)), ((), ())), preferred_element_type=f32
    )
    token_grad = lax.psum(partial_rows.astype(bf16), "tensor")

    landed = lax.all_to_all(grad_part.reshape(inner, outer * share, width), "fsdp", 0, 0, tiled=True)
    inner_sum = jnp.sum(landed.astype(f32), axis=0)
    landed = lax.all_to_all(inner_sum.reshape(outer, share, width), "dp", 0, 0, tiled=True)
    reduced = jnp.sum(landed, axis=0)

    token_count = tokens.shape[0] * outer * inner
    grad_low = reduced / float(token_count)
    new_first_moment = BETA_ONE * first_moment + (1.0 - BETA_ONE) * grad_low
    new_second_moment = BETA_TWO * second_moment + (1.0 - BETA_TWO) * grad_low * grad_low
    first_hat = new_first_moment / (1.0 - BETA_ONE**ADAM_STEP)
    second_hat = new_second_moment / (1.0 - BETA_TWO**ADAM_STEP)
    direction = (first_hat / (jnp.sqrt(second_hat) + EPSILON)).astype(bf16)
    column = spread(direction, "dp").reshape(outer * share, width)
    full_direction = spread(column, "fsdp").reshape(rank, width)
    update = jnp.dot(basis_perm, full_direction, preferred_element_type=f32)
    new_weight = (weight.astype(f32) - LEARN_RATE * update).astype(bf16)
    return (token_grad, new_weight, new_first_moment, new_second_moment)


def solution(mesh):
    in_specs = (
        P(("dp", "fsdp"), None),
        P(("dp", "fsdp"), "tensor"),
        P(("dp", "fsdp"), "tensor"),
        P(("dp", "fsdp"), None),
        P(("dp", "fsdp"), "tensor"),
        P(("dp", "fsdp"), "tensor"),
    )
    out_specs = (
        P(("dp", "fsdp"), None),
        P(("dp", "fsdp"), "tensor"),
        P(("dp", "fsdp"), "tensor"),
        P(("dp", "fsdp"), "tensor"),
    )
    return jax.shard_map(local, mesh=mesh, in_specs=in_specs, out_specs=out_specs, check_vma=False)
```

time: 2230 us -> 307 us (0.14)
  the two profiles are of different devices: /device:TPU:2 before, /device:TPU:1 now
where the time goes in v1:
time: 307 us
  blocking collectives  129 us (42%)
  waiting for transfers between devices  116 us (38%)
  starting transfers between devices  19.7 us (6%)
  matrix products  19.3 us (6%)
  between operations  14.2 us (5%)
  local copies, waits for them, and re-layouts  7.77 us (3%)
    all_to_all x4, blocking collectives, spread(): return lax.all_to_all(copies, axis, 0, 0, tiled=True)  86.8 us
    all_gather x1, waiting for transfers between devices, local(): full_weight = lax.all_gather(weight_plane, 'dp', axis=0, tiled=True)  71.4 us
    psum x1, waiting for transfers between devices, local(): token_grad = lax.psum(partial_rows.astype(bf16), 'tensor')  40.6 us
    all_to_all x1, blocking collectives, local(): lax.all_to_all(grad_part.reshape(inner, outer * share, width), 'fsdp', 0,...  21.1 us
    all_to_all x1, blocking collectives, local(): lax.all_to_all(inner_sum.reshape(outer, share, width), 'dp', 0, 0, tiled=...  21 us
    all_to_all x2, starting transfers between devices, spread(): return lax.all_to_all(copies, axis, 0, 0, tiled=True)  19.6 us
    dot_general x1, matrix products, local(): lax.dot_general(grad_pre, full_weight, (((1,), (1,)), ((), ())), preferre...  8.01 us
    dot_general x1, matrix products, local(): preact = jnp.dot(tokens, full_weight, preferred_element_type=f32)  7.38 us
  transfers between devices with their start and end apart: 4, of which 3 were waited for; matrix products, arithmetic and copies ran while one was open for 6% of the time, Pallas kernels for 0%

profile of v1, /device:TPU:1, one launch (start us, length us, event | category | flops | bytes accessed | tf_op | source)
XLA Modules:
  0.0 306.5 jit_solution(1933529780850597187)
XLA Ops:
  7.2 1.0 broadcast_in_dim.16
  8.3 18.6 %all_to_all.40 = bf16[8,20,1792]{2,1,0:T(8,128)(2,1)S(1)} all-to-all(bf16[8,20,1792]{2,1,0:T(8,128)(2,1)S(1)} %broadcast_in_dim.16), channel_id=1, replica_groups=mesh['dp'=16,'fsdp'=8,'tensor'=4] {'fsdp'}, dimensions={0} | all-to-all | bytes 1146880 | tf_op jit(solution)/shard_map/all_to_all | solution.py:23
  26.9 0.9 reshape.38
  27.9 0.1 copy.27
  28.1 0.1 copy.29
  28.2 0.1 reshape.46
  28.3 9.1 %all_to_all.41 = bf16[8,2,640]{2,1,0:T(2,128)(2,1)S(1)} all-to-all(bf16[8,2,640]{2,1,0:T(2,128)(2,1)S(1)} %reshape.46), channel_id=1, replica_groups=mesh['dp'=16,'fsdp'=8,'tensor'=4] {'fsdp'}, dimensions={0} | all-to-all | bytes 40960 | tf_op jit(solution)/shard_map/all_to_all | solution.py:23
  37.4 0.1 reshape.47
  37.6 0.1 copy.30
  37.7 44.5 %all_to_all.42 = bf16[16,160,64]{1,2,0:T(8,128)(2,1)S(1)} all-to-all(bf16[16,160,64]{1,2,0:T(8,128)(2,1)S(1)} %broadcast_in_dim.19), channel_id=1, replica_groups=mesh['dp'=16,'fsdp'=8,'tensor'=4] {'dp'}, dimensions={0} | all-to-all | bytes 655360 | tf_op jit(solution)/shard_map/all_to_all | solution.py:23
  82.2 0.3 copy.31
  82.5 0.7 reshape.41
  83.3 0.5 convolution_convert_fusion.2
  83.8 0.7 broadcast_in_dim.20
  84.5 11.0 %all-to-all-start.3 = ((bf16[4,64,256]{2,1,0:T(8,128)(2,1)}), bf16[4,64,256]{2,1,0:T(8,128)(2,1)S(1)}, u32[]{:S(2)}, u32[]{:S(2)}) async-start(bf16[4,64,256]{2,1,0:T(8,128)(2,1)} %broadcast_in_dim.20), calls=%async_computation.3 | async-start | bytes 262144 | tf_op jit(solution)/shard_map/all_to_all | solution.py:23
  95.5 71.4 %all-gather.2.cloned.1.call-done = bf16[2560,1792]{1,0:T(8,128)(2,1)} async-done(((bf16[160,1792]{1,0:T(8,128)(2,1)}), bf16[2560,1792]{1,0:T(8,128)(2,1)}) %all-gather.2.cloned.1.call-update) | async-done | bytes 9175056 | tf_op jit(solution)/shard_map/all_gather | solution.py:37
  166.9 7.4 %fusion.10 = f32[256,1792]{1,0:T(8,128)} fusion(bf16[256,2560]{1,0:T(8,128)(2,1)S(1)} %copy-done, bf16[2560,1792]{1,0:T(8,128)(2,1)} %all-gather.2.cloned.1.call-done), kind=kOutput, calls=%fused_computation.20 | convolution fusion | flops 2348810240 | bytes 12320768 | tf_op jit(solution)/shard_map/dot_general | solution.py:45
  174.3 2.5 convolution_convert_fusion.1
  176.8 21.1 %all_to_all.43 = bf16[8,32,1792]{2,1,0:T(8,128)(2,1)S(1)} all-to-all(bf16[8,32,1792]{2,1,0:T(8,128)(2,1)S(1)} %bitcast.24), channel_id=1, replica_groups=mesh['dp'=16,'fsdp'=8,'tensor'=4] {'fsdp'}, dimensions={0} | all-to-all | bytes 1835008 | tf_op jit(solution)/shard_map/all_to_all | solution.py:53
  197.9 0.1 convert_reduce_fusion
  198.0 0.1 reshape.44
  198.2 21.0 %all_to_all.44 = f32[16,2,1792]{2,1,0:T(2,128)S(1)} all-to-all(f32[16,2,1792]{2,1,0:T(2,128)S(1)} %reshape.44), channel_id=1, replica_groups=mesh['dp'=16,'fsdp'=8,'tensor'=4] {'dp'}, dimensions={0} | all-to-all | bytes 458752 | tf_op jit(solution)/shard_map/all_to_all | solution.py:55
  219.1 0.1 reduce_sum.19
  219.2 0.6 fusion.7
  219.9 0.7 broadcast_in_dim.21
  220.6 8.6 %all-to-all-start.6 = ((bf16[16,2,1792]{2,1,0:T(2,128)(2,1)}), bf16[16,2,1792]{2,1,0:T(2,128)(2,1)S(1)}, u32[]{:S(2)}, u32[]{:S(2)}) async-start(bf16[16,2,1792]{2,1,0:T(2,128)(2,1)} %broadcast_in_dim.21), calls=%async_computation.6 | async-start | bytes 229376 | tf_op jit(solution)/shard_map/all_to_all | solution.py:23
  229.2 8.0 %convolution_convert_fusion = bf16[256,2560]{1,0:T(8,128)(2,1)} fusion(bf16[2560,1792]{1,0:T(8,128)(2,1)} %all-gather.2.cloned.1.call-done, f32[256,1792]{1,0:T(8,128)} %fusion.10, bf16[256,1792]{1,0:T(8,128)(2,1)S(1)} %copy-done.5), kind=kOutput, calls=%fused_computation | convolution fusion | flops 2354053120 | bytes 13238272 | tf_op jit(solution)/shard_map/dot_general | solution.py:48
  237.3 3.8 %all-to-all-done.6 = bf16[16,2,1792]{2,1,0:T(2,128)(2,1)S(1)} async-done(((bf16[16,2,1792]{2,1,0:T(2,128)(2,1)}), bf16[16,2,1792]{2,1,0:T(2,128)(2,1)S(1)}, u32[]{:S(2)}, u32[]{:S(2)}) %all-to-all-start.6) | async-done | bytes 114720 | tf_op jit(solution)/shard_map/all_to_all | solution.py:23
  241.2 14.5 %all_to_all.45 = bf16[8,32,1792]{2,1,0:T(8,128)(2,1)S(1)} all-to-all(bf16[8,32,1792]{2,1,0:T(8,128)(2,1)S(1)} %broadcast_in_dim.45), channel_id=1, replica_groups=mesh['dp'=16,'fsdp'=8,'tensor'=4] {'fsdp'}, dimensions={0} | all-to-all | bytes 1835008 | tf_op jit(solution)/shard_map/all_to_all | solution.py:23
  255.7 0.9 fusion.2
  256.7 40.6 %all-reduce.2.cloned.1.call-done = bf16[256,2560]{1,0:T(8,128)(2,1)} async-done(((bf16[256,2560]{1,0:T(8,128)(2,1)}), bf16[256,2560]{1,0:T(8,128)(2,1)}) %all-reduce.2.cloned.1.call-update) | async-done | bytes 1310736 | tf_op jit(solution)/shard_map/psum | solution.py:51
  297.2 2.5 copy.35
  (24 shorter events, 0.4 us)
Async XLA Ops:
  7.2 76.1 %copy-start = (bf16[256,2560]{1,0:T(8,128)(2,1)S(1)}, bf16[256,2560]{1,0:T(8,128)(2,1)}, u32[]{:S(2)}) copy-start(bf16[256,2560]{1,0:T(8,128)(2,1)} %param.6) | copy-start | bytes 3932164
  7.2 20.7 %copy-start.4 = (bf16[20,256]{1,0:T(8,128)(2,1)S(1)}, bf16[20,256]{1,0:T(8,128)(2,1)}, u32[]{:S(2)}) copy-start(bf16[20,256]{1,0:T(8,128)(2,1)} %param.9) | copy-start | bytes 30724
  7.2 159.7 %all-gather.2.cloned.1.call-start = ((), (), s32[]{:S(2)}) async-start(), calls=%async_computation.8 | async-start | bytes 9748480 | tf_op jit(solution)/shard_map/all_gather | solution.py:37
  84.5 89.8 %all-to-all-start.3 = ((bf16[4,64,256]{2,1,0:T(8,128)(2,1)}), bf16[4,64,256]{2,1,0:T(8,128)(2,1)S(1)}, u32[]{:S(2)}, u32[]{:S(2)}) async-start(bf16[4,64,256]{2,1,0:T(8,128)(2,1)} %broadcast_in_dim.20), calls=%async_computation.3 | async-start | bytes 262144 | tf_op jit(solution)/shard_map/all_to_all | solution.py:23
  95.5 78.8 %copy-start.5 = (bf16[256,1792]{1,0:T(8,128)(2,1)S(1)}, bf16[256,1792]{1,0:T(8,128)(2,1)}, u32[]{:S(2)}) copy-start(bf16[256,1792]{1,0:T(8,128)(2,1)} %param.7) | copy-start | bytes 2752516
  176.8 42.5 %copy-start.2 = (f32[2,1792]{1,0:T(2,128)S(1)}, f32[2,1792]{1,0:T(2,128)}, u32[]{:S(2)}) copy-start(f32[2,1792]{1,0:T(2,128)} %param.10) | copy-start | bytes 43012
  176.8 42.5 %copy-start.3 = (f32[2,1792]{1,0:T(2,128)S(1)}, f32[2,1792]{1,0:T(2,128)}, u32[]{:S(2)}) copy-start(f32[2,1792]{1,0:T(2,128)} %param.11) | copy-start | bytes 43012
  220.6 20.5 %all-to-all-start.6 = ((bf16[16,2,1792]{2,1,0:T(2,128)(2,1)}), bf16[16,2,1792]{2,1,0:T(2,128)(2,1)S(1)}, u32[]{:S(2)}, u32[]{:S(2)}) async-start(bf16[16,2,1792]{2,1,0:T(2,128)(2,1)} %broadcast_in_dim.21), calls=%async_computation.6 | async-start | bytes 229376 | tf_op jit(solution)/shard_map/all_to_all | solution.py:23
  229.2 68.1 %all-reduce.2.cloned.1.call-start = ((), (), s32[]{:S(2)}) async-start(), calls=%async_computation.9 | async-start | bytes 2621440 | tf_op jit(solution)/shard_map/psum | solution.py:51
  237.3 18.5 %copy-start.1 = (bf16[20,1792]{1,0:T(8,128)(2,1)S(1)}, bf16[20,1792]{1,0:T(8,128)(2,1)}, u32[]{:S(2)}) copy-start(bf16[20,1792]{1,0:T(8,128)(2,1)} %param.8) | copy-start | bytes 215044
Sparse Core Ops, SparseCore 0:
  28.0 138.8 all-gather.1
  237.4 59.8 all-reduce.1

commit v2 on v1

--- a/solution.py
+++ b/solution.py
@@ -10,6 +10,8 @@
 BETA_TWO = 0.95
 EPSILON = 1e-08
 LEARN_RATE = 0.01
+RING = 4
+PAIR = 2
 
 
 def silu_slope(preact):
@@ -17,10 +19,26 @@
     return logistic * (1.0 + preact * (1.0 - logistic))
 
 
-def spread(block, axis):
+def spread(block, axis, groups=None):
+    count = lax.axis_size(axis) if groups is None else len(groups[0])
+    copies = jnp.broadcast_to(block[None], (count,) + block.shape)
+    return lax.all_to_all(copies, axis, 0, 0, tiled=True, axis_index_groups=groups)
+
+
+def ring_of_four(block, axis, step, place):
     count = lax.axis_size(axis)
-    copies = jnp.broadcast_to(block[None], (count,) + block.shape)
-    return lax.all_to_all(copies, axis, 0, 0, tiled=True)
+    ahead = [((i + step) % count, i) for i in range(count)]
+    behind = [(i, (i + step) % count) for i in range(count)]
+    half = block.shape[0] // 2
+    following = lax.ppermute(block, axis, ahead)
+    preceding = lax.ppermute(block, axis, behind)
+    far_front = lax.ppermute(following[:half], axis, ahead)
+    far_back = lax.ppermute(preceding[half:], axis, behind)
+    far = jnp.concatenate([far_front, far_back], axis=0)
+    stacked = jnp.stack([block, following, far, preceding])
+    return lambda wanted: lax.dynamic_index_in_dim(
+        stacked, lax.rem(wanted - place + RING, RING), 0, keepdims=False
+    )
 
 
 def local(tokens, cotangent, weight, basis, first_moment, second_moment):
@@ -28,31 +46,54 @@
     outer, inner, quarters = lax.axis_size("dp"), lax.axis_size("fsdp"), lax.axis_size("tensor")
     rows, width = weight.shape
     rank = basis.shape[1]
+    depth = outer * inner * rows
     share = rank // (outer * inner)
     basis_perm = basis.reshape(rows, outer, inner, share).transpose(0, 2, 1, 3).reshape(rows, rank)
     part = rank // quarters
     basis_part = lax.dynamic_slice_in_dim(basis_perm, lax.axis_index("tensor") * part, part, 1)
 
-    weight_plane = spread(weight, "fsdp").reshape(inner * rows, width)
-    full_weight = lax.all_gather(weight_plane, "dp", axis=0, tiled=True)
-    basis_plane = spread(basis_part, "fsdp").reshape(inner * rows, part)
-    full_basis = spread(basis_plane, "dp").reshape(outer * inner * rows, part)
+    pairs = [[PAIR * y + x for x in range(PAIR)] for y in range(RING)]
+    columns = [[PAIR * y + x for y in range(RING)] for x in range(PAIR)]
+    strides = [[i + RING * j for j in range(outer // RING)] for i in range(RING)]
+    pair_rows = PAIR * rows
+    both = jnp.concatenate([weight, basis_part], axis=1)
+    block = spread(both, "fsdp", pairs).reshape(pair_rows, width + part)
+    half = width // 2
+    plane = spread(block[:, :half], "fsdp", columns).reshape(inner * rows, half)
+    weight_a = lax.all_gather(plane, "dp", axis=0, tiled=True)
+    second = block[:, half:]
+    strided = spread(second, "dp", strides)
+    place = lax.rem(lax.axis_index("dp"), RING)
+    pick = ring_of_four(strided, "dp", 1, place)
+    line = jnp.stack([pick(r) for r in range(RING)], axis=1).reshape(outer, pair_rows, half + part)
+    pick = ring_of_four(line, "fsdp", PAIR, lax.axis_index("fsdp") // PAIR)
+    full_b = jnp.stack([pick(r) for r in range(RING)], axis=1).reshape(depth, half + part)
+    weight_b, full_basis = full_b[:, :half], full_b[:, half:]
+
     projected_part = lax.dot_general(
         full_basis, tokens, (((0,), (1,)), ((), ())), preferred_element_type=f32
     ).astype(bf16)
     projected = spread(projected_part, "tensor").reshape(rank, tokens.shape[0])
 
-    preact = jnp.dot(tokens, full_weight, preferred_element_type=f32)
-    grad_pre = (cotangent.astype(f32) * silu_slope(preact)).astype(bf16)
-    grad_part = jnp.dot(projected, grad_pre, preferred_element_type=f32).astype(bf16)
-    partial_rows = lax.dot_general(
-        grad_pre, full_weight, (((1,), (1,)), ((), ())), preferred_element_type=f32
-    )
-    token_grad = lax.psum(partial_rows.astype(bf16), "tensor")
+    grad_pre, grad_part = [], []
+    for index, side in enumerate((weight_a, weight_b)):
+        preact = jnp.dot(tokens, side, preferred_element_type=f32)
+        wanted = cotangent[:, index * half : (index + 1) * half].astype(f32)
+        grad_pre.append((wanted * silu_slope(preact)).astype(bf16))
+        grad_part.append(jnp.dot(projected, grad_pre[-1], preferred_element_type=f32).astype(bf16))
+    grad_part = jnp.concatenate(grad_part, axis=1)
+    partial_rows = sum(
+        lax.dot_general(g, w, (((1,), (1,)), ((), ())), preferred_element_type=f32)
+        for g, w in zip(grad_pre, (weight_a, weight_b))
+    ).astype(bf16)
 
     landed = lax.all_to_all(grad_part.reshape(inner, outer * share, width), "fsdp", 0, 0, tiled=True)
+    landed, partial_rows = lax.optimization_barrier((landed, partial_rows))
+    token_rows = lax.psum_scatter(partial_rows, "tensor", scatter_dimension=0, tiled=True)
     inner_sum = jnp.sum(landed.astype(f32), axis=0)
     landed = lax.all_to_all(inner_sum.reshape(outer, share, width), "dp", 0, 0, tiled=True)
+    landed, token_rows = lax.optimization_barrier((landed, token_rows))
+    token_grad = lax.all_gather(token_rows, "tensor", axis=0, tiled=True)
     reduced = jnp.sum(landed, axis=0)
 
     token_count = tokens.shape[0] * outer * inner

time: 307 us -> 270 us (0.88)
  the two profiles are of different devices: /device:TPU:1 before, /device:TPU:32 now
where the time goes in v2:
time: 270 us; the launch traced here: 269 us
  blocking collectives  131 us (49%)
  waiting for transfers between devices  55.4 us (21%)
  starting transfers between devices  30.3 us (11%)
  matrix products  19.3 us (7%)
  between operations  14.3 us (5%)
  local copies, waits for them, and re-layouts  12.8 us (5%)
  other arithmetic  6.03 us (2%)
    all_to_all x5, blocking collectives, spread(): lax.all_to_all(copies, axis, 0, 0, tiled=True, axis_index_groups=groups)  107 us
    ppermute x2, waiting for transfers between devices, ring_of_four(): following = lax.ppermute(block, axis, ahead)  33 us
    all_to_all x1, blocking collectives, local(): lax.all_to_all(inner_sum.reshape(outer, share, width), 'dp', 0, 0, tiled=...  24.2 us
    dot_general x2, matrix products, local(): lax.dot_general(g, w, (((1,), (1,)), ((), ())), preferred_element_type=f32)  9.36 us
    ppermute x2, waiting for transfers between devices, ring_of_four(): far_front = lax.ppermute(following[:half], axis, ahead)  7.69 us
    unnamed x30, local copies, waits for them, and re-layouts  7.63 us
    dot_general x2, matrix products, local(): preact = jnp.dot(tokens, side, preferred_element_type=f32)  7.53 us
    ppermute x2, waiting for transfers between devices, ring_of_four(): far_back = lax.ppermute(preceding[half:], axis, behind)  7.43 us
  transfers between devices with their start and end apart: 13, of which 8 were waited for; matrix products, arithmetic and copies ran while one was open for 9% of the time, Pallas kernels for 0%

profile of v2, /device:TPU:32, one launch (start us, length us, event | category | flops | bytes accessed | tf_op | source)
XLA Modules:
  0.0 269.1 jit_solution(10377256479225364142)
XLA Ops:
  9.3 10.4 %all_to_all.40 = bf16[2,20,1856]{2,1,0:T(8,128)(2,1)S(1)} all-to-all(bf16[2,20,1856]{2,1,0:T(8,128)(2,1)S(1)} %broadcast_in_dim.14), channel_id=1, replica_groups={{0,4},{8,12},{16,20},{24,28},{1,5},{9,13},{17,21},{25,29},{2,6},{10,14}..., dimensions={0} | all-to-all | bytes 296960 | tf_op jit(solution)/shard_map/all_to_all | solution.py:25
  19.7 11.2 %all_to_all.41 = bf16[4,40,896]{2,1,0:T(8,128)(2,1)} all-to-all(bf16[4,40,896]{2,1,0:T(8,128)(2,1)S(1)} %broadcast_in_dim.17), channel_id=1, replica_groups={{0,8,16,24},{4,12,20,28},{1,9,17,25},{5,13,21,29},{2,10,18,26},{6,14,22..., dimensions={0} | all-to-all | bytes 573440 | tf_op jit(solution)/shard_map/all_to_all | solution.py:25
  31.0 39.8 %all_to_all.42 = bf16[4,40,960]{2,1,0:T(8,128)(2,1)S(1)} all-to-all(bf16[4,40,960]{2,1,0:T(8,128)(2,1)S(1)} %broadcast_in_dim.15), channel_id=1, replica_groups={{0,128,256,384},{32,160,288,416},{64,192,320,448},{96,224,352,480},{1,1..., dimensions={0} | all-to-all | bytes 614400 | tf_op jit(solution)/shard_map/all_to_all | solution.py:25
  70.8 1.9 collective-permute-start
  72.7 3.9 %collective-permute-start.2 = (bf16[4,40,960]{2,1,0:T(8,128)(2,1)S(1)}, bf16[4,40,960]{2,1,0:T(8,128)(2,1)S(1)}, u32[]{:S(2)}, u32[]{:S(2)}) collective-permute-start(bf16[4,40,960]{2,1,0:T(8,128)(2,1)S(1)} %all_to_all.42), channel_id=1, source_target_pairs={{0,32},{32,64},{64,96},{96,128},{128,160},{160,192},{192,224},{224... | collective-permute-start | bytes 921608 | tf_op jit(solution)/shard_map/ppermute | solution.py:34
  76.6 11.2 %collective-permute-done = bf16[4,40,960]{2,1,0:T(8,128)(2,1)S(1)} collective-permute-done((bf16[4,40,960]{2,1,0:T(8,128)(2,1)S(1)}, bf16[4,40,960]{2,1,0:T(8,128)(2,1)S(1)}, u32[]{:S(2)}, u32[]{:S(2)}) %collective-permute-start) | collective-permute-done | bytes 307232 | tf_op jit(solution)/shard_map/ppermute | solution.py:33
  87.8 1.9 collective-permute-start.1
  89.8 3.9 %collective-permute-start.3 = (bf16[2,40,960]{2,1,0:T(8,128)(2,1)S(1)}, bf16[2,40,960]{2,1,0:T(8,128)(2,1)S(1)}, u32[]{:S(2)}, u32[]{:S(2)}) collective-permute-start(bf16[2,40,960]{2,1,0:T(8,128)(2,1)S(1)} %slice.42), channel_id=1, source_target_pairs={{0,32},{32,64},{64,96},{96,128},{128,160},{160,192},{192,224},{224... | collective-permute-start | bytes 460808 | tf_op jit(solution)/shard_map/ppermute | solution.py:36
  93.7 4.6 %collective-permute-done.1 = bf16[2,40,960]{2,1,0:T(8,128)(2,1)S(1)} collective-permute-done((bf16[2,40,960]{2,1,0:T(8,128)(2,1)S(1)}, bf16[2,40,960]{2,1,0:T(8,128)(2,1)S(1)}, u32[]{:S(2)}, u32[]{:S(2)}) %collective-permute-start.1) | collective-permute-done | bytes 153632 | tf_op jit(solution)/shard_map/ppermute | solution.py:35
  98.3 1.7 collective-permute-done.3
  100.6 3.1 %collective-permute-start.4 = (bf16[16,40,960]{2,1,0:T(8,128)(2,1)S(1)}, bf16[16,40,960]{2,1,0:T(8,128)(2,1)S(1)}, u32[]{:S(2)}, u32[]{:S(2)}) collective-permute-start(bf16[16,40,960]{2,1,0:T(8,128)(2,1)S(1)} %bitcast.62), channel_id=1, source_target_pairs={{8,0},{12,4},{16,8},{20,12},{24,16},{28,20},{0,24},{4,28},{9,1},{1... | collective-permute-start | bytes 3686408 | tf_op jit(solution)/shard_map/ppermute | solution.py:33
  103.7 2.8 %collective-permute-start.6 = (bf16[16,40,960]{2,1,0:T(8,128)(2,1)S(1)}, bf16[16,40,960]{2,1,0:T(8,128)(2,1)S(1)}, u32[]{:S(2)}, u32[]{:S(2)}) collective-permute-start(bf16[16,40,960]{2,1,0:T(8,128)(2,1)S(1)} %bitcast.63), channel_id=1, source_target_pairs={{0,8},{4,12},{8,16},{12,20},{16,24},{20,28},{24,0},{28,4},{1,9},{5... | collective-permute-start | bytes 3686408 | tf_op jit(solution)/shard_map/ppermute | solution.py:34
  106.5 21.8 %collective-permute-done.4 = bf16[16,40,960]{2,1,0:T(8,128)(2,1)S(1)} collective-permute-done((bf16[16,40,960]{2,1,0:T(8,128)(2,1)S(1)}, bf16[16,40,960]{2,1,0:T(8,128)(2,1)S(1)}, u32[]{:S(2)}, u32[]{:S(2)}) %collective-permute-start.4) | collective-permute-done | bytes 1228832 | tf_op jit(solution)/shard_map/ppermute | solution.py:33
  129.3 3.2 %collective-permute-start.5 = (bf16[8,40,960]{2,1,0:T(8,128)(2,1)}, bf16[8,40,960]{2,1,0:T(8,128)(2,1)}, u32[]{:S(2)}, u32[]{:S(2)}) collective-permute-start(bf16[8,40,960]{2,1,0:T(8,128)(2,1)} %slice.43), channel_id=1, source_target_pairs={{8,0},{12,4},{16,8},{20,12},{24,16},{28,20},{0,24},{4,28},{9,1},{1... | collective-permute-start | bytes 1843208 | tf_op jit(solution)/shard_map/ppermute | solution.py:35
  133.8 2.6 collective-permute-start.7
  136.5 1.2 fusion.27
  137.7 1.0 copy.19
  139.0 3.1 %collective-permute-done.5 = bf16[8,40,960]{2,1,0:T(8,128)(2,1)} collective-permute-done((bf16[8,40,960]{2,1,0:T(8,128)(2,1)}, bf16[8,40,960]{2,1,0:T(8,128)(2,1)}, u32[]{:S(2)}, u32[]{:S(2)}) %collective-permute-start.5) | collective-permute-done | bytes 614432 | tf_op jit(solution)/shard_map/ppermute | solution.py:35
  142.1 5.7 %collective-permute-done.7 = bf16[8,40,960]{2,1,0:T(8,128)(2,1)} collective-permute-done((bf16[8,40,960]{2,1,0:T(8,128)(2,1)}, bf16[8,40,960]{2,1,0:T(8,128)(2,1)}, u32[]{:S(2)}, u32[]{:S(2)}) %collective-permute-start.7) | collective-permute-done | bytes 614432 | tf_op jit(solution)/shard_map/ppermute | solution.py:36
  147.7 1.4 maximum_bitcast_fusion
  151.4 2.3 copy-done.1
  154.9 3.3 %all-to-all-start.2 = ((bf16[4,64,256]{2,1,0:T(8,128)(2,1)}), bf16[4,64,256]{2,1,0:T(8,128)(2,1)S(1)}, u32[]{:S(2)}, u32[]{:S(2)}) async-start(bf16[4,64,256]{2,1,0:T(8,128)(2,1)} %broadcast_in_dim.16), calls=%async_computation.2 | async-start | bytes 262144 | tf_op jit(solution)/shard_map/all_to_all | solution.py:25
  158.2 3.8 %multiply_convert_fusion = bf16[256,896]{0,1:T(8,128)(2,1)S(1)} fusion(bf16[256,896]{0,1:T(8,128)(2,1)S(1)} %copy-done.6, bf16[256,2560]{1,0:T(8,128)(2,1)S(1)} %copy-done, bf16[2560,960]{1,0:T(8,128)(2,1)} %bitcast.60), kind=kOutput, calls=%fused_computation.26 | convolution fusion | flops 1176698880 | bytes 6815744 | tf_op jit(solution)/shard_map/dot_general | solution.py:80
  163.2 3.7 %convolution_bitcast_fusion = f32[256,896]{0,1:T(8,128)S(1)} fusion(bf16[2560,896]{1,0:T(8,128)(2,1)} %all-gather.3.cloned.1.call-done, bf16[256,2560]{1,0:T(8,128)(2,1)S(1)} %copy-done), kind=kOutput, calls=%fused_computation.14 | convolution fusion | flops 1174405120 | bytes 6815744 | tf_op jit(solution)/shard_map/dot_general | solution.py:80
  168.8 3.6 %all-to-all-start.4 = ((bf16[8,32,1792]{2,1,0:T(8,128)(2,1)}), bf16[8,32,1792]{2,1,0:T(8,128)(2,1)S(1)}, u32[]{:S(2)}, u32[]{:S(2)}) async-start(bf16[8,32,1792]{2,1,0:T(8,128)(2,1)} %bitcast.25), calls=%async_computation.4 | async-start | bytes 1835008 | tf_op jit(solution)/shard_map/all_to_all | solution.py:90
  172.4 4.4 %fusion.16 = f32[256,2560]{1,0:T(8,128)S(1)} fusion(bf16[2560,896]{1,0:T(8,128)(2,1)} %all-gather.3.cloned.1.call-done, f32[256,896]{0,1:T(8,128)} %copy-done.12, bf16[256,896]{0,1:T(8,128)(2,1)S(1)} %copy.18), kind=kOutput, calls=%fused_computation.28 | convolution fusion | flops 1176698880 | bytes 8585216 | tf_op jit(solution)/shard_map/dot_general | solution.py:86
  176.8 5.0 %fusion.7 = bf16[256,2560]{1,0:T(8,128)(2,1)} fusion(f32[256,2560]{1,0:T(8,128)S(1)} %fusion.16, bf16[256,896]{0,1:T(8,128)(2,1)S(1)} %multiply_convert_fusion, bf16[2560,960]{1,0:T(8,128)(2,1)} %bitcast.61), kind=kOutput, calls=%fused_computation.7 | convolution fusion | flops 1175715840 | bytes 8978432 | tf_op jit(solution)/shard_map/dot_general | solution.py:86
  181.8 6.5 %all-to-all-done.4 = bf16[8,32,1792]{2,1,0:T(8,128)(2,1)S(1)} async-done(((bf16[8,32,1792]{2,1,0:T(8,128)(2,1)}), bf16[8,32,1792]{2,1,0:T(8,128)(2,1)S(1)}, u32[]{:S(2)}, u32[]{:S(2)}) %all-to-all-start.4) | async-done | bytes 917536 | tf_op jit(solution)/shard_map/all_to_all | solution.py:90
  188.7 24.2 %all_to_all.43 = f32[16,2,1792]{2,1,0:T(2,128)S(1)} all-to-all(f32[16,2,1792]{2,1,0:T(2,128)S(1)} %reshape.60), channel_id=1, replica_groups=mesh['dp'=16,'fsdp'=8,'tensor'=4] {'dp'}, dimensions={0} | all-to-all | bytes 458752 | tf_op jit(solution)/shard_map/all_to_all | solution.py:94
  213.7 24.8 %all_to_all.44 = bf16[16,2,1792]{2,1,0:T(2,128)(2,1)S(1)} all-to-all(bf16[16,2,1792]{2,1,0:T(2,128)(2,1)S(1)} %broadcast_in_dim.18), channel_id=1, replica_groups=mesh['dp'=16,'fsdp'=8,'tensor'=4] {'dp'}, dimensions={0} | all-to-all | bytes 229376 | tf_op jit(solution)/shard_map/all_to_all | solution.py:25
  238.6 20.5 %all_to_all.45 = bf16[8,32,1792]{2,1,0:T(8,128)(2,1)S(1)} all-to-all(bf16[8,32,1792]{2,1,0:T(8,128)(2,1)S(1)} %broadcast_in_dim.20), channel_id=1, replica_groups=mesh['dp'=16,'fsdp'=8,'tensor'=4] {'fsdp'}, dimensions={0} | all-to-all | bytes 1835008 | tf_op jit(solution)/shard_map/all_to_all | solution.py:25
  260.1 2.5 copy.21
  (73 shorter events, 13.8 us)
Async XLA Ops:
  7.2 146.5 %copy-start = (bf16[256,2560]{1,0:T(8,128)(2,1)S(1)}, bf16[256,2560]{1,0:T(8,128)(2,1)}, u32[]{:S(2)}) copy-start(bf16[256,2560]{1,0:T(8,128)(2,1)} %param.6) | copy-start | bytes 3932164
  7.2 156.0 %all-gather.3.cloned.1.call-start = ((), (), s32[]{:S(2)}) async-start(), calls=%async_computation.9 | async-start | bytes 4874240 | tf_op jit(solution)/shard_map/all_gather | solution.py:63
  8.2 1.0 copy-start.8
  70.8 17.0 %collective-permute-start = (bf16[4,40,960]{2,1,0:T(8,128)(2,1)S(1)}, bf16[4,40,960]{2,1,0:T(8,128)(2,1)S(1)}, u32[]{:S(2)}, u32[]{:S(2)}) collective-permute-start(bf16[4,40,960]{2,1,0:T(8,128)(2,1)S(1)} %all_to_all.42), channel_id=1, source_target_pairs={{32,0},{64,32},{96,64},{128,96},{160,128},{192,160},{224,192},{256... | collective-permute-start | bytes 921608 | tf_op jit(solution)/shard_map/ppermute | solution.py:33
  72.7 17.0 %collective-permute-start.2 = (bf16[4,40,960]{2,1,0:T(8,128)(2,1)S(1)}, bf16[4,40,960]{2,1,0:T(8,128)(2,1)S(1)}, u32[]{:S(2)}, u32[]{:S(2)}) collective-permute-start(bf16[4,40,960]{2,1,0:T(8,128)(2,1)S(1)} %all_to_all.42), channel_id=1, source_target_pairs={{0,32},{32,64},{64,96},{96,128},{128,160},{160,192},{192,224},{224... | collective-permute-start | bytes 921608 | tf_op jit(solution)/shard_map/ppermute | solution.py:34
  87.8 10.5 %collective-permute-start.1 = (bf16[2,40,960]{2,1,0:T(8,128)(2,1)S(1)}, bf16[2,40,960]{2,1,0:T(8,128)(2,1)S(1)}, u32[]{:S(2)}, u32[]{:S(2)}) collective-permute-start(bf16[2,40,960]{2,1,0:T(8,128)(2,1)S(1)} %slice.41), channel_id=1, source_target_pairs={{32,0},{64,32},{96,64},{128,96},{160,128},{192,160},{224,192},{256... | collective-permute-start | bytes 460808 | tf_op jit(solution)/shard_map/ppermute | solution.py:35
  89.8 10.3 %collective-permute-start.3 = (bf16[2,40,960]{2,1,0:T(8,128)(2,1)S(1)}, bf16[2,40,960]{2,1,0:T(8,128)(2,1)S(1)}, u32[]{:S(2)}, u32[]{:S(2)}) collective-permute-start(bf16[2,40,960]{2,1,0:T(8,128)(2,1)S(1)} %slice.42), channel_id=1, source_target_pairs={{0,32},{32,64},{64,96},{96,128},{128,160},{160,192},{192,224},{224... | collective-permute-start | bytes 460808 | tf_op jit(solution)/shard_map/ppermute | solution.py:36
  100.6 27.7 %collective-permute-start.4 = (bf16[16,40,960]{2,1,0:T(8,128)(2,1)S(1)}, bf16[16,40,960]{2,1,0:T(8,128)(2,1)S(1)}, u32[]{:S(2)}, u32[]{:S(2)}) collective-permute-start(bf16[16,40,960]{2,1,0:T(8,128)(2,1)S(1)} %bitcast.62), channel_id=1, source_target_pairs={{8,0},{12,4},{16,8},{20,12},{24,16},{28,20},{0,24},{4,28},{9,1},{1... | collective-permute-start | bytes 3686408 | tf_op jit(solution)/shard_map/ppermute | solution.py:33
  103.7 28.7 %collective-permute-start.6 = (bf16[16,40,960]{2,1,0:T(8,128)(2,1)S(1)}, bf16[16,40,960]{2,1,0:T(8,128)(2,1)S(1)}, u32[]{:S(2)}, u32[]{:S(2)}) collective-permute-start(bf16[16,40,960]{2,1,0:T(8,128)(2,1)S(1)} %bitcast.63), channel_id=1, source_target_pairs={{0,8},{4,12},{8,16},{12,20},{16,24},{20,28},{24,0},{28,4},{1,9},{5... | collective-permute-start | bytes 3686408 | tf_op jit(solution)/shard_map/ppermute | solution.py:34
  128.3 4.1 %copy-start.2 = (bf16[16,40,960]{2,1,0:T(8,128)(2,1)}, bf16[16,40,960]{2,1,0:T(8,128)(2,1)S(1)}, u32[]{:S(2)}) copy-start(bf16[16,40,960]{2,1,0:T(8,128)(2,1)S(1)} %collective-permute-done.4) | copy-start | bytes 3686404
  129.3 12.8 %collective-permute-start.5 = (bf16[8,40,960]{2,1,0:T(8,128)(2,1)}, bf16[8,40,960]{2,1,0:T(8,128)(2,1)}, u32[]{:S(2)}, u32[]{:S(2)}) collective-permute-start(bf16[8,40,960]{2,1,0:T(8,128)(2,1)} %slice.43), channel_id=1, source_target_pairs={{8,0},{12,4},{16,8},{20,12},{24,16},{28,20},{0,24},{4,28},{9,1},{1... | collective-permute-start | bytes 1843208 | tf_op jit(solution)/shard_map/ppermute | solution.py:35
  132.5 1.3 copy-start.4
  133.8 14.0 %collective-permute-start.7 = (bf16[8,40,960]{2,1,0:T(8,128)(2,1)}, bf16[8,40,960]{2,1,0:T(8,128)(2,1)}, u32[]{:S(2)}, u32[]{:S(2)}) collective-permute-start(bf16[8,40,960]{2,1,0:T(8,128)(2,1)} %slice.44), channel_id=1, source_target_pairs={{0,8},{4,12},{8,16},{12,20},{16,24},{20,28},{24,0},{28,4},{1,9},{5... | collective-permute-start | bytes 1843208 | tf_op jit(solution)/shard_map/ppermute | solution.py:36
  138.9 10.2 %copy-start.3 = (bf16[16,40,960]{2,1,0:T(8,128)(2,1)S(1)}, bf16[16,40,960]{2,1,0:T(8,128)(2,1)}, u32[]{:S(2)}) copy-start(bf16[16,40,960]{2,1,0:T(8,128)(2,1)} %copy-done.2) | copy-start | bytes 3686404
  139.0 10.2 %copy-start.5 = (bf16[16,40,960]{2,1,0:T(8,128)(2,1)S(1)}, bf16[16,40,960]{2,1,0:T(8,128)(2,1)}, u32[]{:S(2)}) copy-start(bf16[16,40,960]{2,1,0:T(8,128)(2,1)} %copy-done.4) | copy-start | bytes 3686404
  151.3 2.3 copy-start.1
  151.4 6.9 %copy-start.6 = (bf16[256,896]{0,1:T(8,128)(2,1)S(1)}, bf16[256,896]{0,1:T(8,128)(2,1)}, u32[]{:S(2)}) copy-start(bf16[256,896]{0,1:T(8,128)(2,1)} %copy.19) | copy-start | bytes 1376260
  154.9 7.9 %all-to-all-start.2 = ((bf16[4,64,256]{2,1,0:T(8,128)(2,1)}), bf16[4,64,256]{2,1,0:T(8,128)(2,1)S(1)}, u32[]{:S(2)}, u32[]{:S(2)}) async-start(bf16[4,64,256]{2,1,0:T(8,128)(2,1)} %broadcast_in_dim.16), calls=%async_computation.2 | async-start | bytes 262144 | tf_op jit(solution)/shard_map/all_to_all | solution.py:25
  166.9 0.9 copy-start.12
  168.8 19.5 %all-to-all-start.4 = ((bf16[8,32,1792]{2,1,0:T(8,128)(2,1)}), bf16[8,32,1792]{2,1,0:T(8,128)(2,1)S(1)}, u32[]{:S(2)}, u32[]{:S(2)}) async-start(bf16[8,32,1792]{2,1,0:T(8,128)(2,1)} %bitcast.25), calls=%async_computation.4 | async-start | bytes 1835008 | tf_op jit(solution)/shard_map/all_to_all | solution.py:90
  172.4 40.5 %reduce-scatter.2.cloned.1.call-start = ((), (), s32[]{:S(2)}) async-start(), calls=%async_computation.10 | async-start | bytes 1638400 | tf_op jit(solution)/shard_map/reduce_scatter | solution.py:92
  188.3 24.7 %copy-start.10 = (f32[2,1792]{1,0:T(2,128)S(1)}, f32[2,1792]{1,0:T(2,128)}, u32[]{:S(2)}) copy-start(f32[2,1792]{1,0:T(2,128)} %param.10) | copy-start | bytes 43012
  188.3 24.7 %copy-start.11 = (f32[2,1792]{1,0:T(2,128)S(1)}, f32[2,1792]{1,0:T(2,128)}, u32[]{:S(2)}) copy-start(f32[2,1792]{1,0:T(2,128)} %param.11) | copy-start | bytes 43012
  188.3 71.7 %all-gather.5.cloned.1.call-start = ((), (), s32[]{:S(2)}) async-start(), calls=%async_computation.11 | async-start | bytes 1638400 | tf_op jit(solution)/shard_map/all_gather | solution.py:96
  238.5 20.6 %copy-start.7 = (bf16[20,1792]{1,0:T(8,128)(2,1)S(1)}, bf16[20,1792]{1,0:T(8,128)(2,1)}, u32[]{:S(2)}) copy-start(bf16[20,1792]{1,0:T(8,128)(2,1)} %param.8) | copy-start | bytes 215044
  238.6 20.6 %copy-start.9 = (bf16[20,8,16,2]{0,3,2,1:T(2,128)(2,1)S(1)}, bf16[20,8,16,2]{0,3,2,1:T(2,128)(2,1)}, u32[]{:S(2)}) copy-start(bf16[20,8,16,2]{0,3,2,1:T(2,128)(2,1)} %copy-done.8) | copy-start | bytes 30724
Sparse Core Ops, SparseCore 0:
  31.1 93.5 all-gather.2
  188.4 22.9 reduce-scatter.1
  213.6 31.5 all-gather.4

commit v3 on v2

--- a/solution.py
+++ b/solution.py
@@ -48,27 +48,31 @@
     rank = basis.shape[1]
     depth = outer * inner * rows
     share = rank // (outer * inner)
-    basis_perm = basis.reshape(rows, outer, inner, share).transpose(0, 2, 1, 3).reshape(rows, rank)
+    far = outer // RING
+    basis_perm = (
+        basis.reshape(rows, far, RING, inner, share).transpose(0, 3, 2, 1, 4).reshape(rows, rank)
+    )
     part = rank // quarters
     basis_part = lax.dynamic_slice_in_dim(basis_perm, lax.axis_index("tensor") * part, part, 1)
 
     pairs = [[PAIR * y + x for x in range(PAIR)] for y in range(RING)]
     columns = [[PAIR * y + x for y in range(RING)] for x in range(PAIR)]
-    strides = [[i + RING * j for j in range(outer // RING)] for i in range(RING)]
+    strides = [[i + RING * j for j in range(far)] for i in range(RING)]
+    fours = [[RING * j + i for i in range(RING)] for j in range(far)]
     pair_rows = PAIR * rows
-    both = jnp.concatenate([weight, basis_part], axis=1)
-    block = spread(both, "fsdp", pairs).reshape(pair_rows, width + part)
-    half = width // 2
-    plane = spread(block[:, :half], "fsdp", columns).reshape(inner * rows, half)
+    half = width * 9 // 14
+    plane = spread(weight[:, :half], "fsdp").reshape(inner * rows, half)
     weight_a = lax.all_gather(plane, "dp", axis=0, tiled=True)
-    second = block[:, half:]
+    second = jnp.concatenate([weight[:, half:], basis_part], axis=1)
+    plane, second = lax.optimization_barrier((plane, second))
+    second = spread(second, "fsdp", pairs).reshape(pair_rows, width - half + part)
     strided = spread(second, "dp", strides)
     place = lax.rem(lax.axis_index("dp"), RING)
     pick = ring_of_four(strided, "dp", 1, place)
-    line = jnp.stack([pick(r) for r in range(RING)], axis=1).reshape(outer, pair_rows, half + part)
+    line = jnp.stack([pick(r) for r in range(RING)], axis=1).reshape(outer, pair_rows, width - half + part)
     pick = ring_of_four(line, "fsdp", PAIR, lax.axis_index("fsdp") // PAIR)
-    full_b = jnp.stack([pick(r) for r in range(RING)], axis=1).reshape(depth, half + part)
-    weight_b, full_basis = full_b[:, :half], full_b[:, half:]
+    full_b = jnp.stack([pick(r) for r in range(RING)], axis=1).reshape(depth, width - half + part)
+    weight_b, full_basis = full_b[:, : width - half], full_b[:, width - half :]
 
     projected_part = lax.dot_general(
         full_basis, tokens, (((0,), (1,)), ((), ())), preferred_element_type=f32
@@ -76,10 +80,9 @@
     projected = spread(projected_part, "tensor").reshape(rank, tokens.shape[0])
 
     grad_pre, grad_part = [], []
-    for index, side in enumerate((weight_a, weight_b)):
+    for side, wanted in ((weight_a, cotangent[:, :half]), (weight_b, cotangent[:, half:])):
         preact = jnp.dot(tokens, side, preferred_element_type=f32)
-        wanted = cotangent[:, index * half : (index + 1) * half].astype(f32)
-        grad_pre.append((wanted * silu_slope(preact)).astype(bf16))
+        grad_pre.append((wanted.astype(f32) * silu_slope(preact)).astype(bf16))
         grad_part.append(jnp.dot(projected, grad_pre[-1], preferred_element_type=f32).astype(bf16))
     grad_part = jnp.concatenate(grad_part, axis=1)
     partial_rows = sum(
@@ -91,9 +94,10 @@
     landed, partial_rows = lax.optimization_barrier((landed, partial_rows))
     token_rows = lax.psum_scatter(partial_rows, "tensor", scatter_dimension=0, tiled=True)
     inner_sum = jnp.sum(landed.astype(f32), axis=0)
-    landed = lax.all_to_all(inner_sum.reshape(outer, share, width), "dp", 0, 0, tiled=True)
-    landed, token_rows = lax.optimization_barrier((landed, token_rows))
-    token_grad = lax.all_gather(token_rows, "tensor", axis=0, tiled=True)
+    blocks = inner_sum.astype(bf16).reshape(RING, far * share, width)
+    landed = lax.all_to_all(blocks, "dp", 0, 0, tiled=True, axis_index_groups=fours)
+    blocks = jnp.sum(landed.astype(f32), axis=0).reshape(far, share, width)
+    landed = lax.all_to_all(blocks, "dp", 0, 0, tiled=True, axis_index_groups=strides)
     reduced = jnp.sum(landed, axis=0)
 
     token_count = tokens.shape[0] * outer * inner
@@ -103,7 +107,10 @@
     first_hat = new_first_moment / (1.0 - BETA_ONE**ADAM_STEP)
     second_hat = new_second_moment / (1.0 - BETA_TWO**ADAM_STEP)
     direction = (first_hat / (jnp.sqrt(second_hat) + EPSILON)).astype(bf16)
-    column = spread(direction, "dp").reshape(outer * share, width)
+    column = spread(direction, "dp", strides).reshape(far * share, width)
+    column, token_rows = lax.optimization_barrier((column, token_rows))
+    token_grad = lax.all_gather(token_rows, "tensor", axis=0, tiled=True)
+    column = spread(column, "dp", fours).reshape(outer * share, width)
     full_direction = spread(column, "fsdp").reshape(rank, width)
     update = jnp.dot(basis_perm, full_direction, preferred_element_type=f32)
     new_weight = (weight.astype(f32) - LEARN_RATE * update).astype(bf16)

time: 270 us -> 267 us (0.989)
  waiting for transfers between devices: 55.4 us -> 45.7 us
  blocking collectives: 131 us -> 139 us
    ppermute x2, waiting for transfers between devices: 33 us -> 23.1 us  [ring_of_four(): following = lax.ppermute(block, axis, ahead)]
    ppermute x2, waiting for transfers between devices: 7.69 us -> 3.29 us  [ring_of_four(): far_front = lax.ppermute(following[:half], axis, ahead)]
    all_to_all x1 -> x2, blocking collectives: 24.2 us -> 28.4 us  [the longest x1 18.6 us: local(): lax.all_to_all(blocks, 'dp', 0, 0, tiled=True, axis_index_groups=strides)]
    all_to_all x5 -> x6, blocking collectives: 107 us -> 110 us  [spread(): lax.all_to_all(copies, axis, 0, 0, tiled=True, axis_index_groups=groups)]
    unnamed x30 -> x27, local copies, waits for them, and re-layouts: 7.63 us -> 7.72 us
  transfers between devices with their start and end apart: 13 -> 13, of which waited for: 8 -> 7; matrix products, arithmetic and copies ran while one was open for 9% -> 9% of each run, Pallas kernels for 0% -> 0%
where the time goes in v3:
time: 267 us; the launch traced here: 266 us
  blocking collectives  139 us (52%)
  waiting for transfers between devices  45.7 us (17%)
  starting transfers between devices  30.4 us (11%)
  matrix products  17.8 us (7%)
  local copies, waits for them, and re-layouts  14.3 us (5%)
  between operations  14.3 us (5%)
  other arithmetic  4.6 us (2%)
    all_to_all x6, blocking collectives, spread(): lax.all_to_all(copies, axis, 0, 0, tiled=True, axis_index_groups=groups)  110 us
    ppermute x2, waiting for transfers between devices, ring_of_four(): following = lax.ppermute(block, axis, ahead)  23.1 us
    all_to_all x1, blocking collectives, local(): lax.all_to_all(blocks, 'dp', 0, 0, tiled=True, axis_index_groups=strides)  18.6 us
    all_to_all x1, blocking collectives, local(): lax.all_to_all(blocks, 'dp', 0, 0, tiled=True, axis_index_groups=fours)  9.83 us
    ppermute x2, waiting for transfers between devices, ring_of_four(): far_back = lax.ppermute(preceding[half:], axis, behind)  9.77 us
    all_to_all x1, waiting for transfers between devices, local(): lax.all_to_all(grad_part.reshape(inner, outer * share, width), 'fsdp', 0,...  7.89 us
    unnamed x27, local copies, waits for them, and re-layouts  7.72 us
    dot_general x2, matrix products, local(): preact = jnp.dot(tokens, side, preferred_element_type=f32)  7.69 us
  transfers between devices with their start and end apart: 13, of which 7 were waited for; matrix products, arithmetic and copies ran while one was open for 9% of the time, Pallas kernels for 0%

profile of v3, /device:TPU:32, one launch (start us, length us, event | category | flops | bytes accessed | tf_op | source)
XLA Modules:
  0.0 265.5 jit_solution(6216016151662761305)
XLA Ops:
  8.2 17.5 %all_to_all.50 = bf16[8,20,1152]{2,1,0:T(8,128)(2,1)S(1)} all-to-all(bf16[8,20,1152]{2,1,0:T(8,128)(2,1)S(1)} %broadcast_in_dim.18), channel_id=1, replica_groups=mesh['dp'=16,'fsdp'=8,'tensor'=4] {'fsdp'}, dimensions={0} | all-to-all | bytes 737280 | tf_op jit(solution)/shard_map/all_to_all | solution.py:25
  26.9 8.0 %all_to_all.51 = bf16[2,20,704]{2,1,0:T(8,128)(2,1)S(1)} all-to-all(bf16[2,20,704]{2,1,0:T(8,128)(2,1)S(1)} %broadcast_in_dim.19), channel_id=1, replica_groups={{0,4},{8,12},{16,20},{24,28},{1,5},{9,13},{17,21},{25,29},{2,6},{10,14}..., dimensions={0} | all-to-all | bytes 112640 | tf_op jit(solution)/shard_map/all_to_all | solution.py:25
  34.9 37.0 %all_to_all.52 = bf16[4,40,704]{2,1,0:T(8,128)(2,1)S(1)} all-to-all(bf16[4,40,704]{2,1,0:T(8,128)(2,1)S(1)} %broadcast_in_dim.21), channel_id=1, replica_groups={{0,128,256,384},{32,160,288,416},{64,192,320,448},{96,224,352,480},{1,1..., dimensions={0} | all-to-all | bytes 450560 | tf_op jit(solution)/shard_map/all_to_all | solution.py:25
  71.9 2.2 collective-permute-start
  74.1 3.7 %collective-permute-start.2 = (bf16[4,40,704]{2,1,0:T(8,128)(2,1)S(1)}, bf16[4,40,704]{2,1,0:T(8,128)(2,1)S(1)}, u32[]{:S(2)}, u32[]{:S(2)}) collective-permute-start(bf16[4,40,704]{2,1,0:T(8,128)(2,1)S(1)} %all_to_all.52), channel_id=1, source_target_pairs={{0,32},{32,64},{64,96},{96,128},{128,160},{160,192},{192,224},{224... | collective-permute-start | bytes 675848 | tf_op jit(solution)/shard_map/ppermute | solution.py:34
  77.8 8.1 %collective-permute-done = bf16[4,40,704]{2,1,0:T(8,128)(2,1)S(1)} collective-permute-done((bf16[4,40,704]{2,1,0:T(8,128)(2,1)S(1)}, bf16[4,40,704]{2,1,0:T(8,128)(2,1)S(1)}, u32[]{:S(2)}, u32[]{:S(2)}) %collective-permute-start) | collective-permute-done | bytes 225312 | tf_op jit(solution)/shard_map/ppermute | solution.py:33
  85.9 2.9 %collective-permute-start.1 = (bf16[2,40,704]{2,1,0:T(8,128)(2,1)S(1)}, bf16[2,40,704]{2,1,0:T(8,128)(2,1)S(1)}, u32[]{:S(2)}, u32[]{:S(2)}) collective-permute-start(bf16[2,40,704]{2,1,0:T(8,128)(2,1)S(1)} %slice.40), channel_id=1, source_target_pairs={{32,0},{64,32},{96,64},{128,96},{160,128},{192,160},{224,192},{256... | collective-permute-start | bytes 337928 | tf_op jit(solution)/shard_map/ppermute | solution.py:35
  88.8 2.9 %collective-permute-start.3 = (bf16[2,40,704]{2,1,0:T(8,128)(2,1)S(1)}, bf16[2,40,704]{2,1,0:T(8,128)(2,1)S(1)}, u32[]{:S(2)}, u32[]{:S(2)}) collective-permute-start(bf16[2,40,704]{2,1,0:T(8,128)(2,1)S(1)} %slice.41), channel_id=1, source_target_pairs={{0,32},{32,64},{64,96},{96,128},{128,160},{160,192},{192,224},{224... | collective-permute-start | bytes 337928 | tf_op jit(solution)/shard_map/ppermute | solution.py:36
  91.8 3.3 %collective-permute-done.1 = bf16[2,40,704]{2,1,0:T(8,128)(2,1)S(1)} collective-permute-done((bf16[2,40,704]{2,1,0:T(8,128)(2,1)S(1)}, bf16[2,40,704]{2,1,0:T(8,128)(2,1)S(1)}, u32[]{:S(2)}, u32[]{:S(2)}) %collective-permute-start.1) | collective-permute-done | bytes 112672 | tf_op jit(solution)/shard_map/ppermute | solution.py:35
  95.1 3.1 %collective-permute-done.3 = bf16[2,40,704]{2,1,0:T(8,128)(2,1)S(1)} collective-permute-done((bf16[2,40,704]{2,1,0:T(8,128)(2,1)S(1)}, bf16[2,40,704]{2,1,0:T(8,128)(2,1)S(1)}, u32[]{:S(2)}, u32[]{:S(2)}) %collective-permute-start.3) | collective-permute-done | bytes 112672 | tf_op jit(solution)/shard_map/ppermute | solution.py:36
  98.6 2.6 collective-permute-start.4
  101.2 3.3 %collective-permute-start.6 = (bf16[16,40,704]{2,1,0:T(8,128)(2,1)S(1)}, bf16[16,40,704]{2,1,0:T(8,128)(2,1)S(1)}, u32[]{:S(2)}, u32[]{:S(2)}) collective-permute-start(bf16[16,40,704]{2,1,0:T(8,128)(2,1)S(1)} %bitcast.62), channel_id=1, source_target_pairs={{0,8},{4,12},{8,16},{12,20},{16,24},{20,28},{24,0},{28,4},{1,9},{5... | collective-permute-start | bytes 2703368 | tf_op jit(solution)/shard_map/ppermute | solution.py:34
  104.5 15.1 %collective-permute-done.4 = bf16[16,40,704]{2,1,0:T(8,128)(2,1)S(1)} collective-permute-done((bf16[16,40,704]{2,1,0:T(8,128)(2,1)S(1)}, bf16[16,40,704]{2,1,0:T(8,128)(2,1)S(1)}, u32[]{:S(2)}, u32[]{:S(2)}) %collective-permute-start.4) | collective-permute-done | bytes 901152 | tf_op jit(solution)/shard_map/ppermute | solution.py:33
  120.4 3.9 %collective-permute-start.5 = (bf16[8,40,704]{2,1,0:T(8,128)(2,1)}, bf16[8,40,704]{2,1,0:T(8,128)(2,1)}, u32[]{:S(2)}, u32[]{:S(2)}) collective-permute-start(bf16[8,40,704]{2,1,0:T(8,128)(2,1)} %slice.42), channel_id=1, source_target_pairs={{8,0},{12,4},{16,8},{20,12},{24,16},{28,20},{0,24},{4,28},{9,1},{1... | collective-permute-start | bytes 1351688 | tf_op jit(solution)/shard_map/ppermute | solution.py:35
  126.1 1.9 collective-permute-start.7
  128.1 1.7 slice.38
  129.8 1.9 copy.27
  131.7 6.6 %collective-permute-done.7 = bf16[8,40,704]{2,1,0:T(8,128)(2,1)} collective-permute-done((bf16[8,40,704]{2,1,0:T(8,128)(2,1)}, bf16[8,40,704]{2,1,0:T(8,128)(2,1)}, u32[]{:S(2)}, u32[]{:S(2)}) %collective-permute-start.7) | collective-permute-done | bytes 450592 | tf_op jit(solution)/shard_map/ppermute | solution.py:36
  141.1 1.9 copy-done.1
  144.3 3.3 %all-to-all-start.3 = ((bf16[4,64,256]{2,1,0:T(8,128)(2,1)}), bf16[4,64,256]{2,1,0:T(8,128)(2,1)S(1)}, u32[]{:S(2)}, u32[]{:S(2)}) async-start(bf16[4,64,256]{2,1,0:T(8,128)(2,1)} %broadcast_in_dim.22), calls=%async_computation.3 | async-start | bytes 262144 | tf_op jit(solution)/shard_map/all_to_all | solution.py:25
  147.6 3.1 %multiply_convert_fusion.3 = bf16[256,640]{0,1:T(8,128)(2,1)S(1)} fusion(bf16[256,2560]{1,0:T(8,128)(2,1)S(1)} %copy-done, bf16[2560,704]{1,0:T(8,128)(2,1)} %bitcast.59, bf16[256,640]{0,1:T(8,128)(2,1)S(1)} %copy-done.6), kind=kOutput, calls=%fused_computation.28 | convolution fusion | flops 840499200 | bytes 5242880 | tf_op jit(solution)/shard_map/dot_general | solution.py:84
  152.5 4.6 %fusion.23 = f32[256,1152]{1,0:T(8,128)S(1)} fusion(bf16[256,2560]{1,0:T(8,128)(2,1)S(1)} %copy-done, bf16[2560,1152]{1,0:T(8,128)(2,1)} %all-gather.3.cloned.1.call-done), kind=kOutput, calls=%fused_computation.47 | convolution fusion | flops 1509949440 | bytes 8388608 | tf_op jit(solution)/shard_map/dot_general | solution.py:84
  159.2 3.6 %all-to-all-start.4 = ((bf16[8,32,1792]{2,1,0:T(8,128)(2,1)}), bf16[8,32,1792]{2,1,0:T(8,128)(2,1)S(1)}, u32[]{:S(2)}, u32[]{:S(2)}) async-start(bf16[8,32,1792]{2,1,0:T(8,128)(2,1)} %bitcast.23), calls=%async_computation.4 | async-start | bytes 1835008 | tf_op jit(solution)/shard_map/all_to_all | solution.py:93
  162.8 5.4 %fusion.10 = f32[256,2560]{1,0:T(8,128)S(1)} fusion(bf16[2560,1152]{1,0:T(8,128)(2,1)} %all-gather.3.cloned.1.call-done, f32[256,1152]{1,0:T(8,128)} %copy-done.11, bf16[256,1792]{1,0:T(8,128)(2,1)} %param.7), kind=kOutput, calls=%fused_computation.15 | convolution fusion | flops 1512898560 | bytes 10289152 | tf_op jit(solution)/shard_map/dot_general | solution.py:89
  168.2 2.3 fusion
  170.5 7.9 %all-to-all-done.4 = bf16[8,32,1792]{2,1,0:T(8,128)(2,1)S(1)} async-done(((bf16[8,32,1792]{2,1,0:T(8,128)(2,1)}), bf16[8,32,1792]{2,1,0:T(8,128)(2,1)S(1)}, u32[]{:S(2)}, u32[]{:S(2)}) %all-to-all-start.4) | async-done | bytes 917536 | tf_op jit(solution)/shard_map/all_to_all | solution.py:93
  178.6 9.8 %all_to_all.53 = bf16[4,8,1792]{2,1,0:T(8,128)(2,1)S(1)} all-to-all(bf16[4,8,1792]{2,1,0:T(8,128)(2,1)S(1)} %bitcast.72), channel_id=1, replica_groups={{0,32,64,96},{128,160,192,224},{256,288,320,352},{384,416,448,480},{1,3..., dimensions={0} | all-to-all | bytes 229376 | tf_op jit(solution)/shard_map/all_to_all | solution.py:98
  188.5 18.6 %all_to_all.54 = f32[4,2,1792]{2,1,0:T(2,128)S(1)} all-to-all(f32[4,2,1792]{2,1,0:T(2,128)S(1)} %reshape.64), channel_id=1, replica_groups={{0,128,256,384},{32,160,288,416},{64,192,320,448},{96,224,352,480},{1,1..., dimensions={0} | all-to-all | bytes 114688 | tf_op jit(solution)/shard_map/all_to_all | solution.py:100
  207.8 15.2 %all_to_all.55 = bf16[4,2,1792]{2,1,0:T(2,128)(2,1)S(1)} all-to-all(bf16[4,2,1792]{2,1,0:T(2,128)(2,1)S(1)} %broadcast_in_dim.23), channel_id=1, replica_groups={{0,128,256,384},{32,160,288,416},{64,192,320,448},{96,224,352,480},{1,1..., dimensions={0} | all-to-all | bytes 57344 | tf_op jit(solution)/shard_map/all_to_all | solution.py:25
  223.1 8.1 %all_to_all.56 = bf16[4,8,1792]{2,1,0:T(8,128)(2,1)S(1)} all-to-all(bf16[4,8,1792]{2,1,0:T(8,128)(2,1)S(1)} %broadcast_in_dim.24), channel_id=1, replica_groups={{0,32,64,96},{128,160,192,224},{256,288,320,352},{384,416,448,480},{1,3..., dimensions={0} | all-to-all | bytes 229376 | tf_op jit(solution)/shard_map/all_to_all | solution.py:25
  231.3 24.3 %all_to_all.57 = bf16[8,32,1792]{2,1,0:T(8,128)(2,1)S(1)} all-to-all(bf16[8,32,1792]{2,1,0:T(8,128)(2,1)S(1)} %broadcast_in_dim.52), channel_id=1, replica_groups=mesh['dp'=16,'fsdp'=8,'tensor'=4] {'fsdp'}, dimensions={0} | all-to-all | bytes 1835008 | tf_op jit(solution)/shard_map/all_to_all | solution.py:25
  256.5 2.5 copy.29
  (76 shorter events, 15.0 us)
Async XLA Ops:
  7.2 135.9 %copy-start = (bf16[256,2560]{1,0:T(8,128)(2,1)S(1)}, bf16[256,2560]{1,0:T(8,128)(2,1)}, u32[]{:S(2)}) copy-start(bf16[256,2560]{1,0:T(8,128)(2,1)} %param.6) | copy-start | bytes 3932164
  7.2 145.3 %all-gather.3.cloned.1.call-start = ((), (), s32[]{:S(2)}) async-start(), calls=%async_computation.11 | async-start | bytes 6266880 | tf_op jit(solution)/shard_map/all_gather | solution.py:65
  8.1 18.4 %copy-start.10 = (bf16[20,256]{1,0:T(8,128)(2,1)S(1)}, bf16[20,256]{1,0:T(8,128)(2,1)}, u32[]{:S(2)}) copy-start(bf16[20,256]{1,0:T(8,128)(2,1)} %param.9) | copy-start | bytes 30724
  8.2 18.7 %slice-start = ((bf16[20,1792]{1,0:T(8,128)(2,1)}), bf16[20,640]{1,0:T(8,128)(2,1)S(1)}, s32[]{:S(2)}) async-start(bf16[20,1792]{1,0:T(8,128)(2,1)} %param.8), calls=%async_computation.14 | async-start | bytes 61440 | tf_op jit(solution)/shard_map/slice | solution.py:66
  71.9 13.9 %collective-permute-start = (bf16[4,40,704]{2,1,0:T(8,128)(2,1)S(1)}, bf16[4,40,704]{2,1,0:T(8,128)(2,1)S(1)}, u32[]{:S(2)}, u32[]{:S(2)}) collective-permute-start(bf16[4,40,704]{2,1,0:T(8,128)(2,1)S(1)} %all_to_all.52), channel_id=1, source_target_pairs={{32,0},{64,32},{96,64},{128,96},{160,128},{192,160},{224,192},{256... | collective-permute-start | bytes 675848 | tf_op jit(solution)/shard_map/ppermute | solution.py:33
  74.1 14.7 %collective-permute-start.2 = (bf16[4,40,704]{2,1,0:T(8,128)(2,1)S(1)}, bf16[4,40,704]{2,1,0:T(8,128)(2,1)S(1)}, u32[]{:S(2)}, u32[]{:S(2)}) collective-permute-start(bf16[4,40,704]{2,1,0:T(8,128)(2,1)S(1)} %all_to_all.52), channel_id=1, source_target_pairs={{0,32},{32,64},{64,96},{96,128},{128,160},{160,192},{192,224},{224... | collective-permute-start | bytes 675848 | tf_op jit(solution)/shard_map/ppermute | solution.py:34
  85.9 9.2 %collective-permute-start.1 = (bf16[2,40,704]{2,1,0:T(8,128)(2,1)S(1)}, bf16[2,40,704]{2,1,0:T(8,128)(2,1)S(1)}, u32[]{:S(2)}, u32[]{:S(2)}) collective-permute-start(bf16[2,40,704]{2,1,0:T(8,128)(2,1)S(1)} %slice.40), channel_id=1, source_target_pairs={{32,0},{64,32},{96,64},{128,96},{160,128},{192,160},{224,192},{256... | collective-permute-start | bytes 337928 | tf_op jit(solution)/shard_map/ppermute | solution.py:35
  88.8 9.4 %collective-permute-start.3 = (bf16[2,40,704]{2,1,0:T(8,128)(2,1)S(1)}, bf16[2,40,704]{2,1,0:T(8,128)(2,1)S(1)}, u32[]{:S(2)}, u32[]{:S(2)}) collective-permute-start(bf16[2,40,704]{2,1,0:T(8,128)(2,1)S(1)} %slice.41), channel_id=1, source_target_pairs={{0,32},{32,64},{64,96},{96,128},{128,160},{160,192},{192,224},{224... | collective-permute-start | bytes 337928 | tf_op jit(solution)/shard_map/ppermute | solution.py:36
  98.6 20.9 %collective-permute-start.4 = (bf16[16,40,704]{2,1,0:T(8,128)(2,1)S(1)}, bf16[16,40,704]{2,1,0:T(8,128)(2,1)S(1)}, u32[]{:S(2)}, u32[]{:S(2)}) collective-permute-start(bf16[16,40,704]{2,1,0:T(8,128)(2,1)S(1)} %bitcast.61), channel_id=1, source_target_pairs={{8,0},{12,4},{16,8},{20,12},{24,16},{28,20},{0,24},{4,28},{9,1},{1... | collective-permute-start | bytes 2703368 | tf_op jit(solution)/shard_map/ppermute | solution.py:33
  101.2 23.1 %collective-permute-start.6 = (bf16[16,40,704]{2,1,0:T(8,128)(2,1)S(1)}, bf16[16,40,704]{2,1,0:T(8,128)(2,1)S(1)}, u32[]{:S(2)}, u32[]{:S(2)}) collective-permute-start(bf16[16,40,704]{2,1,0:T(8,128)(2,1)S(1)} %bitcast.62), channel_id=1, source_target_pairs={{0,8},{4,12},{8,16},{12,20},{16,24},{20,28},{24,0},{28,4},{1,9},{5... | collective-permute-start | bytes 2703368 | tf_op jit(solution)/shard_map/ppermute | solution.py:34
  120.4 11.4 %collective-permute-start.5 = (bf16[8,40,704]{2,1,0:T(8,128)(2,1)}, bf16[8,40,704]{2,1,0:T(8,128)(2,1)}, u32[]{:S(2)}, u32[]{:S(2)}) collective-permute-start(bf16[8,40,704]{2,1,0:T(8,128)(2,1)} %slice.42), channel_id=1, source_target_pairs={{8,0},{12,4},{16,8},{20,12},{24,16},{28,20},{0,24},{4,28},{9,1},{1... | collective-permute-start | bytes 1351688 | tf_op jit(solution)/shard_map/ppermute | solution.py:35
  124.3 0.9 copy-start.3
  126.1 12.2 %collective-permute-start.7 = (bf16[8,40,704]{2,1,0:T(8,128)(2,1)}, bf16[8,40,704]{2,1,0:T(8,128)(2,1)}, u32[]{:S(2)}, u32[]{:S(2)}) collective-permute-start(bf16[8,40,704]{2,1,0:T(8,128)(2,1)} %slice.43), channel_id=1, source_target_pairs={{0,8},{4,12},{8,16},{12,20},{16,24},{20,28},{24,0},{28,4},{1,9},{5... | collective-permute-start | bytes 1351688 | tf_op jit(solution)/shard_map/ppermute | solution.py:36
  131.7 7.9 %copy-start.4 = (bf16[16,40,704]{2,1,0:T(8,128)(2,1)S(1)}, bf16[16,40,704]{2,1,0:T(8,128)(2,1)}, u32[]{:S(2)}) copy-start(bf16[16,40,704]{2,1,0:T(8,128)(2,1)} %copy-done.3) | copy-start | bytes 2703364
  141.1 1.9 copy-start.1
  141.1 6.5 %copy-start.6 = (bf16[256,640]{0,1:T(8,128)(2,1)S(1)}, bf16[256,640]{0,1:T(8,128)(2,1)}, u32[]{:S(2)}) copy-start(bf16[256,640]{0,1:T(8,128)(2,1)} %copy.27) | copy-start | bytes 983044
  144.3 7.9 %all-to-all-start.3 = ((bf16[4,64,256]{2,1,0:T(8,128)(2,1)}), bf16[4,64,256]{2,1,0:T(8,128)(2,1)S(1)}, u32[]{:S(2)}, u32[]{:S(2)}) async-start(bf16[4,64,256]{2,1,0:T(8,128)(2,1)} %broadcast_in_dim.22), calls=%async_computation.3 | async-start | bytes 262144 | tf_op jit(solution)/shard_map/all_to_all | solution.py:25
  152.5 4.6 %copy-start.7 = (bf16[256,1792]{1,0:T(8,128)(2,1)S(1)}, bf16[256,1792]{1,0:T(8,128)(2,1)}, u32[]{:S(2)}) copy-start(bf16[256,1792]{1,0:T(8,128)(2,1)} %param.7) | copy-start | bytes 2752516
  157.2 1.0 copy-start.11
  159.2 19.2 %all-to-all-start.4 = ((bf16[8,32,1792]{2,1,0:T(8,128)(2,1)}), bf16[8,32,1792]{2,1,0:T(8,128)(2,1)S(1)}, u32[]{:S(2)}, u32[]{:S(2)}) async-start(bf16[8,32,1792]{2,1,0:T(8,128)(2,1)} %bitcast.23), calls=%async_computation.4 | async-start | bytes 1835008 | tf_op jit(solution)/shard_map/all_to_all | solution.py:93
  162.8 60.3 %reduce-scatter.2.cloned.1.call-start = ((), (), s32[]{:S(2)}) async-start(), calls=%async_computation.12 | async-start | bytes 1638400 | tf_op jit(solution)/shard_map/reduce_scatter | solution.py:95
  162.8 5.4 %copy-start.2 = (bf16[16,4,40,704]{3,2,1,0:T(8,128)(2,1)S(1)}, bf16[16,4,40,704]{3,2,1,0:T(8,128)(2,1)}, u32[]{:S(2)}) copy-start(bf16[16,4,40,704]{3,2,1,0:T(8,128)(2,1)} %copy-done.1) | copy-start | bytes 10813444
  170.5 36.6 %copy-start.8 = (f32[2,1792]{1,0:T(2,128)S(1)}, f32[2,1792]{1,0:T(2,128)}, u32[]{:S(2)}) copy-start(f32[2,1792]{1,0:T(2,128)} %param.10) | copy-start | bytes 43012
  170.5 36.6 %copy-start.9 = (f32[2,1792]{1,0:T(2,128)S(1)}, f32[2,1792]{1,0:T(2,128)}, u32[]{:S(2)}) copy-start(f32[2,1792]{1,0:T(2,128)} %param.11) | copy-start | bytes 43012
  178.4 78.1 %all-gather.5.cloned.1.call-start = ((), (), s32[]{:S(2)}) async-start(), calls=%async_computation.13 | async-start | bytes 1638400 | tf_op jit(solution)/shard_map/all_gather | solution.py:112
  231.2 24.4 %copy-start.5 = (bf16[20,1792]{1,0:T(8,128)(2,1)S(1)}, bf16[20,1792]{1,0:T(8,128)(2,1)}, u32[]{:S(2)}) copy-start(bf16[20,1792]{1,0:T(8,128)(2,1)} %param.8) | copy-start | bytes 215044
Sparse Core Ops, SparseCore 0:
  26.6 101.3 all-gather.2
  178.5 22.2 reduce-scatter.1
  223.2 26.8 all-gather.4

commit v4 on v3

--- a/solution.py
+++ b/solution.py
@@ -66,12 +66,12 @@
     second = jnp.concatenate([weight[:, half:], basis_part], axis=1)
     plane, second = lax.optimization_barrier((plane, second))
     second = spread(second, "fsdp", pairs).reshape(pair_rows, width - half + part)
-    strided = spread(second, "dp", strides)
-    place = lax.rem(lax.axis_index("dp"), RING)
-    pick = ring_of_four(strided, "dp", 1, place)
-    line = jnp.stack([pick(r) for r in range(RING)], axis=1).reshape(outer, pair_rows, width - half + part)
+    line = lax.all_gather(second, "dp", axis=0)
     pick = ring_of_four(line, "fsdp", PAIR, lax.axis_index("fsdp") // PAIR)
     full_b = jnp.stack([pick(r) for r in range(RING)], axis=1).reshape(depth, width - half + part)
+    moments = jnp.stack([first_moment, second_moment])
+    full_b, moments = lax.optimization_barrier((full_b, moments))
+    moments = spread(moments, "dp", strides)
     weight_b, full_basis = full_b[:, : width - half], full_b[:, width - half :]
 
     projected_part = lax.dot_general(
@@ -84,7 +84,8 @@
         preact = jnp.dot(tokens, side, preferred_element_type=f32)
         grad_pre.append((wanted.astype(f32) * silu_slope(preact)).astype(bf16))
         grad_part.append(jnp.dot(projected, grad_pre[-1], preferred_element_type=f32).astype(bf16))
-    grad_part = jnp.concatenate(grad_part, axis=1)
+    grad_part, moments = lax.optimization_barrier((jnp.concatenate(grad_part, axis=1), moments))
+    old_first, old_second = (moments[:, i].reshape(far * share, width) for i in range(2))
     partial_rows = sum(
         lax.dot_general(g, w, (((1,), (1,)), ((), ())), preferred_element_type=f32)
         for g, w in zip(grad_pre, (weight_a, weight_b))
@@ -96,21 +97,25 @@
     inner_sum = jnp.sum(landed.astype(f32), axis=0)
     blocks = inner_sum.astype(bf16).reshape(RING, far * share, width)
     landed = lax.all_to_all(blocks, "dp", 0, 0, tiled=True, axis_index_groups=fours)
-    blocks = jnp.sum(landed.astype(f32), axis=0).reshape(far, share, width)
-    landed = lax.all_to_all(blocks, "dp", 0, 0, tiled=True, axis_index_groups=strides)
-    reduced = jnp.sum(landed, axis=0)
+    blocks = jnp.sum(landed.astype(f32), axis=0).astype(bf16)
+    landed = spread(blocks, "dp", strides)
+    landed, token_rows = lax.optimization_barrier((landed, token_rows))
+    token_grad = lax.all_gather(token_rows, "tensor", axis=0, tiled=True)
+    reduced = jnp.sum(landed.astype(f32), axis=0)
 
     token_count = tokens.shape[0] * outer * inner
     grad_low = reduced / float(token_count)
-    new_first_moment = BETA_ONE * first_moment + (1.0 - BETA_ONE) * grad_low
-    new_second_moment = BETA_TWO * second_moment + (1.0 - BETA_TWO) * grad_low * grad_low
-    first_hat = new_first_moment / (1.0 - BETA_ONE**ADAM_STEP)
-    second_hat = new_second_moment / (1.0 - BETA_TWO**ADAM_STEP)
+    new_first = BETA_ONE * old_first + (1.0 - BETA_ONE) * grad_low
+    new_second = BETA_TWO * old_second + (1.0 - BETA_TWO) * grad_low * grad_low
+    first_hat = new_first / (1.0 - BETA_ONE**ADAM_STEP)
+    second_hat = new_second / (1.0 - BETA_TWO**ADAM_STEP)
     direction = (first_hat / (jnp.sqrt(second_hat) + EPSILON)).astype(bf16)
-    column = spread(direction, "dp", strides).reshape(far * share, width)
-    column, token_rows = lax.optimization_barrier((column, token_rows))
-    token_grad = lax.all_gather(token_rows, "tensor", axis=0, tiled=True)
-    column = spread(column, "dp", fours).reshape(outer * share, width)
+    own = lax.axis_index("dp") // RING
+    new_first_moment, new_second_moment = (
+        lax.dynamic_index_in_dim(m.reshape(far, share, width), own, 0, keepdims=False)
+        for m in (new_first, new_second)
+    )
+    column = spread(direction, "dp", fours).reshape(outer * share, width)
     full_direction = spread(column, "fsdp").reshape(rank, width)
     update = jnp.dot(basis_perm, full_direction, preferred_element_type=f32)
     new_weight = (weight.astype(f32) - LEARN_RATE * update).astype(bf16)

time: 267 us -> 253 us (0.948)
  blocking collectives: 139 us -> 96.3 us
  waiting for transfers between devices: 45.7 us -> 68.5 us
  starting transfers between devices: 30.4 us -> 34.3 us
    all_to_all x6 -> x3, blocking collectives: 110 us -> 34.1 us  [spread(): lax.all_to_all(copies, axis, 0, 0, tiled=True, axis_index_groups=groups)]
    all_gather x0 -> x1, blocking collectives: none -> 50.9 us  [local(): line = lax.all_gather(second, 'dp', axis=0)]
    all_to_all x1 -> x4, waiting for transfers between devices: 1.5 us -> 44.1 us  [spread(): lax.all_to_all(copies, axis, 0, 0, tiled=True, axis_index_groups=groups)]
    all_to_all x1 -> x0, blocking collectives: 18.6 us -> none  [local(): lax.all_to_all(blocks, 'dp', 0, 0, tiled=True, axis_index_groups=strides)]
    all_to_all x1 -> x4, starting transfers between devices: 3.33 us -> 18.9 us  [spread(): lax.all_to_all(copies, axis, 0, 0, tiled=True, axis_index_groups=groups)]
    ppermute x2 -> x1, waiting for transfers between devices: 23.1 us -> 14.9 us  [ring_of_four(): following = lax.ppermute(block, axis, ahead)]
    ppermute x2 -> x1, waiting for transfers between devices: 9.77 us -> 4.57 us  [ring_of_four(): far_back = lax.ppermute(preceding[half:], axis, behind)]
    ppermute x2 -> x1, starting transfers between devices: 6.87 us -> 2.04 us  [ring_of_four(): far_front = lax.ppermute(following[:half], axis, ahead)]
  transfers between devices with their start and end apart: 13 -> 12, of which waited for: 7 -> 7; matrix products, arithmetic and copies ran while one was open for 9% -> 12% of each run, Pallas kernels for 0% -> 0%
where the time goes in v4:
time: 253 us; the launch traced here: 252 us
  blocking collectives  96.3 us (38%)
  waiting for transfers between devices  68.5 us (27%)
  starting transfers between devices  34.3 us (14%)
  matrix products  17.8 us (7%)
  local copies, waits for them, and re-layouts  16.5 us (7%)
  between operations  14.2 us (6%)
  other arithmetic  4.41 us (2%)
    all_gather x1, blocking collectives, local(): line = lax.all_gather(second, 'dp', axis=0)  50.9 us
    all_to_all x4, waiting for transfers between devices, spread(): lax.all_to_all(copies, axis, 0, 0, tiled=True, axis_index_groups=groups)  44.1 us
    all_to_all x3, blocking collectives, spread(): lax.all_to_all(copies, axis, 0, 0, tiled=True, axis_index_groups=groups)  34.1 us
    all_to_all x4, starting transfers between devices, spread(): lax.all_to_all(copies, axis, 0, 0, tiled=True, axis_index_groups=groups)  18.9 us
    ppermute x1, waiting for transfers between devices, ring_of_four(): following = lax.ppermute(block, axis, ahead)  14.9 us
    all_to_all x1, blocking collectives, local(): lax.all_to_all(blocks, 'dp', 0, 0, tiled=True, axis_index_groups=fours)  11.3 us
    unnamed x27, local copies, waits for them, and re-layouts  7.72 us
    dot_general x2, matrix products, local(): preact = jnp.dot(tokens, side, preferred_element_type=f32)  7.69 us
  transfers between devices with their start and end apart: 12, of which 7 were waited for; matrix products, arithmetic and copies ran while one was open for 12% of the time, Pallas kernels for 0%

profile of v4, /device:TPU:32, one launch (start us, length us, event | category | flops | bytes accessed | tf_op | source)
XLA Modules:
  0.0 252.0 jit_solution(10540775056260064053)
XLA Ops:
  8.2 17.5 %all_to_all.45 = bf16[8,20,1152]{2,1,0:T(8,128)(2,1)S(1)} all-to-all(bf16[8,20,1152]{2,1,0:T(8,128)(2,1)S(1)} %broadcast_in_dim.16), channel_id=1, replica_groups=mesh['dp'=16,'fsdp'=8,'tensor'=4] {'fsdp'}, dimensions={0} | all-to-all | bytes 737280 | tf_op jit(solution)/shard_map/all_to_all | solution.py:25
  26.9 8.0 %all_to_all.46 = bf16[2,20,704]{2,1,0:T(8,128)(2,1)S(1)} all-to-all(bf16[2,20,704]{2,1,0:T(8,128)(2,1)S(1)} %broadcast_in_dim.17), channel_id=1, replica_groups={{0,4},{8,12},{16,20},{24,28},{1,5},{9,13},{17,21},{25,29},{2,6},{10,14}..., dimensions={0} | all-to-all | bytes 112640 | tf_op jit(solution)/shard_map/all_to_all | solution.py:25
  34.9 50.9 %all_gather.9 = bf16[16,40,704]{2,1,0:T(8,128)(2,1)S(1)} all-gather(bf16[1,40,704]{2,1,0:T(8,128)(2,1)S(1)} %all_gather_reshape.3), channel_id=1, replica_groups=mesh['dp'=16,'fsdp'=8,'tensor'=4] {'dp'}, dimensions={0}, use_global_device_ids=true | all-gather | bytes 957440 | tf_op jit(solution)/shard_map/all_gather | solution.py:69
  85.8 1.9 collective-permute-start
  87.7 3.9 %collective-permute-start.2 = (bf16[16,40,704]{2,1,0:T(8,128)(2,1)S(1)}, bf16[16,40,704]{2,1,0:T(8,128)(2,1)S(1)}, u32[]{:S(2)}, u32[]{:S(2)}) collective-permute-start(bf16[16,40,704]{2,1,0:T(8,128)(2,1)S(1)} %all_gather.9), channel_id=1, source_target_pairs={{0,8},{4,12},{8,16},{12,20},{16,24},{20,28},{24,0},{28,4},{1,9},{5... | collective-permute-start | bytes 2703368 | tf_op jit(solution)/shard_map/ppermute | solution.py:34
  91.6 14.9 %collective-permute-done = bf16[16,40,704]{2,1,0:T(8,128)(2,1)S(1)} collective-permute-done((bf16[16,40,704]{2,1,0:T(8,128)(2,1)S(1)}, bf16[16,40,704]{2,1,0:T(8,128)(2,1)S(1)}, u32[]{:S(2)}, u32[]{:S(2)}) %collective-permute-start) | collective-permute-done | bytes 901152 | tf_op jit(solution)/shard_map/ppermute | solution.py:33
  107.4 2.0 collective-permute-start.1
  111.2 3.9 %collective-permute-start.3 = (bf16[8,40,704]{2,1,0:T(8,128)(2,1)}, bf16[8,40,704]{2,1,0:T(8,128)(2,1)}, u32[]{:S(2)}, u32[]{:S(2)}) collective-permute-start(bf16[8,40,704]{2,1,0:T(8,128)(2,1)} %slice.41), channel_id=1, source_target_pairs={{0,8},{4,12},{8,16},{12,20},{16,24},{20,28},{24,0},{28,4},{1,9},{5... | collective-permute-start | bytes 1351688 | tf_op jit(solution)/shard_map/ppermute | solution.py:36
  115.2 1.8 slice.36
  116.9 1.9 copy.24
  118.9 4.6 %collective-permute-done.3 = bf16[8,40,704]{2,1,0:T(8,128)(2,1)} collective-permute-done((bf16[8,40,704]{2,1,0:T(8,128)(2,1)}, bf16[8,40,704]{2,1,0:T(8,128)(2,1)}, u32[]{:S(2)}, u32[]{:S(2)}) %collective-permute-start.3) | collective-permute-done | bytes 450592 | tf_op jit(solution)/shard_map/ppermute | solution.py:36
  123.5 1.3 maximum_bitcast_fusion
  126.2 1.9 copy-done.1
  129.4 3.3 %all-to-all-start.2 = ((bf16[4,64,256]{2,1,0:T(8,128)(2,1)}), bf16[4,64,256]{2,1,0:T(8,128)(2,1)S(1)}, u32[]{:S(2)}, u32[]{:S(2)}) async-start(bf16[4,64,256]{2,1,0:T(8,128)(2,1)} %broadcast_in_dim.18), calls=%async_computation.2 | async-start | bytes 262144 | tf_op jit(solution)/shard_map/all_to_all | solution.py:25
  132.7 3.1 %multiply_convert_fusion.3 = bf16[256,640]{0,1:T(8,128)(2,1)S(1)} fusion(bf16[256,2560]{1,0:T(8,128)(2,1)S(1)} %copy-done, bf16[2560,704]{1,0:T(8,128)(2,1)} %bitcast.55, bf16[256,640]{0,1:T(8,128)(2,1)S(1)} %copy-done.6), kind=kOutput, calls=%fused_computation.25 | convolution fusion | flops 840499200 | bytes 5242880 | tf_op jit(solution)/shard_map/dot_general | solution.py:84
  135.8 1.5 all-to-all-done.2
  138.0 5.6 %all-to-all-start.3 = ((f32[4,2,2,1792]{3,2,1,0:T(2,128)}), f32[4,2,2,1792]{3,2,1,0:T(2,128)S(1)}, u32[]{:S(2)}, u32[]{:S(2)}) async-start(f32[4,2,2,1792]{3,2,1,0:T(2,128)} %broadcast_in_dim.19), calls=%async_computation.3 | async-start | bytes 229376 | tf_op jit(solution)/shard_map/all_to_all | solution.py:25
  143.9 4.6 %fusion.26 = f32[256,1152]{1,0:T(8,128)S(1)} fusion(bf16[256,2560]{1,0:T(8,128)(2,1)S(1)} %copy-done, bf16[2560,1152]{1,0:T(8,128)(2,1)} %all-gather.3.cloned.1.call-done), kind=kOutput, calls=%fused_computation.48 | convolution fusion | flops 1509949440 | bytes 8388608 | tf_op jit(solution)/shard_map/dot_general | solution.py:84
  149.6 1.0 pad_maximum_fusion.2
  150.6 7.8 %all-to-all-done.3 = f32[4,2,2,1792]{3,2,1,0:T(2,128)S(1)} async-done(((f32[4,2,2,1792]{3,2,1,0:T(2,128)}), f32[4,2,2,1792]{3,2,1,0:T(2,128)S(1)}, u32[]{:S(2)}, u32[]{:S(2)}) %all-to-all-start.3) | async-done | bytes 114720 | tf_op jit(solution)/shard_map/all_to_all | solution.py:25
  158.3 3.6 %all-to-all-start.4 = ((bf16[8,32,1792]{2,1,0:T(8,128)(2,1)}), bf16[8,32,1792]{2,1,0:T(8,128)(2,1)S(1)}, u32[]{:S(2)}, u32[]{:S(2)}) async-start(bf16[8,32,1792]{2,1,0:T(8,128)(2,1)} %bitcast.16), calls=%async_computation.4 | async-start | bytes 1835008 | tf_op jit(solution)/shard_map/all_to_all | solution.py:94
  161.9 5.4 %fusion.10 = f32[256,2560]{1,0:T(8,128)S(1)} fusion(bf16[2560,1152]{1,0:T(8,128)(2,1)} %all-gather.3.cloned.1.call-done, f32[256,1152]{1,0:T(8,128)} %copy-done.11, bf16[256,1792]{1,0:T(8,128)(2,1)} %param.7), kind=kOutput, calls=%fused_computation.15 | convolution fusion | flops 1512898560 | bytes 10289152 | tf_op jit(solution)/shard_map/dot_general | solution.py:90
  167.3 2.3 fusion
  169.6 4.8 %all-to-all-done.4 = bf16[8,32,1792]{2,1,0:T(8,128)(2,1)S(1)} async-done(((bf16[8,32,1792]{2,1,0:T(8,128)(2,1)}), bf16[8,32,1792]{2,1,0:T(8,128)(2,1)S(1)}, u32[]{:S(2)}, u32[]{:S(2)}) %all-to-all-start.4) | async-done | bytes 917536 | tf_op jit(solution)/shard_map/all_to_all | solution.py:94
  174.6 11.3 %all_to_all.47 = bf16[4,8,1792]{2,1,0:T(8,128)(2,1)S(1)} all-to-all(bf16[4,8,1792]{2,1,0:T(8,128)(2,1)S(1)} %bitcast.63), channel_id=1, replica_groups={{0,32,64,96},{128,160,192,224},{256,288,320,352},{384,416,448,480},{1,3..., dimensions={0} | all-to-all | bytes 229376 | tf_op jit(solution)/shard_map/all_to_all | solution.py:99
  186.6 6.3 %all-to-all-start.6 = ((bf16[4,8,1792]{2,1,0:T(8,128)(2,1)}), bf16[4,8,1792]{2,1,0:T(8,128)(2,1)S(1)}, u32[]{:S(2)}, u32[]{:S(2)}) async-start(bf16[4,8,1792]{2,1,0:T(8,128)(2,1)} %broadcast_in_dim.20), calls=%async_computation.6 | async-start | bytes 229376 | tf_op jit(solution)/shard_map/all_to_all | solution.py:25
  193.0 13.5 %all-to-all-done.6 = bf16[4,8,1792]{2,1,0:T(8,128)(2,1)S(1)} async-done(((bf16[4,8,1792]{2,1,0:T(8,128)(2,1)}), bf16[4,8,1792]{2,1,0:T(8,128)(2,1)S(1)}, u32[]{:S(2)}, u32[]{:S(2)}) %all-to-all-start.6) | async-done | bytes 114720 | tf_op jit(solution)/shard_map/all_to_all | solution.py:25
  206.6 8.6 %all_to_all.48 = bf16[4,8,1792]{2,1,0:T(8,128)(2,1)S(1)} all-to-all(bf16[4,8,1792]{2,1,0:T(8,128)(2,1)S(1)} %broadcast_in_dim.21), channel_id=1, replica_groups={{0,32,64,96},{128,160,192,224},{256,288,320,352},{384,416,448,480},{1,3..., dimensions={0} | all-to-all | bytes 229376 | tf_op jit(solution)/shard_map/all_to_all | solution.py:25
  215.2 1.0 broadcast_in_dim.23
  216.2 3.7 %all-to-all-start.8 = ((bf16[8,32,1792]{2,1,0:T(8,128)(2,1)}), bf16[8,32,1792]{2,1,0:T(8,128)(2,1)S(1)}, u32[]{:S(2)}, u32[]{:S(2)}) async-start(bf16[8,32,1792]{2,1,0:T(8,128)(2,1)} %broadcast_in_dim.23), calls=%async_computation.9 | async-start | bytes 1835008 | tf_op jit(solution)/shard_map/all_to_all | solution.py:25
  220.7 21.4 %all-to-all-done.8 = bf16[8,32,1792]{2,1,0:T(8,128)(2,1)S(1)} async-done(((bf16[8,32,1792]{2,1,0:T(8,128)(2,1)}), bf16[8,32,1792]{2,1,0:T(8,128)(2,1)S(1)}, u32[]{:S(2)}, u32[]{:S(2)}) %all-to-all-start.8) | async-done | bytes 917536 | tf_op jit(solution)/shard_map/all_to_all | solution.py:25
  243.0 2.5 copy.26
  (70 shorter events, 12.2 us)
Async XLA Ops:
  7.2 121.0 %copy-start = (bf16[256,2560]{1,0:T(8,128)(2,1)S(1)}, bf16[256,2560]{1,0:T(8,128)(2,1)}, u32[]{:S(2)}) copy-start(bf16[256,2560]{1,0:T(8,128)(2,1)} %param.6) | copy-start | bytes 3932164
  7.2 136.7 %all-gather.3.cloned.1.call-start = ((), (), s32[]{:S(2)}) async-start(), calls=%async_computation.10 | async-start | bytes 6266880 | tf_op jit(solution)/shard_map/all_gather | solution.py:65
  8.1 18.4 %copy-start.10 = (bf16[20,256]{1,0:T(8,128)(2,1)S(1)}, bf16[20,256]{1,0:T(8,128)(2,1)}, u32[]{:S(2)}) copy-start(bf16[20,256]{1,0:T(8,128)(2,1)} %param.9) | copy-start | bytes 30724
  8.2 18.7 %slice-start = ((bf16[20,1792]{1,0:T(8,128)(2,1)}), bf16[20,640]{1,0:T(8,128)(2,1)S(1)}, s32[]{:S(2)}) async-start(bf16[20,1792]{1,0:T(8,128)(2,1)} %param.8), calls=%async_computation.13 | async-start | bytes 61440 | tf_op jit(solution)/shard_map/slice | solution.py:66
  85.8 20.8 %collective-permute-start = (bf16[16,40,704]{2,1,0:T(8,128)(2,1)S(1)}, bf16[16,40,704]{2,1,0:T(8,128)(2,1)S(1)}, u32[]{:S(2)}, u32[]{:S(2)}) collective-permute-start(bf16[16,40,704]{2,1,0:T(8,128)(2,1)S(1)} %all_gather.9), channel_id=1, source_target_pairs={{8,0},{12,4},{16,8},{20,12},{24,16},{28,20},{0,24},{4,28},{9,1},{1... | collective-permute-start | bytes 2703368 | tf_op jit(solution)/shard_map/ppermute | solution.py:33
  87.7 21.7 %collective-permute-start.2 = (bf16[16,40,704]{2,1,0:T(8,128)(2,1)S(1)}, bf16[16,40,704]{2,1,0:T(8,128)(2,1)S(1)}, u32[]{:S(2)}, u32[]{:S(2)}) collective-permute-start(bf16[16,40,704]{2,1,0:T(8,128)(2,1)S(1)} %all_gather.9), channel_id=1, source_target_pairs={{0,8},{4,12},{8,16},{12,20},{16,24},{20,28},{24,0},{28,4},{1,9},{5... | collective-permute-start | bytes 2703368 | tf_op jit(solution)/shard_map/ppermute | solution.py:34
  107.4 11.5 %copy-start.8 = (f32[2,1792]{1,0:T(2,128)S(1)}, f32[2,1792]{1,0:T(2,128)}, u32[]{:S(2)}) copy-start(f32[2,1792]{1,0:T(2,128)} %param.11) | copy-start | bytes 43012
  107.4 11.5 %copy-start.9 = (f32[2,1792]{1,0:T(2,128)S(1)}, f32[2,1792]{1,0:T(2,128)}, u32[]{:S(2)}) copy-start(f32[2,1792]{1,0:T(2,128)} %param.10) | copy-start | bytes 43012
  107.4 11.5 %collective-permute-start.1 = (bf16[8,40,704]{2,1,0:T(8,128)(2,1)}, bf16[8,40,704]{2,1,0:T(8,128)(2,1)}, u32[]{:S(2)}, u32[]{:S(2)}) collective-permute-start(bf16[8,40,704]{2,1,0:T(8,128)(2,1)} %slice.40), channel_id=1, source_target_pairs={{8,0},{12,4},{16,8},{20,12},{24,16},{28,20},{0,24},{4,28},{9,1},{1... | collective-permute-start | bytes 1351688 | tf_op jit(solution)/shard_map/ppermute | solution.py:35
  109.4 0.9 copy-start.3
  111.2 12.2 %collective-permute-start.3 = (bf16[8,40,704]{2,1,0:T(8,128)(2,1)}, bf16[8,40,704]{2,1,0:T(8,128)(2,1)}, u32[]{:S(2)}, u32[]{:S(2)}) collective-permute-start(bf16[8,40,704]{2,1,0:T(8,128)(2,1)} %slice.41), channel_id=1, source_target_pairs={{0,8},{4,12},{8,16},{12,20},{16,24},{20,28},{24,0},{28,4},{1,9},{5... | collective-permute-start | bytes 1351688 | tf_op jit(solution)/shard_map/ppermute | solution.py:36
  118.8 5.9 %copy-start.4 = (bf16[16,40,704]{2,1,0:T(8,128)(2,1)S(1)}, bf16[16,40,704]{2,1,0:T(8,128)(2,1)}, u32[]{:S(2)}) copy-start(bf16[16,40,704]{2,1,0:T(8,128)(2,1)} %copy-done.3) | copy-start | bytes 2703364
  126.2 1.9 copy-start.1
  126.2 6.5 %copy-start.6 = (bf16[256,640]{0,1:T(8,128)(2,1)S(1)}, bf16[256,640]{0,1:T(8,128)(2,1)}, u32[]{:S(2)}) copy-start(bf16[256,640]{0,1:T(8,128)(2,1)} %copy.24) | copy-start | bytes 983044
  129.4 7.9 %all-to-all-start.2 = ((bf16[4,64,256]{2,1,0:T(8,128)(2,1)}), bf16[4,64,256]{2,1,0:T(8,128)(2,1)S(1)}, u32[]{:S(2)}, u32[]{:S(2)}) async-start(bf16[4,64,256]{2,1,0:T(8,128)(2,1)} %broadcast_in_dim.18), calls=%async_computation.2 | async-start | bytes 262144 | tf_op jit(solution)/shard_map/all_to_all | solution.py:25
  138.0 20.4 %all-to-all-start.3 = ((f32[4,2,2,1792]{3,2,1,0:T(2,128)}), f32[4,2,2,1792]{3,2,1,0:T(2,128)S(1)}, u32[]{:S(2)}, u32[]{:S(2)}) async-start(f32[4,2,2,1792]{3,2,1,0:T(2,128)} %broadcast_in_dim.19), calls=%async_computation.3 | async-start | bytes 229376 | tf_op jit(solution)/shard_map/all_to_all | solution.py:25
  143.9 4.6 %copy-start.7 = (bf16[256,1792]{1,0:T(8,128)(2,1)S(1)}, bf16[256,1792]{1,0:T(8,128)(2,1)}, u32[]{:S(2)}) copy-start(bf16[256,1792]{1,0:T(8,128)(2,1)} %param.7) | copy-start | bytes 2752516
  148.5 1.0 copy-start.11
  158.3 16.1 %all-to-all-start.4 = ((bf16[8,32,1792]{2,1,0:T(8,128)(2,1)}), bf16[8,32,1792]{2,1,0:T(8,128)(2,1)S(1)}, u32[]{:S(2)}, u32[]{:S(2)}) async-start(bf16[8,32,1792]{2,1,0:T(8,128)(2,1)} %bitcast.16), calls=%async_computation.4 | async-start | bytes 1835008 | tf_op jit(solution)/shard_map/all_to_all | solution.py:94
  161.9 44.6 %reduce-scatter.2.cloned.1.call-start = ((), (), s32[]{:S(2)}) async-start(), calls=%async_computation.11 | async-start | bytes 1638400 | tf_op jit(solution)/shard_map/reduce_scatter | solution.py:96
  161.9 5.4 %copy-start.2 = (bf16[16,4,40,704]{3,2,1,0:T(8,128)(2,1)S(1)}, bf16[16,4,40,704]{3,2,1,0:T(8,128)(2,1)}, u32[]{:S(2)}) copy-start(bf16[16,4,40,704]{3,2,1,0:T(8,128)(2,1)} %copy-done.1) | copy-start | bytes 10813444
  186.6 19.9 %all-to-all-start.6 = ((bf16[4,8,1792]{2,1,0:T(8,128)(2,1)}), bf16[4,8,1792]{2,1,0:T(8,128)(2,1)S(1)}, u32[]{:S(2)}, u32[]{:S(2)}) async-start(bf16[4,8,1792]{2,1,0:T(8,128)(2,1)} %broadcast_in_dim.20), calls=%async_computation.6 | async-start | bytes 229376 | tf_op jit(solution)/shard_map/all_to_all | solution.py:25
  192.8 50.1 %all-gather.5.cloned.1.call-start = ((), (), s32[]{:S(2)}) async-start(), calls=%async_computation.12 | async-start | bytes 1638400 | tf_op jit(solution)/shard_map/all_gather | solution.py:103
  216.2 25.8 %copy-start.5 = (bf16[20,1792]{1,0:T(8,128)(2,1)S(1)}, bf16[20,1792]{1,0:T(8,128)(2,1)}, u32[]{:S(2)}) copy-start(bf16[20,1792]{1,0:T(8,128)(2,1)} %param.8) | copy-start | bytes 215044
  216.2 25.8 %all-to-all-start.8 = ((bf16[8,32,1792]{2,1,0:T(8,128)(2,1)}), bf16[8,32,1792]{2,1,0:T(8,128)(2,1)S(1)}, u32[]{:S(2)}, u32[]{:S(2)}) async-start(bf16[8,32,1792]{2,1,0:T(8,128)(2,1)} %broadcast_in_dim.23), calls=%async_computation.9 | async-start | bytes 1835008 | tf_op jit(solution)/shard_map/all_to_all | solution.py:25
Sparse Core Ops, SparseCore 0:
  26.6 91.1 all-gather.2
  174.6 24.5 reduce-scatter.1
  206.6 31.0 all-gather.4

commit v5 on v4

--- a/solution.py
+++ b/solution.py
@@ -25,20 +25,19 @@
     return lax.all_to_all(copies, axis, 0, 0, tiled=True, axis_index_groups=groups)
 
 
-def ring_of_four(block, axis, step, place):
+def ring_permutes(axis, step):
     count = lax.axis_size(axis)
     ahead = [((i + step) % count, i) for i in range(count)]
     behind = [(i, (i + step) % count) for i in range(count)]
-    half = block.shape[0] // 2
-    following = lax.ppermute(block, axis, ahead)
-    preceding = lax.ppermute(block, axis, behind)
-    far_front = lax.ppermute(following[:half], axis, ahead)
-    far_back = lax.ppermute(preceding[half:], axis, behind)
-    far = jnp.concatenate([far_front, far_back], axis=0)
-    stacked = jnp.stack([block, following, far, preceding])
-    return lambda wanted: lax.dynamic_index_in_dim(
-        stacked, lax.rem(wanted - place + RING, RING), 0, keepdims=False
-    )
+    return (lambda x: lax.ppermute(x, axis, ahead)), (lambda x: lax.ppermute(x, axis, behind))
+
+
+def by_class(blocks, place):
+    stacked = jnp.stack(blocks)
+    return [
+        lax.dynamic_index_in_dim(stacked, lax.rem(wanted - place + RING, RING), 0, keepdims=False)
+        for wanted in range(RING)
+    ]
 
 
 def local(tokens, cotangent, weight, basis, first_moment, second_moment):
@@ -60,35 +59,47 @@
     strides = [[i + RING * j for j in range(far)] for i in range(RING)]
     fours = [[RING * j + i for i in range(RING)] for j in range(far)]
     pair_rows = PAIR * rows
-    half = width * 9 // 14
-    plane = spread(weight[:, :half], "fsdp").reshape(inner * rows, half)
-    weight_a = lax.all_gather(plane, "dp", axis=0, tiled=True)
-    second = jnp.concatenate([weight[:, half:], basis_part], axis=1)
-    plane, second = lax.optimization_barrier((plane, second))
-    second = spread(second, "fsdp", pairs).reshape(pair_rows, width - half + part)
+    half = width * 4 // 7
+    first = jnp.concatenate([weight[:, :half], basis_part], axis=1)
+    plane = spread(first, "fsdp").reshape(inner * rows, half + part)
+    full_a = lax.all_gather(plane, "dp", axis=0, tiled=True)
+    plane, second = lax.optimization_barrier((plane, weight[:, half:]))
+    second = spread(second, "fsdp", pairs).reshape(pair_rows, width - half)
     line = lax.all_gather(second, "dp", axis=0)
-    pick = ring_of_four(line, "fsdp", PAIR, lax.axis_index("fsdp") // PAIR)
-    full_b = jnp.stack([pick(r) for r in range(RING)], axis=1).reshape(depth, width - half + part)
     moments = jnp.stack([first_moment, second_moment])
-    full_b, moments = lax.optimization_barrier((full_b, moments))
+    line, moments = lax.optimization_barrier((line, moments))
+    from_ahead, from_behind = ring_permutes("fsdp", PAIR)
+    ahead, behind = from_ahead(line), from_behind(line)
     moments = spread(moments, "dp", strides)
-    weight_b, full_basis = full_b[:, : width - half], full_b[:, width - half :]
+    ahead, behind, moments = lax.optimization_barrier((ahead, behind, moments))
+    old_first, old_second = (moments[:, i].reshape(far * share, width) for i in range(2))
+    across = from_ahead(ahead[: outer // 2]), from_behind(behind[outer // 2 :])
 
+    def grad_of_preact(side, wanted):
+        preact = jnp.dot(tokens, side, preferred_element_type=f32)
+        return (wanted.astype(f32) * silu_slope(preact)).astype(bf16)
+
+    weight_a, full_basis = full_a[:, :half], full_a[:, half:]
     projected_part = lax.dot_general(
         full_basis, tokens, (((0,), (1,)), ((), ())), preferred_element_type=f32
     ).astype(bf16)
     projected = spread(projected_part, "tensor").reshape(rank, tokens.shape[0])
+    grad_pre_a = grad_of_preact(weight_a, cotangent[:, :half])
+    across, grad_pre_a = lax.optimization_barrier((across, grad_pre_a))
 
-    grad_pre, grad_part = [], []
-    for side, wanted in ((weight_a, cotangent[:, :half]), (weight_b, cotangent[:, half:])):
-        preact = jnp.dot(tokens, side, preferred_element_type=f32)
-        grad_pre.append((wanted.astype(f32) * silu_slope(preact)).astype(bf16))
-        grad_part.append(jnp.dot(projected, grad_pre[-1], preferred_element_type=f32).astype(bf16))
-    grad_part, moments = lax.optimization_barrier((jnp.concatenate(grad_part, axis=1), moments))
-    old_first, old_second = (moments[:, i].reshape(far * share, width) for i in range(2))
+    blocks = by_class([line, ahead, jnp.concatenate(across), behind], lax.axis_index("fsdp") // PAIR)
+    weight_b = jnp.stack(blocks, axis=1).reshape(depth, width - half)
+    grad_pre_b = grad_of_preact(weight_b, cotangent[:, half:])
+    grad_part = jnp.concatenate(
+        [
+            jnp.dot(projected, g, preferred_element_type=f32).astype(bf16)
+            for g in (grad_pre_a, grad_pre_b)
+        ],
+        axis=1,
+    )
     partial_rows = sum(
         lax.dot_general(g, w, (((1,), (1,)), ((), ())), preferred_element_type=f32)
-        for g, w in zip(grad_pre, (weight_a, weight_b))
+        for g, w in ((grad_pre_a, weight_a), (grad_pre_b, weight_b))
     ).astype(bf16)
 
     landed = lax.all_to_all(grad_part.reshape(inner, outer * share, width), "fsdp", 0, 0, tiled=True)

time: 253 us -> 247 us (0.976)
  blocking collectives: 96.3 us -> 86.7 us
  waiting for transfers between devices: 68.5 us -> 60 us
  local copies, waits for them, and re-layouts: 16.5 us -> 22.4 us
  starting transfers between devices: 34.3 us -> 37.7 us
    ppermute x4, waiting for transfers between devices: 19.5 us -> 4.4 us  [the longest x2 4.39 us: ring_permutes(): lax.ppermute(x, axis, behind)]
    all_to_all x3 -> x2, blocking collectives: 34.1 us -> 26.2 us  [spread(): lax.all_to_all(copies, axis, 0, 0, tiled=True, axis_index_groups=groups)]
    slice x6, local copies, waits for them, and re-layouts: 4.31 us -> 7.97 us  [the longest x2 2.74 us: local(): across = (from_ahead(ahead[:outer // 2]), from_behind(behind[outer // 2:]))]
    all_to_all x4 -> x5, waiting for transfers between devices: 44.1 us -> 47.5 us  [spread(): lax.all_to_all(copies, axis, 0, 0, tiled=True, axis_index_groups=groups)]
    all_to_all x4 -> x5, starting transfers between devices: 18.9 us -> 22.2 us  [spread(): lax.all_to_all(copies, axis, 0, 0, tiled=True, axis_index_groups=groups)]
    all_to_all x1, waiting for transfers between devices: 4.82 us -> 8.01 us  [local(): lax.all_to_all(grad_part.reshape(inner, outer * share, width), 'fsdp', 0,...]
    unnamed x27 -> x20, local copies, waits for them, and re-layouts: 7.72 us -> 9.32 us
  transfers between devices with their start and end apart: 12 -> 13, of which waited for: 7 -> 6; matrix products, arithmetic and copies ran while one was open for 12% -> 15% of each run, Pallas kernels for 0% -> 0%
where the time goes in v5:
time: 247 us; the launch traced here: 245 us
  blocking collectives  86.7 us (35%)
  waiting for transfers between devices  60 us (24%)
  starting transfers between devices  37.7 us (15%)
  local copies, waits for them, and re-layouts  22.4 us (9%)
  matrix products  18.2 us (7%)
  between operations  14.1 us (6%)
  other arithmetic  6.05 us (2%)
    all_gather x1, blocking collectives, local(): line = lax.all_gather(second, 'dp', axis=0)  49.4 us
    all_to_all x5, waiting for transfers between devices, spread(): lax.all_to_all(copies, axis, 0, 0, tiled=True, axis_index_groups=groups)  47.5 us
    all_to_all x2, blocking collectives, spread(): lax.all_to_all(copies, axis, 0, 0, tiled=True, axis_index_groups=groups)  26.2 us
    all_to_all x5, starting transfers between devices, spread(): lax.all_to_all(copies, axis, 0, 0, tiled=True, axis_index_groups=groups)  22.2 us
    all_to_all x1, blocking collectives, local(): lax.all_to_all(blocks, 'dp', 0, 0, tiled=True, axis_index_groups=fours)  11 us
    unnamed x20, local copies, waits for them, and re-layouts  9.32 us
    dot_general x2, matrix products, local(): lax.dot_general(g, w, (((1,), (1,)), ((), ())), preferred_element_type=f32)  8.55 us
    all_to_all x1, waiting for transfers between devices, local(): lax.all_to_all(grad_part.reshape(inner, outer * share, width), 'fsdp', 0,...  8.01 us
  transfers between devices with their start and end apart: 13, of which 6 were waited for; matrix products, arithmetic and copies ran while one was open for 15% of the time, Pallas kernels for 0%

profile of v5, /device:TPU:32, one launch (start us, length us, event | category | flops | bytes accessed | tf_op | source)
XLA Modules:
  0.0 245.1 jit_solution(18019295057279315089)
XLA Ops:
  9.2 17.5 %all_to_all.45 = bf16[8,20,1088]{2,1,0:T(8,128)(2,1)S(1)} all-to-all(bf16[8,20,1088]{2,1,0:T(8,128)(2,1)S(1)} %broadcast_in_dim.16), channel_id=1, replica_groups=mesh['dp'=16,'fsdp'=8,'tensor'=4] {'fsdp'}, dimensions={0} | all-to-all | bytes 696320 | tf_op jit(solution)/shard_map/all_to_all | solution.py:25
  29.0 3.3 %all-to-all-start.2 = ((bf16[2,20,768]{2,1,0:T(8,128)(2,1)}), bf16[2,20,768]{2,1,0:T(8,128)(2,1)S(1)}, u32[]{:S(2)}, u32[]{:S(2)}) async-start(bf16[2,20,768]{2,1,0:T(8,128)(2,1)} %broadcast_in_dim.18), calls=%async_computation.2 | async-start | bytes 147456 | tf_op jit(solution)/shard_map/all_to_all | solution.py:25
  33.1 4.9 %all-to-all-done.2 = bf16[2,20,768]{2,1,0:T(8,128)(2,1)S(1)} async-done(((bf16[2,20,768]{2,1,0:T(8,128)(2,1)}), bf16[2,20,768]{2,1,0:T(8,128)(2,1)S(1)}, u32[]{:S(2)}, u32[]{:S(2)}) %all-to-all-start.2) | async-done | bytes 61472 | tf_op jit(solution)/shard_map/all_to_all | solution.py:25
  38.0 49.4 %all_gather.10 = bf16[16,40,768]{2,1,0:T(8,128)(2,1)S(1)} all-gather(bf16[1,40,768]{2,1,0:T(8,128)(2,1)S(1)} %all_gather_reshape.3), channel_id=1, replica_groups=mesh['dp'=16,'fsdp'=8,'tensor'=4] {'dp'}, dimensions={0}, use_global_device_ids=true | all-gather | bytes 1044480 | tf_op jit(solution)/shard_map/all_gather | solution.py:68
  87.4 4.1 %collective-permute-start = (bf16[16,40,768]{2,1,0:T(8,128)(2,1)S(1)}, bf16[16,40,768]{2,1,0:T(8,128)(2,1)S(1)}, u32[]{:S(2)}, u32[]{:S(2)}) collective-permute-start(bf16[16,40,768]{2,1,0:T(8,128)(2,1)S(1)} %all_gather.10), channel_id=1, source_target_pairs={{8,0},{12,4},{16,8},{20,12},{24,16},{28,20},{0,24},{4,28},{9,1},{1... | collective-permute-start | bytes 2949128 | tf_op jit(solution)/shard_map/ppermute | solution.py:32
  91.5 1.9 collective-permute-start.1
  94.1 7.1 %all-to-all-start.3 = ((f32[4,2,2,1792]{3,2,1,0:T(2,128)}), f32[4,2,2,1792]{3,2,1,0:T(2,128)S(1)}, u32[]{:S(2)}, u32[]{:S(2)}) async-start(f32[4,2,2,1792]{3,2,1,0:T(2,128)} %broadcast_in_dim.19), calls=%async_computation.3 | async-start | bytes 229376 | tf_op jit(solution)/shard_map/all_to_all | solution.py:25
  101.2 1.9 slice.35
  103.1 1.8 slice.37
  104.9 2.0 copy.28
  106.9 1.9 copy.29
  108.8 7.2 %all-to-all-done.3 = f32[4,2,2,1792]{3,2,1,0:T(2,128)S(1)} async-done(((f32[4,2,2,1792]{3,2,1,0:T(2,128)}), f32[4,2,2,1792]{3,2,1,0:T(2,128)S(1)}, u32[]{:S(2)}, u32[]{:S(2)}) %all-to-all-start.3) | async-done | bytes 114720 | tf_op jit(solution)/shard_map/all_to_all | solution.py:25
  117.0 3.2 %collective-permute-start.2 = (bf16[8,40,768]{2,1,0:T(8,128)(2,1)}, bf16[8,40,768]{2,1,0:T(8,128)(2,1)}, u32[]{:S(2)}, u32[]{:S(2)}) collective-permute-start(bf16[8,40,768]{2,1,0:T(8,128)(2,1)} %slice.33), channel_id=1, source_target_pairs={{8,0},{12,4},{16,8},{20,12},{24,16},{28,20},{0,24},{4,28},{9,1},{1... | collective-permute-start | bytes 1474568 | tf_op jit(solution)/shard_map/ppermute | solution.py:32
  120.2 1.9 slice.34
  122.0 2.6 %collective-permute-start.3 = (bf16[8,40,768]{2,1,0:T(8,128)(2,1)}, bf16[8,40,768]{2,1,0:T(8,128)(2,1)}, u32[]{:S(2)}, u32[]{:S(2)}) collective-permute-start(bf16[8,40,768]{2,1,0:T(8,128)(2,1)} %slice.34), channel_id=1, source_target_pairs={{0,8},{4,12},{8,16},{12,20},{16,24},{20,28},{24,0},{28,4},{1,9},{5... | collective-permute-start | bytes 1474568 | tf_op jit(solution)/shard_map/ppermute | solution.py:32
  124.7 5.2 %multiply_convert_fusion = bf16[256,1024]{0,1:T(8,128)(2,1)} fusion(bf16[256,1024]{0,1:T(8,128)(2,1)} %copy.28, bf16[256,2560]{1,0:T(8,128)(2,1)S(1)} %copy-done, bf16[2560,1088]{1,0:T(8,128)(2,1)} %all-gather.3.cloned.1.call-done), kind=kOutput, calls=%fused_computation.17 | convolution fusion | flops 1344798720 | bytes 7602176 | tf_op jit(solution)/shard_map/dot_general | solution.py:79
  129.9 4.4 %collective-permute-done.3 = bf16[8,40,768]{2,1,0:T(8,128)(2,1)} collective-permute-done((bf16[8,40,768]{2,1,0:T(8,128)(2,1)}, bf16[8,40,768]{2,1,0:T(8,128)(2,1)}, u32[]{:S(2)}, u32[]{:S(2)}) %collective-permute-start.3) | collective-permute-done | bytes 491552 | tf_op jit(solution)/shard_map/ppermute | solution.py:32
  134.3 1.6 convolution_convert_fusion.2
  136.5 3.3 %all-to-all-start.1 = ((bf16[4,64,256]{2,1,0:T(8,128)(2,1)}), bf16[4,64,256]{2,1,0:T(8,128)(2,1)S(1)}, u32[]{:S(2)}, u32[]{:S(2)}) async-start(bf16[4,64,256]{2,1,0:T(8,128)(2,1)} %broadcast_in_dim.17), calls=%async_computation.1 | async-start | bytes 262144 | tf_op jit(solution)/shard_map/all_to_all | solution.py:25
  141.1 1.6 pad_maximum_fusion
  143.5 1.9 copy-done.1
  148.5 3.6 %all-to-all-start.4 = ((bf16[8,32,1792]{2,1,0:T(8,128)(2,1)}), bf16[8,32,1792]{2,1,0:T(8,128)(2,1)S(1)}, u32[]{:S(2)}, u32[]{:S(2)}) async-start(bf16[8,32,1792]{2,1,0:T(8,128)(2,1)} %bitcast.17), calls=%async_computation.4 | async-start | bytes 1835008 | tf_op jit(solution)/shard_map/all_to_all | solution.py:105
  152.1 3.4 %fusion.23 = f32[256,2560]{1,0:T(8,128)S(1)} fusion(bf16[256,768]{0,1:T(8,128)(2,1)S(1)} %multiply_convert_fusion.1, bf16[2560,768]{1,0:T(8,128)(2,1)} %bitcast.61), kind=kOutput, calls=%fused_computation.41 | convolution fusion | flops 1006632960 | bytes 6946816 | tf_op jit(solution)/shard_map/dot_general | solution.py:101
  155.5 5.2 %fusion.7 = bf16[256,2560]{1,0:T(8,128)(2,1)} fusion(f32[256,2560]{1,0:T(8,128)S(1)} %fusion.23, bf16[256,1024]{0,1:T(8,128)(2,1)S(1)} %copy-done.3, bf16[2560,1088]{1,0:T(8,128)(2,1)} %all-gather.3.cloned.1.call-done), kind=kOutput, calls=%fused_computation.7 | convolution fusion | flops 1343488000 | bytes 9699328 | tf_op jit(solution)/shard_map/dot_general | solution.py:101
  160.7 8.0 %all-to-all-done.4 = bf16[8,32,1792]{2,1,0:T(8,128)(2,1)S(1)} async-done(((bf16[8,32,1792]{2,1,0:T(8,128)(2,1)}), bf16[8,32,1792]{2,1,0:T(8,128)(2,1)S(1)}, u32[]{:S(2)}, u32[]{:S(2)}) %all-to-all-start.4) | async-done | bytes 917536 | tf_op jit(solution)/shard_map/all_to_all | solution.py:105
  168.9 11.0 %all_to_all.46 = bf16[4,8,1792]{2,1,0:T(8,128)(2,1)S(1)} all-to-all(bf16[4,8,1792]{2,1,0:T(8,128)(2,1)S(1)} %bitcast.67), channel_id=1, replica_groups={{0,32,64,96},{128,160,192,224},{256,288,320,352},{384,416,448,480},{1,3..., dimensions={0} | all-to-all | bytes 229376 | tf_op jit(solution)/shard_map/all_to_all | solution.py:110
  180.5 5.0 %all-to-all-start.6 = ((bf16[4,8,1792]{2,1,0:T(8,128)(2,1)}), bf16[4,8,1792]{2,1,0:T(8,128)(2,1)S(1)}, u32[]{:S(2)}, u32[]{:S(2)}) async-start(bf16[4,8,1792]{2,1,0:T(8,128)(2,1)} %broadcast_in_dim.20), calls=%async_computation.6 | async-start | bytes 229376 | tf_op jit(solution)/shard_map/all_to_all | solution.py:25
  185.7 14.1 %all-to-all-done.6 = bf16[4,8,1792]{2,1,0:T(8,128)(2,1)S(1)} async-done(((bf16[4,8,1792]{2,1,0:T(8,128)(2,1)}), bf16[4,8,1792]{2,1,0:T(8,128)(2,1)S(1)}, u32[]{:S(2)}, u32[]{:S(2)}) %all-to-all-start.6) | async-done | bytes 114720 | tf_op jit(solution)/shard_map/all_to_all | solution.py:25
  199.9 8.8 %all_to_all.47 = bf16[4,8,1792]{2,1,0:T(8,128)(2,1)S(1)} all-to-all(bf16[4,8,1792]{2,1,0:T(8,128)(2,1)S(1)} %broadcast_in_dim.21), channel_id=1, replica_groups={{0,32,64,96},{128,160,192,224},{256,288,320,352},{384,416,448,480},{1,3..., dimensions={0} | all-to-all | bytes 229376 | tf_op jit(solution)/shard_map/all_to_all | solution.py:25
  209.7 3.6 %all-to-all-start.8 = ((bf16[8,32,1792]{2,1,0:T(8,128)(2,1)}), bf16[8,32,1792]{2,1,0:T(8,128)(2,1)S(1)}, u32[]{:S(2)}, u32[]{:S(2)}) async-start(bf16[8,32,1792]{2,1,0:T(8,128)(2,1)} %broadcast_in_dim.23), calls=%async_computation.9 | async-start | bytes 1835008 | tf_op jit(solution)/shard_map/all_to_all | solution.py:25
  214.0 21.3 %all-to-all-done.8 = bf16[8,32,1792]{2,1,0:T(8,128)(2,1)S(1)} async-done(((bf16[8,32,1792]{2,1,0:T(8,128)(2,1)}), bf16[8,32,1792]{2,1,0:T(8,128)(2,1)S(1)}, u32[]{:S(2)}, u32[]{:S(2)}) %all-to-all-start.8) | async-done | bytes 917536 | tf_op jit(solution)/shard_map/all_to_all | solution.py:25
  236.2 2.5 %copy.31 = bf16[256,2560]{1,0:T(8,128)(2,1)} copy(bf16[256,2560]{1,0:T(8,128)(2,1)} %all-gather.5.cloned.1.call-done) | data formatting | bytes 2621440
  (64 shorter events, 16.1 us)
Async XLA Ops:
  7.2 117.5 %copy-start = (bf16[256,2560]{1,0:T(8,128)(2,1)S(1)}, bf16[256,2560]{1,0:T(8,128)(2,1)}, u32[]{:S(2)}) copy-start(bf16[256,2560]{1,0:T(8,128)(2,1)} %param.6) | copy-start | bytes 3932164
  7.2 117.5 %all-gather.3.cloned.1.call-start = ((), (), s32[]{:S(2)}) async-start(), calls=%async_computation.10 | async-start | bytes 6266880 | tf_op jit(solution)/shard_map/all_gather | solution.py:65
  8.2 0.9 copy-start.6
  29.0 9.0 %all-to-all-start.2 = ((bf16[2,20,768]{2,1,0:T(8,128)(2,1)}), bf16[2,20,768]{2,1,0:T(8,128)(2,1)S(1)}, u32[]{:S(2)}, u32[]{:S(2)}) async-start(bf16[2,20,768]{2,1,0:T(8,128)(2,1)} %broadcast_in_dim.18), calls=%async_computation.2 | async-start | bytes 147456 | tf_op jit(solution)/shard_map/all_to_all | solution.py:25
  87.4 28.6 %collective-permute-start = (bf16[16,40,768]{2,1,0:T(8,128)(2,1)S(1)}, bf16[16,40,768]{2,1,0:T(8,128)(2,1)S(1)}, u32[]{:S(2)}, u32[]{:S(2)}) collective-permute-start(bf16[16,40,768]{2,1,0:T(8,128)(2,1)S(1)} %all_gather.10), channel_id=1, source_target_pairs={{8,0},{12,4},{16,8},{20,12},{24,16},{28,20},{0,24},{4,28},{9,1},{1... | collective-permute-start | bytes 2949128 | tf_op jit(solution)/shard_map/ppermute | solution.py:32
  91.5 24.6 %collective-permute-start.1 = (bf16[16,40,768]{2,1,0:T(8,128)(2,1)S(1)}, bf16[16,40,768]{2,1,0:T(8,128)(2,1)}, u32[]{:S(2)}, u32[]{:S(2)}) collective-permute-start(bf16[16,40,768]{2,1,0:T(8,128)(2,1)S(1)} %all_gather.10), channel_id=1, source_target_pairs={{0,8},{4,12},{8,16},{12,20},{16,24},{20,28},{24,0},{28,4},{1,9},{5... | collective-permute-start | bytes 2949128 | tf_op jit(solution)/shard_map/ppermute | solution.py:32
  94.1 21.9 %all-to-all-start.3 = ((f32[4,2,2,1792]{3,2,1,0:T(2,128)}), f32[4,2,2,1792]{3,2,1,0:T(2,128)S(1)}, u32[]{:S(2)}, u32[]{:S(2)}) async-start(f32[4,2,2,1792]{3,2,1,0:T(2,128)} %broadcast_in_dim.19), calls=%async_computation.3 | async-start | bytes 229376 | tf_op jit(solution)/shard_map/all_to_all | solution.py:25
  117.0 12.9 %collective-permute-start.2 = (bf16[8,40,768]{2,1,0:T(8,128)(2,1)}, bf16[8,40,768]{2,1,0:T(8,128)(2,1)}, u32[]{:S(2)}, u32[]{:S(2)}) collective-permute-start(bf16[8,40,768]{2,1,0:T(8,128)(2,1)} %slice.33), channel_id=1, source_target_pairs={{8,0},{12,4},{16,8},{20,12},{24,16},{28,20},{0,24},{4,28},{9,1},{1... | collective-permute-start | bytes 1474568 | tf_op jit(solution)/shard_map/ppermute | solution.py:32
  122.0 12.2 %collective-permute-start.3 = (bf16[8,40,768]{2,1,0:T(8,128)(2,1)}, bf16[8,40,768]{2,1,0:T(8,128)(2,1)}, u32[]{:S(2)}, u32[]{:S(2)}) collective-permute-start(bf16[8,40,768]{2,1,0:T(8,128)(2,1)} %slice.34), channel_id=1, source_target_pairs={{0,8},{4,12},{8,16},{12,20},{16,24},{20,28},{24,0},{28,4},{1,9},{5... | collective-permute-start | bytes 1474568 | tf_op jit(solution)/shard_map/ppermute | solution.py:32
  136.5 10.3 %all-to-all-start.1 = ((bf16[4,64,256]{2,1,0:T(8,128)(2,1)}), bf16[4,64,256]{2,1,0:T(8,128)(2,1)S(1)}, u32[]{:S(2)}, u32[]{:S(2)}) async-start(bf16[4,64,256]{2,1,0:T(8,128)(2,1)} %broadcast_in_dim.17), calls=%async_computation.1 | async-start | bytes 262144 | tf_op jit(solution)/shard_map/all_to_all | solution.py:25
  143.0 2.5 %copy-start.4 = (bf16[256,768]{0,1:T(8,128)(2,1)S(1)}, bf16[256,768]{0,1:T(8,128)(2,1)}, u32[]{:S(2)}) copy-start(bf16[256,768]{0,1:T(8,128)(2,1)} %copy.29) | copy-start | bytes 1179652
  143.5 1.9 copy-start.1
  145.5 1.7 copy-start.2
  148.5 20.2 %all-to-all-start.4 = ((bf16[8,32,1792]{2,1,0:T(8,128)(2,1)}), bf16[8,32,1792]{2,1,0:T(8,128)(2,1)S(1)}, u32[]{:S(2)}, u32[]{:S(2)}) async-start(bf16[8,32,1792]{2,1,0:T(8,128)(2,1)} %bitcast.17), calls=%async_computation.4 | async-start | bytes 1835008 | tf_op jit(solution)/shard_map/all_to_all | solution.py:105
  152.1 3.5 %copy-start.3 = (bf16[256,1024]{0,1:T(8,128)(2,1)S(1)}, bf16[256,1024]{0,1:T(8,128)(2,1)}, u32[]{:S(2)}) copy-start(bf16[256,1024]{0,1:T(8,128)(2,1)} %multiply_convert_fusion) | copy-start | bytes 1572868
  152.1 47.7 %reduce-scatter.2.cloned.1.call-start = ((), (), s32[]{:S(2)}) async-start(), calls=%async_computation.11 | async-start | bytes 1638400 | tf_op jit(solution)/shard_map/reduce_scatter | solution.py:107
  160.7 74.5 %copy-start.5 = (bf16[20,1792]{1,0:T(8,128)(2,1)S(1)}, bf16[20,1792]{1,0:T(8,128)(2,1)}, u32[]{:S(2)}) copy-start(bf16[20,1792]{1,0:T(8,128)(2,1)} %param.8) | copy-start | bytes 215044
  160.7 74.5 %copy-start.7 = (bf16[20,8,4,4,2]{0,4,3,2,1:T(2,128)(2,1)S(1)}, bf16[20,8,4,4,2]{0,4,3,2,1:T(2,128)(2,1)}, u32[]{:S(2)}) copy-start(bf16[20,8,4,4,2]{0,4,3,2,1:T(2,128)(2,1)} %copy-done.6) | copy-start | bytes 30724
  180.5 19.3 %all-to-all-start.6 = ((bf16[4,8,1792]{2,1,0:T(8,128)(2,1)}), bf16[4,8,1792]{2,1,0:T(8,128)(2,1)S(1)}, u32[]{:S(2)}, u32[]{:S(2)}) async-start(bf16[4,8,1792]{2,1,0:T(8,128)(2,1)} %broadcast_in_dim.20), calls=%async_computation.6 | async-start | bytes 229376 | tf_op jit(solution)/shard_map/all_to_all | solution.py:25
  185.5 50.7 %all-gather.5.cloned.1.call-start = ((), (), s32[]{:S(2)}) async-start(), calls=%async_computation.12 | async-start | bytes 1638400 | tf_op jit(solution)/shard_map/all_gather | solution.py:114
  209.7 25.6 %all-to-all-start.8 = ((bf16[8,32,1792]{2,1,0:T(8,128)(2,1)}), bf16[8,32,1792]{2,1,0:T(8,128)(2,1)S(1)}, u32[]{:S(2)}, u32[]{:S(2)}) async-start(bf16[8,32,1792]{2,1,0:T(8,128)(2,1)} %broadcast_in_dim.23), calls=%async_computation.9 | async-start | bytes 1835008 | tf_op jit(solution)/shard_map/all_to_all | solution.py:25
Sparse Core Ops, SparseCore 0:
  27.7 96.3 all-gather.2
  168.9 23.4 reduce-scatter.1
  199.9 31.1 all-gather.4

commit v6 on v5

--- a/solution.py
+++ b/solution.py
@@ -71,8 +71,6 @@
     from_ahead, from_behind = ring_permutes("fsdp", PAIR)
     ahead, behind = from_ahead(line), from_behind(line)
     moments = spread(moments, "dp", strides)
-    ahead, behind, moments = lax.optimization_barrier((ahead, behind, moments))
-    old_first, old_second = (moments[:, i].reshape(far * share, width) for i in range(2))
     across = from_ahead(ahead[: outer // 2]), from_behind(behind[outer // 2 :])
 
     def grad_of_preact(side, wanted):
@@ -85,7 +83,8 @@
     ).astype(bf16)
     projected = spread(projected_part, "tensor").reshape(rank, tokens.shape[0])
     grad_pre_a = grad_of_preact(weight_a, cotangent[:, :half])
-    across, grad_pre_a = lax.optimization_barrier((across, grad_pre_a))
+    across, moments = lax.optimization_barrier((across, moments))
+    old_first, old_second = (moments[:, i].reshape(far * share, width) for i in range(2))
 
     blocks = by_class([line, ahead, jnp.concatenate(across), behind], lax.axis_index("fsdp") // PAIR)
     weight_b = jnp.stack(blocks, axis=1).reshape(depth, width - half)
@@ -97,21 +96,24 @@
         ],
         axis=1,
     )
+    grad_part, grad_pre_a, grad_pre_b = lax.optimization_barrier(
+        (grad_part, grad_pre_a, grad_pre_b)
+    )
     partial_rows = sum(
         lax.dot_general(g, w, (((1,), (1,)), ((), ())), preferred_element_type=f32)
         for g, w in ((grad_pre_a, weight_a), (grad_pre_b, weight_b))
     ).astype(bf16)
 
     landed = lax.all_to_all(grad_part.reshape(inner, outer * share, width), "fsdp", 0, 0, tiled=True)
-    landed, partial_rows = lax.optimization_barrier((landed, partial_rows))
+    landed, _ = lax.optimization_barrier((landed, partial_rows))
     token_rows = lax.psum_scatter(partial_rows, "tensor", scatter_dimension=0, tiled=True)
     inner_sum = jnp.sum(landed.astype(f32), axis=0)
     blocks = inner_sum.astype(bf16).reshape(RING, far * share, width)
     landed = lax.all_to_all(blocks, "dp", 0, 0, tiled=True, axis_index_groups=fours)
+    landed, token_rows = lax.optimization_barrier((landed, token_rows))
+    token_grad = lax.all_gather(token_rows, "tensor", axis=0, tiled=True)
     blocks = jnp.sum(landed.astype(f32), axis=0).astype(bf16)
     landed = spread(blocks, "dp", strides)
-    landed, token_rows = lax.optimization_barrier((landed, token_rows))
-    token_grad = lax.all_gather(token_rows, "tensor", axis=0, tiled=True)
     reduced = jnp.sum(landed.astype(f32), axis=0)
 
     token_count = tokens.shape[0] * outer * inner

time: 247 us -> 260 us (1.053)
  blocking collectives: 86.7 us -> 110 us
  starting transfers between devices: 37.7 us -> 34.5 us
  matrix products: 18.2 us -> 15.3 us
    all_to_all x0 -> x1, blocking collectives: none -> 21.9 us  [local(): lax.all_to_all(grad_part.reshape(inner, outer * share, width), 'fsdp', 0,...]
    ppermute x2, waiting for transfers between devices: 0.01 us -> 14.8 us  [ring_permutes(): lax.ppermute(x, axis, ahead)]
    all_to_all x1 -> x0, waiting for transfers between devices: 8.01 us -> none  [local(): lax.all_to_all(grad_part.reshape(inner, outer * share, width), 'fsdp', 0,...]
    all_to_all x5, waiting for transfers between devices: 47.5 us -> 42.3 us  [spread(): lax.all_to_all(copies, axis, 0, 0, tiled=True, axis_index_groups=groups)]
    ppermute x2, waiting for transfers between devices: 4.39 us -> 0.01 us  [ring_permutes(): lax.ppermute(x, axis, behind)]
    all_to_all x1 -> x0, starting transfers between devices: 3.55 us -> none  [local(): lax.all_to_all(grad_part.reshape(inner, outer * share, width), 'fsdp', 0,...]
    unnamed x20 -> x26, local copies, waits for them, and re-layouts: 9.32 us -> 10.3 us
  transfers between devices with their start and end apart: 13 -> 12, of which waited for: 6 -> 6; matrix products, arithmetic and copies ran while one was open for 15% -> 9% of each run, Pallas kernels for 0% -> 0%
where the time goes in v6:
time: 260 us; the launch traced here: 259 us
  blocking collectives  110 us (42%)
  waiting for transfers between devices  57.6 us (22%)
  starting transfers between devices  34.5 us (13%)
  local copies, waits for them, and re-layouts  22.4 us (9%)
  matrix products  15.3 us (6%)
  between operations  14.1 us (5%)
  other arithmetic  5.15 us (2%)
    all_gather x1, blocking collectives, local(): line = lax.all_gather(second, 'dp', axis=0)  49.4 us
    all_to_all x5, waiting for transfers between devices, spread(): lax.all_to_all(copies, axis, 0, 0, tiled=True, axis_index_groups=groups)  42.3 us
    all_to_all x2, blocking collectives, spread(): lax.all_to_all(copies, axis, 0, 0, tiled=True, axis_index_groups=groups)  26.5 us
    all_to_all x5, starting transfers between devices, spread(): lax.all_to_all(copies, axis, 0, 0, tiled=True, axis_index_groups=groups)  22.3 us
    all_to_all x1, blocking collectives, local(): lax.all_to_all(grad_part.reshape(inner, outer * share, width), 'fsdp', 0,...  21.9 us
    ppermute x2, waiting for transfers between devices, ring_permutes(): lax.ppermute(x, axis, ahead)  14.8 us
    all_to_all x1, blocking collectives, local(): lax.all_to_all(blocks, 'dp', 0, 0, tiled=True, axis_index_groups=fours)  11.9 us
    unnamed x26, local copies, waits for them, and re-layouts  10.3 us
  transfers between devices with their start and end apart: 12, of which 6 were waited for; matrix products, arithmetic and copies ran while one was open for 9% of the time, Pallas kernels for 0%

profile of v6, /device:TPU:32, one launch (start us, length us, event | category | flops | bytes accessed | tf_op | source)
XLA Modules:
  0.0 258.9 jit_solution(16819120914154785122)
XLA Ops:
  9.2 17.5 %all_to_all.45 = bf16[8,20,1088]{2,1,0:T(8,128)(2,1)S(1)} all-to-all(bf16[8,20,1088]{2,1,0:T(8,128)(2,1)S(1)} %broadcast_in_dim.16), channel_id=1, replica_groups=mesh['dp'=16,'fsdp'=8,'tensor'=4] {'fsdp'}, dimensions={0} | all-to-all | bytes 696320 | tf_op jit(solution)/shard_map/all_to_all | solution.py:25
  29.0 3.3 %all-to-all-start.2 = ((bf16[2,20,768]{2,1,0:T(8,128)(2,1)}), bf16[2,20,768]{2,1,0:T(8,128)(2,1)S(1)}, u32[]{:S(2)}, u32[]{:S(2)}) async-start(bf16[2,20,768]{2,1,0:T(8,128)(2,1)} %broadcast_in_dim.18), calls=%async_computation.2 | async-start | bytes 147456 | tf_op jit(solution)/shard_map/all_to_all | solution.py:25
  33.1 4.9 %all-to-all-done.2 = bf16[2,20,768]{2,1,0:T(8,128)(2,1)S(1)} async-done(((bf16[2,20,768]{2,1,0:T(8,128)(2,1)}), bf16[2,20,768]{2,1,0:T(8,128)(2,1)S(1)}, u32[]{:S(2)}, u32[]{:S(2)}) %all-to-all-start.2) | async-done | bytes 61472 | tf_op jit(solution)/shard_map/all_to_all | solution.py:25
  38.0 49.4 %all_gather.10 = bf16[16,40,768]{2,1,0:T(8,128)(2,1)S(1)} all-gather(bf16[1,40,768]{2,1,0:T(8,128)(2,1)S(1)} %all_gather_reshape.3), channel_id=1, replica_groups=mesh['dp'=16,'fsdp'=8,'tensor'=4] {'dp'}, dimensions={0}, use_global_device_ids=true | all-gather | bytes 1044480 | tf_op jit(solution)/shard_map/all_gather | solution.py:68
  87.4 4.1 %collective-permute-start = (bf16[16,40,768]{2,1,0:T(8,128)(2,1)S(1)}, bf16[16,40,768]{2,1,0:T(8,128)(2,1)S(1)}, u32[]{:S(2)}, u32[]{:S(2)}) collective-permute-start(bf16[16,40,768]{2,1,0:T(8,128)(2,1)S(1)} %all_gather.10), channel_id=1, source_target_pairs={{8,0},{12,4},{16,8},{20,12},{24,16},{28,20},{0,24},{4,28},{9,1},{1... | collective-permute-start | bytes 2949128 | tf_op jit(solution)/shard_map/ppermute | solution.py:32
  91.5 1.9 collective-permute-start.2
  93.4 14.8 %collective-permute-done = bf16[16,40,768]{2,1,0:T(8,128)(2,1)S(1)} collective-permute-done((bf16[16,40,768]{2,1,0:T(8,128)(2,1)S(1)}, bf16[16,40,768]{2,1,0:T(8,128)(2,1)S(1)}, u32[]{:S(2)}, u32[]{:S(2)}) %collective-permute-start) | collective-permute-done | bytes 983072 | tf_op jit(solution)/shard_map/ppermute | solution.py:32
  109.0 4.2 %collective-permute-start.1 = (bf16[8,40,768]{2,1,0:T(8,128)(2,1)}, bf16[8,40,768]{2,1,0:T(8,128)(2,1)}, u32[]{:S(2)}, u32[]{:S(2)}) collective-permute-start(bf16[8,40,768]{2,1,0:T(8,128)(2,1)} %slice.42), channel_id=1, source_target_pairs={{8,0},{12,4},{16,8},{20,12},{24,16},{28,20},{0,24},{4,28},{9,1},{1... | collective-permute-start | bytes 1474568 | tf_op jit(solution)/shard_map/ppermute | solution.py:32
  115.0 1.9 collective-permute-start.3
  117.6 7.0 %all-to-all-start.3 = ((f32[4,2,2,1792]{3,2,1,0:T(2,128)}), f32[4,2,2,1792]{3,2,1,0:T(2,128)S(1)}, u32[]{:S(2)}, u32[]{:S(2)}) async-start(f32[4,2,2,1792]{3,2,1,0:T(2,128)} %broadcast_in_dim.19), calls=%async_computation.3 | async-start | bytes 229376 | tf_op jit(solution)/shard_map/all_to_all | solution.py:25
  124.6 1.8 slice.34
  126.4 1.9 slice.32
  128.3 1.9 copy.29
  130.2 2.1 copy.28
  132.3 7.3 %all-to-all-done.3 = f32[4,2,2,1792]{3,2,1,0:T(2,128)S(1)} async-done(((f32[4,2,2,1792]{3,2,1,0:T(2,128)}), f32[4,2,2,1792]{3,2,1,0:T(2,128)S(1)}, u32[]{:S(2)}, u32[]{:S(2)}) %all-to-all-start.3) | async-done | bytes 114720 | tf_op jit(solution)/shard_map/all_to_all | solution.py:25
  139.6 1.3 maximum_bitcast_fusion
  140.9 1.6 pad_maximum_fusion
  143.3 1.9 copy-done.1
  145.3 1.4 multiply_convert_fusion.1
  146.6 1.6 convolution_convert_fusion.2
  148.9 3.3 %all-to-all-start.1 = ((bf16[4,64,256]{2,1,0:T(8,128)(2,1)}), bf16[4,64,256]{2,1,0:T(8,128)(2,1)S(1)}, u32[]{:S(2)}, u32[]{:S(2)}) async-start(bf16[4,64,256]{2,1,0:T(8,128)(2,1)} %broadcast_in_dim.17), calls=%async_computation.1 | async-start | bytes 262144 | tf_op jit(solution)/shard_map/all_to_all | solution.py:25
  152.3 4.3 %multiply_convert_fusion = bf16[256,1024]{0,1:T(8,128)(2,1)S(1)} fusion(bf16[256,1024]{0,1:T(8,128)(2,1)S(1)} %copy-done.4, bf16[256,2560]{1,0:T(8,128)(2,1)S(1)} %copy-done, bf16[2560,1088]{1,0:T(8,128)(2,1)} %all-gather.3.cloned.1.call-done), kind=kOutput, calls=%fused_computation.17 | convolution fusion | flops 1344798720 | bytes 7602176 | tf_op jit(solution)/shard_map/dot_general | solution.py:77
  157.6 4.2 %fusion = f32[256,2560]{1,0:T(8,128)S(1)} fusion(bf16[256,1024]{0,1:T(8,128)(2,1)S(1)} %multiply_convert_fusion, bf16[2560,1088]{1,0:T(8,128)(2,1)} %all-gather.3.cloned.1.call-done), kind=kOutput, calls=%fused_computation | convolution fusion | flops 1342177280 | bytes 8388608 | tf_op jit(solution)/shard_map/dot_general | solution.py:103
  161.8 2.3 fusion.4
  164.1 21.9 %all_to_all.46 = bf16[8,32,1792]{2,1,0:T(8,128)(2,1)S(1)} all-to-all(bf16[8,32,1792]{2,1,0:T(8,128)(2,1)S(1)} %bitcast.64), channel_id=1, replica_groups=mesh['dp'=16,'fsdp'=8,'tensor'=4] {'fsdp'}, dimensions={0} | all-to-all | bytes 1835008 | tf_op jit(solution)/shard_map/all_to_all | solution.py:107
  186.2 11.9 %all_to_all.47 = bf16[4,8,1792]{2,1,0:T(8,128)(2,1)S(1)} all-to-all(bf16[4,8,1792]{2,1,0:T(8,128)(2,1)S(1)} %bitcast.69), channel_id=1, replica_groups={{0,32,64,96},{128,160,192,224},{256,288,320,352},{384,416,448,480},{1,3..., dimensions={0} | all-to-all | bytes 229376 | tf_op jit(solution)/shard_map/all_to_all | solution.py:112
  198.8 3.3 %all-to-all-start.6 = ((bf16[4,8,1792]{2,1,0:T(8,128)(2,1)}), bf16[4,8,1792]{2,1,0:T(8,128)(2,1)S(1)}, u32[]{:S(2)}, u32[]{:S(2)}) async-start(bf16[4,8,1792]{2,1,0:T(8,128)(2,1)} %broadcast_in_dim.20), calls=%async_computation.7 | async-start | bytes 229376 | tf_op jit(solution)/shard_map/all_to_all | solution.py:25
  202.9 13.2 %all-to-all-done.6 = bf16[4,8,1792]{2,1,0:T(8,128)(2,1)S(1)} async-done(((bf16[4,8,1792]{2,1,0:T(8,128)(2,1)}), bf16[4,8,1792]{2,1,0:T(8,128)(2,1)S(1)}, u32[]{:S(2)}, u32[]{:S(2)}) %all-to-all-start.6) | async-done | bytes 114720 | tf_op jit(solution)/shard_map/all_to_all | solution.py:25
  216.2 9.0 %all_to_all.48 = bf16[4,8,1792]{2,1,0:T(8,128)(2,1)S(1)} all-to-all(bf16[4,8,1792]{2,1,0:T(8,128)(2,1)S(1)} %broadcast_in_dim.21), channel_id=1, replica_groups={{0,32,64,96},{128,160,192,224},{256,288,320,352},{384,416,448,480},{1,3..., dimensions={0} | all-to-all | bytes 229376 | tf_op jit(solution)/shard_map/all_to_all | solution.py:25
  226.2 5.4 %all-to-all-start.8 = ((bf16[8,32,1792]{2,1,0:T(8,128)(2,1)}), bf16[8,32,1792]{2,1,0:T(8,128)(2,1)S(1)}, u32[]{:S(2)}, u32[]{:S(2)}) async-start(bf16[8,32,1792]{2,1,0:T(8,128)(2,1)} %broadcast_in_dim.23), calls=%async_computation.9 | async-start | bytes 1835008 | tf_op jit(solution)/shard_map/all_to_all | solution.py:25
  232.3 16.6 %all-to-all-done.8 = bf16[8,32,1792]{2,1,0:T(8,128)(2,1)S(1)} async-done(((bf16[8,32,1792]{2,1,0:T(8,128)(2,1)}), bf16[8,32,1792]{2,1,0:T(8,128)(2,1)S(1)}, u32[]{:S(2)}, u32[]{:S(2)}) %all-to-all-start.8) | async-done | bytes 917536 | tf_op jit(solution)/shard_map/all_to_all | solution.py:25
  249.9 2.5 copy.31
  (69 shorter events, 15.1 us)
Async XLA Ops:
  7.2 138.1 %copy-start = (bf16[256,2560]{1,0:T(8,128)(2,1)S(1)}, bf16[256,2560]{1,0:T(8,128)(2,1)}, u32[]{:S(2)}) copy-start(bf16[256,2560]{1,0:T(8,128)(2,1)} %param.6) | copy-start | bytes 3932164
  7.2 139.5 %all-gather.3.cloned.1.call-start = ((), (), s32[]{:S(2)}) async-start(), calls=%async_computation.10 | async-start | bytes 6266880 | tf_op jit(solution)/shard_map/all_gather | solution.py:65
  8.2 0.9 copy-start.9
  29.0 9.0 %all-to-all-start.2 = ((bf16[2,20,768]{2,1,0:T(8,128)(2,1)}), bf16[2,20,768]{2,1,0:T(8,128)(2,1)S(1)}, u32[]{:S(2)}, u32[]{:S(2)}) async-start(bf16[2,20,768]{2,1,0:T(8,128)(2,1)} %broadcast_in_dim.18), calls=%async_computation.2 | async-start | bytes 147456 | tf_op jit(solution)/shard_map/all_to_all | solution.py:25
  87.4 20.8 %collective-permute-start = (bf16[16,40,768]{2,1,0:T(8,128)(2,1)S(1)}, bf16[16,40,768]{2,1,0:T(8,128)(2,1)S(1)}, u32[]{:S(2)}, u32[]{:S(2)}) collective-permute-start(bf16[16,40,768]{2,1,0:T(8,128)(2,1)S(1)} %all_gather.10), channel_id=1, source_target_pairs={{8,0},{12,4},{16,8},{20,12},{24,16},{28,20},{0,24},{4,28},{9,1},{1... | collective-permute-start | bytes 2949128 | tf_op jit(solution)/shard_map/ppermute | solution.py:32
  91.5 21.7 %collective-permute-start.2 = (bf16[16,40,768]{2,1,0:T(8,128)(2,1)S(1)}, bf16[16,40,768]{2,1,0:T(8,128)(2,1)S(1)}, u32[]{:S(2)}, u32[]{:S(2)}) collective-permute-start(bf16[16,40,768]{2,1,0:T(8,128)(2,1)S(1)} %all_gather.10), channel_id=1, source_target_pairs={{0,8},{4,12},{8,16},{12,20},{16,24},{20,28},{24,0},{28,4},{1,9},{5... | collective-permute-start | bytes 2949128 | tf_op jit(solution)/shard_map/ppermute | solution.py:32
  109.0 30.5 %collective-permute-start.1 = (bf16[8,40,768]{2,1,0:T(8,128)(2,1)}, bf16[8,40,768]{2,1,0:T(8,128)(2,1)}, u32[]{:S(2)}, u32[]{:S(2)}) collective-permute-start(bf16[8,40,768]{2,1,0:T(8,128)(2,1)} %slice.42), channel_id=1, source_target_pairs={{8,0},{12,4},{16,8},{20,12},{24,16},{28,20},{0,24},{4,28},{9,1},{1... | collective-permute-start | bytes 1474568 | tf_op jit(solution)/shard_map/ppermute | solution.py:32
  113.2 0.9 copy-start.3
  115.0 24.5 %collective-permute-start.3 = (bf16[8,40,768]{2,1,0:T(8,128)(2,1)}, bf16[8,40,768]{2,1,0:T(8,128)(2,1)}, u32[]{:S(2)}, u32[]{:S(2)}) collective-permute-start(bf16[8,40,768]{2,1,0:T(8,128)(2,1)} %slice.43), channel_id=1, source_target_pairs={{0,8},{4,12},{8,16},{12,20},{16,24},{20,28},{24,0},{28,4},{1,9},{5... | collective-permute-start | bytes 1474568 | tf_op jit(solution)/shard_map/ppermute | solution.py:32
  117.6 21.9 %all-to-all-start.3 = ((f32[4,2,2,1792]{3,2,1,0:T(2,128)}), f32[4,2,2,1792]{3,2,1,0:T(2,128)S(1)}, u32[]{:S(2)}, u32[]{:S(2)}) async-start(f32[4,2,2,1792]{3,2,1,0:T(2,128)} %broadcast_in_dim.19), calls=%async_computation.3 | async-start | bytes 229376 | tf_op jit(solution)/shard_map/all_to_all | solution.py:25
  139.6 2.9 %copy-start.5 = (f32[4,2,2,1792]{3,2,1,0:T(2,128)}, f32[4,2,2,1792]{3,2,1,0:T(2,128)S(1)}, u32[]{:S(2)}) copy-start(f32[4,2,2,1792]{3,2,1,0:T(2,128)S(1)} %all-to-all-done.3) | copy-start | bytes 344068
  142.7 2.5 copy-start.7
  143.3 1.9 copy-start.1
  145.3 7.1 %copy-start.4 = (bf16[256,1024]{0,1:T(8,128)(2,1)S(1)}, bf16[256,1024]{0,1:T(8,128)(2,1)}, u32[]{:S(2)}) copy-start(bf16[256,1024]{0,1:T(8,128)(2,1)} %copy.28) | copy-start | bytes 1572868
  148.9 7.9 %all-to-all-start.1 = ((bf16[4,64,256]{2,1,0:T(8,128)(2,1)}), bf16[4,64,256]{2,1,0:T(8,128)(2,1)S(1)}, u32[]{:S(2)}, u32[]{:S(2)}) async-start(bf16[4,64,256]{2,1,0:T(8,128)(2,1)} %broadcast_in_dim.17), calls=%async_computation.1 | async-start | bytes 262144 | tf_op jit(solution)/shard_map/all_to_all | solution.py:25
  152.3 45.9 %reduce-scatter.2.cloned.1.call-start = ((), (), s32[]{:S(2)}) async-start(), calls=%async_computation.11 | async-start | bytes 1638400 | tf_op jit(solution)/shard_map/reduce_scatter | solution.py:109
  157.6 4.2 %copy-start.2 = (bf16[16,4,40,768]{3,2,1,0:T(8,128)(2,1)S(1)}, bf16[16,4,40,768]{3,2,1,0:T(8,128)(2,1)}, u32[]{:S(2)}) copy-start(bf16[16,4,40,768]{3,2,1,0:T(8,128)(2,1)} %copy-done.1) | copy-start | bytes 11796484
  164.1 38.1 %copy-start.6 = (f32[4,2,2,1792]{3,2,1,0:T(2,128)S(1)}, f32[4,2,2,1792]{3,2,1,0:T(2,128)}, u32[]{:S(2)}) copy-start(f32[4,2,2,1792]{3,2,1,0:T(2,128)} %copy-done.5) | copy-start | bytes 344068
  186.1 62.9 %copy-start.8 = (bf16[20,1792]{1,0:T(8,128)(2,1)S(1)}, bf16[20,1792]{1,0:T(8,128)(2,1)}, u32[]{:S(2)}) copy-start(bf16[20,1792]{1,0:T(8,128)(2,1)} %param.8) | copy-start | bytes 215044
  186.1 62.9 %copy-start.10 = (bf16[20,8,4,4,2]{0,4,3,2,1:T(2,128)(2,1)S(1)}, bf16[20,8,4,4,2]{0,4,3,2,1:T(2,128)(2,1)}, u32[]{:S(2)}) copy-start(bf16[20,8,4,4,2]{0,4,3,2,1:T(2,128)(2,1)} %copy-done.9) | copy-start | bytes 30724
  198.8 17.3 %all-to-all-start.6 = ((bf16[4,8,1792]{2,1,0:T(8,128)(2,1)}), bf16[4,8,1792]{2,1,0:T(8,128)(2,1)S(1)}, u32[]{:S(2)}, u32[]{:S(2)}) async-start(bf16[4,8,1792]{2,1,0:T(8,128)(2,1)} %broadcast_in_dim.20), calls=%async_computation.7 | async-start | bytes 229376 | tf_op jit(solution)/shard_map/all_to_all | solution.py:25
  202.1 47.7 %all-gather.5.cloned.1.call-start = ((), (), s32[]{:S(2)}) async-start(), calls=%async_computation.12 | async-start | bytes 1638400 | tf_op jit(solution)/shard_map/all_gather | solution.py:114
  226.2 22.8 %all-to-all-start.8 = ((bf16[8,32,1792]{2,1,0:T(8,128)(2,1)}), bf16[8,32,1792]{2,1,0:T(8,128)(2,1)S(1)}, u32[]{:S(2)}, u32[]{:S(2)}) async-start(bf16[8,32,1792]{2,1,0:T(8,128)(2,1)} %broadcast_in_dim.23), calls=%async_computation.9 | async-start | bytes 1835008 | tf_op jit(solution)/shard_map/all_to_all | solution.py:25
Sparse Core Ops, SparseCore 0:
  27.7 92.8 all-gather.2
  164.3 26.6 reduce-scatter.1
  205.1 33.9 all-gather.4

commit v7 on v5

--- a/solution.py
+++ b/solution.py
@@ -33,10 +33,11 @@
 
 
 def by_class(blocks, place):
+    count = len(blocks)
     stacked = jnp.stack(blocks)
     return [
-        lax.dynamic_index_in_dim(stacked, lax.rem(wanted - place + RING, RING), 0, keepdims=False)
-        for wanted in range(RING)
+        lax.dynamic_index_in_dim(stacked, lax.rem(wanted - place + count, count), 0, keepdims=False)
+        for wanted in range(count)
     ]
 
 
@@ -59,7 +60,7 @@
     strides = [[i + RING * j for j in range(far)] for i in range(RING)]
     fours = [[RING * j + i for i in range(RING)] for j in range(far)]
     pair_rows = PAIR * rows
-    half = width * 4 // 7
+    half = width * 9 // 14
     first = jnp.concatenate([weight[:, :half], basis_part], axis=1)
     plane = spread(first, "fsdp").reshape(inner * rows, half + part)
     full_a = lax.all_gather(plane, "dp", axis=0, tiled=True)
@@ -70,9 +71,8 @@
     line, moments = lax.optimization_barrier((line, moments))
     from_ahead, from_behind = ring_permutes("fsdp", PAIR)
     ahead, behind = from_ahead(line), from_behind(line)
-    moments = spread(moments, "dp", strides)
-    ahead, behind, moments = lax.optimization_barrier((ahead, behind, moments))
-    old_first, old_second = (moments[:, i].reshape(far * share, width) for i in range(2))
+    carried = [moments] + [ring_permutes("dp", RING * j)[0](moments) for j in range(1, far)]
+    ahead, behind = lax.optimization_barrier((ahead, behind))
     across = from_ahead(ahead[: outer // 2]), from_behind(behind[outer // 2 :])
 
     def grad_of_preact(side, wanted):
@@ -85,7 +85,8 @@
     ).astype(bf16)
     projected = spread(projected_part, "tensor").reshape(rank, tokens.shape[0])
     grad_pre_a = grad_of_preact(weight_a, cotangent[:, :half])
-    across, grad_pre_a = lax.optimization_barrier((across, grad_pre_a))
+    across, carried = lax.optimization_barrier((across, carried))
+    moments = jnp.stack(by_class(carried, lax.axis_index("dp") // RING))
 
     blocks = by_class([line, ahead, jnp.concatenate(across), behind], lax.axis_index("fsdp") // PAIR)
     weight_b = jnp.stack(blocks, axis=1).reshape(depth, width - half)
@@ -110,13 +111,14 @@
     landed = lax.all_to_all(blocks, "dp", 0, 0, tiled=True, axis_index_groups=fours)
     blocks = jnp.sum(landed.astype(f32), axis=0).astype(bf16)
     landed = spread(blocks, "dp", strides)
-    landed, token_rows = lax.optimization_barrier((landed, token_rows))
+    old_first, old_second = (moments[:, i].reshape(far * share, width) for i in range(2))
+    old_first, token_rows = lax.optimization_barrier((BETA_ONE * old_first, token_rows))
     token_grad = lax.all_gather(token_rows, "tensor", axis=0, tiled=True)
     reduced = jnp.sum(landed.astype(f32), axis=0)
 
     token_count = tokens.shape[0] * outer * inner
     grad_low = reduced / float(token_count)
-    new_first = BETA_ONE * old_first + (1.0 - BETA_ONE) * grad_low
+    new_first = old_first + (1.0 - BETA_ONE) * grad_low
     new_second = BETA_TWO * old_second + (1.0 - BETA_TWO) * grad_low * grad_low
     first_hat = new_first / (1.0 - BETA_ONE**ADAM_STEP)
     second_hat = new_second / (1.0 - BETA_TWO**ADAM_STEP)

time: 247 us -> 253 us (1.024)
  starting transfers between devices: 37.7 us -> 55.6 us
  blocking collectives: 86.7 us -> 74 us
  local copies, waits for them, and re-layouts: 22.4 us -> 13.6 us
  waiting for transfers between devices: 60 us -> 68.6 us
    ppermute x2 -> x5, starting transfers between devices: 7.25 us -> 27.1 us  [ring_permutes(): lax.ppermute(x, axis, ahead)]
    all_to_all x5 -> x4, waiting for transfers between devices: 47.5 us -> 36.4 us  [spread(): lax.all_to_all(copies, axis, 0, 0, tiled=True, axis_index_groups=groups)]
    all_to_all x1 -> x0, blocking collectives: 11 us -> none  [local(): lax.all_to_all(blocks, 'dp', 0, 0, tiled=True, axis_index_groups=fours)]
    all_to_all x5 -> x4, starting transfers between devices: 22.2 us -> 15.5 us  [spread(): lax.all_to_all(copies, axis, 0, 0, tiled=True, axis_index_groups=groups)]
    all_to_all x0 -> x1, waiting for transfers between devices: none -> 4.96 us  [local(): lax.all_to_all(blocks, 'dp', 0, 0, tiled=True, axis_index_groups=fours)]
    ppermute x2 -> x5, waiting for transfers between devices: 0.01 us -> 4.91 us  [ring_permutes(): lax.ppermute(x, axis, ahead)]
    all_to_all x0 -> x1, starting transfers between devices: none -> 4.86 us  [local(): lax.all_to_all(blocks, 'dp', 0, 0, tiled=True, axis_index_groups=fours)]
    ppermute x2, waiting for transfers between devices: 4.39 us -> 9.1 us  [ring_permutes(): lax.ppermute(x, axis, behind)]
  transfers between devices with their start and end apart: 13 -> 16, of which waited for: 6 -> 9; matrix products, arithmetic and copies ran while one was open for 15% -> 10% of each run, Pallas kernels for 0% -> 0%
where the time goes in v7:
time: 253 us; the launch traced here: 251 us
  blocking collectives  74 us (29%)
  waiting for transfers between devices  68.6 us (27%)
  starting transfers between devices  55.6 us (22%)
  matrix products  18 us (7%)
  between operations  14.3 us (6%)
  local copies, waits for them, and re-layouts  13.6 us (5%)
  other arithmetic  6.86 us (3%)
    all_gather x1, blocking collectives, local(): line = lax.all_gather(second, 'dp', axis=0)  47.2 us
    all_to_all x4, waiting for transfers between devices, spread(): lax.all_to_all(copies, axis, 0, 0, tiled=True, axis_index_groups=groups)  36.4 us
    ppermute x5, starting transfers between devices, ring_permutes(): lax.ppermute(x, axis, ahead)  27.1 us
    all_to_all x2, blocking collectives, spread(): lax.all_to_all(copies, axis, 0, 0, tiled=True, axis_index_groups=groups)  26.9 us
    all_to_all x4, starting transfers between devices, spread(): lax.all_to_all(copies, axis, 0, 0, tiled=True, axis_index_groups=groups)  15.5 us
    all_to_all x1, waiting for transfers between devices, local(): lax.all_to_all(grad_part.reshape(inner, outer * share, width), 'fsdp', 0,...  9.27 us
    ppermute x2, waiting for transfers between devices, ring_permutes(): lax.ppermute(x, axis, behind)  9.1 us
    unnamed x30, local copies, waits for them, and re-layouts  7.17 us
  transfers between devices with their start and end apart: 16, of which 9 were waited for; matrix products, arithmetic and copies ran while one was open for 10% of the time, Pallas kernels for 0%

profile of v7, /device:TPU:32, one launch (start us, length us, event | category | flops | bytes accessed | tf_op | source)
XLA Modules:
  0.0 251.0 jit_solution(1106004094517858036)
XLA Ops:
  9.2 18.0 %all_to_all.40 = bf16[8,20,1216]{2,1,0:T(8,128)(2,1)S(1)} all-to-all(bf16[8,20,1216]{2,1,0:T(8,128)(2,1)S(1)} %broadcast_in_dim.14), channel_id=1, replica_groups=mesh['dp'=16,'fsdp'=8,'tensor'=4] {'fsdp'}, dimensions={0} | all-to-all | bytes 778240 | tf_op jit(solution)/shard_map/all_to_all | solution.py:25
  28.8 3.3 %all-to-all-start.1 = ((bf16[2,20,640]{2,1,0:T(8,128)(2,1)}), bf16[2,20,640]{2,1,0:T(8,128)(2,1)S(1)}, u32[]{:S(2)}, u32[]{:S(2)}) async-start(bf16[2,20,640]{2,1,0:T(8,128)(2,1)} %broadcast_in_dim.15), calls=%async_computation.1 | async-start | bytes 122880 | tf_op jit(solution)/shard_map/all_to_all | solution.py:25
  32.2 5.5 %all-to-all-done.1 = bf16[2,20,640]{2,1,0:T(8,128)(2,1)S(1)} async-done(((bf16[2,20,640]{2,1,0:T(8,128)(2,1)}), bf16[2,20,640]{2,1,0:T(8,128)(2,1)S(1)}, u32[]{:S(2)}, u32[]{:S(2)}) %all-to-all-start.1) | async-done | bytes 51232 | tf_op jit(solution)/shard_map/all_to_all | solution.py:25
  37.7 47.2 %all_gather.9 = bf16[16,40,640]{2,1,0:T(8,128)(2,1)S(1)} all-gather(bf16[1,40,640]{2,1,0:T(8,128)(2,1)S(1)} %all_gather_reshape.3), channel_id=1, replica_groups=mesh['dp'=16,'fsdp'=8,'tensor'=4] {'dp'}, dimensions={0}, use_global_device_ids=true | all-gather | bytes 870400 | tf_op jit(solution)/shard_map/all_gather | solution.py:69
  84.9 1.9 collective-permute-start.1
  86.8 5.1 %collective-permute-start = (bf16[16,40,640]{2,1,0:T(8,128)(2,1)S(1)}, bf16[16,40,640]{2,1,0:T(8,128)(2,1)S(1)}, u32[]{:S(2)}, u32[]{:S(2)}) collective-permute-start(bf16[16,40,640]{2,1,0:T(8,128)(2,1)S(1)} %all_gather.9), channel_id=1, source_target_pairs={{8,0},{12,4},{16,8},{20,12},{24,16},{28,20},{0,24},{4,28},{9,1},{1... | collective-permute-start | bytes 2457608 | tf_op jit(solution)/shard_map/ppermute | solution.py:32
  91.9 9.1 %collective-permute-done.1 = bf16[16,40,640]{2,1,0:T(8,128)(2,1)S(1)} collective-permute-done((bf16[16,40,640]{2,1,0:T(8,128)(2,1)S(1)}, bf16[16,40,640]{2,1,0:T(8,128)(2,1)S(1)}, u32[]{:S(2)}, u32[]{:S(2)}) %collective-permute-start.1) | collective-permute-done | bytes 819232 | tf_op jit(solution)/shard_map/ppermute | solution.py:32
  101.0 1.9 collective-permute-done
  104.0 1.9 collective-permute-start.3
  105.9 5.6 %collective-permute-start.2 = (bf16[8,40,640]{2,1,0:T(8,128)(2,1)S(1)}, bf16[8,40,640]{2,1,0:T(8,128)(2,1)}, u32[]{:S(2)}, u32[]{:S(2)}) collective-permute-start(bf16[8,40,640]{2,1,0:T(8,128)(2,1)S(1)} %slice.32), channel_id=1, source_target_pairs={{8,0},{12,4},{16,8},{20,12},{24,16},{28,20},{0,24},{4,28},{9,1},{1... | collective-permute-start | bytes 1228808 | tf_op jit(solution)/shard_map/ppermute | solution.py:32
  111.5 2.1 collective-permute-start.6
  113.7 9.3 %collective-permute-start.5 = (f32[2,2,1792]{2,1,0:T(2,128)S(1)}, f32[2,2,1792]{2,1,0:T(2,128)}, u32[]{:S(2)}, u32[]{:S(2)}) collective-permute-start(f32[2,2,1792]{2,1,0:T(2,128)S(1)} %pad_maximum_fusion.6), channel_id=1, source_target_pairs={{256,0},{288,32},{320,64},{352,96},{384,128},{416,160},{448,192},{... | collective-permute-start | bytes 86024 | tf_op jit(solution)/shard_map/ppermute | solution.py:32
  122.9 5.0 %collective-permute-start.4 = (f32[2,2,1792]{2,1,0:T(2,128)S(1)}, f32[2,2,1792]{2,1,0:T(2,128)}, u32[]{:S(2)}, u32[]{:S(2)}) collective-permute-start(f32[2,2,1792]{2,1,0:T(2,128)S(1)} %pad_maximum_fusion.6), channel_id=1, source_target_pairs={{128,0},{160,32},{192,64},{224,96},{256,128},{288,160},{320,192},{... | collective-permute-start | bytes 86024 | tf_op jit(solution)/shard_map/ppermute | solution.py:32
  130.0 3.0 %collective-permute-done.4 = f32[2,2,1792]{2,1,0:T(2,128)} collective-permute-done((f32[2,2,1792]{2,1,0:T(2,128)S(1)}, f32[2,2,1792]{2,1,0:T(2,128)}, u32[]{:S(2)}, u32[]{:S(2)}) %collective-permute-start.4) | collective-permute-done | bytes 28704 | tf_op jit(solution)/shard_map/ppermute | solution.py:32
  134.2 1.7 pad_maximum_fusion
  136.7 1.7 copy-done.1
  139.7 1.6 convolution_convert_fusion.2
  142.0 3.3 %all-to-all-start.2 = ((bf16[4,64,256]{2,1,0:T(8,128)(2,1)}), bf16[4,64,256]{2,1,0:T(8,128)(2,1)S(1)}, u32[]{:S(2)}, u32[]{:S(2)}) async-start(bf16[4,64,256]{2,1,0:T(8,128)(2,1)} %broadcast_in_dim.16), calls=%async_computation.2 | async-start | bytes 262144 | tf_op jit(solution)/shard_map/all_to_all | solution.py:25
  145.3 5.5 %multiply_convert_fusion = bf16[256,1152]{0,1:T(8,128)(2,1)} fusion(bf16[256,2560]{1,0:T(8,128)(2,1)S(1)} %copy-done, bf16[2560,1216]{1,0:T(8,128)(2,1)} %all-gather.3.cloned.1.call-done, bf16[256,1152]{0,1:T(8,128)(2,1)S(1)} %copy-done.5), kind=kOutput, calls=%fused_computation.16 | convolution fusion | flops 1512898560 | bytes 8388608 | tf_op jit(solution)/shard_map/dot_general | solution.py:79
  153.6 4.2 %all-to-all-start.3 = ((bf16[8,32,1792]{2,1,0:T(8,128)(2,1)}), bf16[8,32,1792]{2,1,0:T(8,128)(2,1)S(1)}, u32[]{:S(2)}, u32[]{:S(2)}) async-start(bf16[8,32,1792]{2,1,0:T(8,128)(2,1)} %bitcast.21), calls=%async_computation.3 | async-start | bytes 1835008 | tf_op jit(solution)/shard_map/all_to_all | solution.py:106
  157.8 4.7 %fusion = f32[256,2560]{1,0:T(8,128)S(1)} fusion(bf16[256,1152]{0,1:T(8,128)(2,1)S(1)} %copy-done.6, bf16[2560,1216]{1,0:T(8,128)(2,1)} %all-gather.3.cloned.1.call-done), kind=kOutput, calls=%fused_computation | convolution fusion | flops 1509949440 | bytes 9109504 | tf_op jit(solution)/shard_map/dot_general | solution.py:102
  162.6 2.3 fusion.4
  164.9 9.3 %all-to-all-done.3 = bf16[8,32,1792]{2,1,0:T(8,128)(2,1)S(1)} async-done(((bf16[8,32,1792]{2,1,0:T(8,128)(2,1)}), bf16[8,32,1792]{2,1,0:T(8,128)(2,1)S(1)}, u32[]{:S(2)}, u32[]{:S(2)}) %all-to-all-start.3) | async-done | bytes 917536 | tf_op jit(solution)/shard_map/all_to_all | solution.py:106
  175.9 4.9 %all-to-all-start.4 = ((bf16[4,8,1792]{2,1,0:T(8,128)(2,1)}), bf16[4,8,1792]{2,1,0:T(8,128)(2,1)S(1)}, u32[]{:S(2)}, u32[]{:S(2)}) async-start(bf16[4,8,1792]{2,1,0:T(8,128)(2,1)} %bitcast.22), calls=%async_computation.5 | async-start | bytes 229376 | tf_op jit(solution)/shard_map/all_to_all | solution.py:111
  180.8 5.0 %all-to-all-done.4 = bf16[4,8,1792]{2,1,0:T(8,128)(2,1)S(1)} async-done(((bf16[4,8,1792]{2,1,0:T(8,128)(2,1)}), bf16[4,8,1792]{2,1,0:T(8,128)(2,1)S(1)}, u32[]{:S(2)}, u32[]{:S(2)}) %all-to-all-start.4) | async-done | bytes 114720 | tf_op jit(solution)/shard_map/all_to_all | solution.py:111
  186.5 5.4 %all-to-all-start.5 = ((bf16[4,8,1792]{2,1,0:T(8,128)(2,1)}), bf16[4,8,1792]{2,1,0:T(8,128)(2,1)S(1)}, u32[]{:S(2)}, u32[]{:S(2)}) async-start(bf16[4,8,1792]{2,1,0:T(8,128)(2,1)} %broadcast_in_dim.17), calls=%async_computation.6 | async-start | bytes 229376 | tf_op jit(solution)/shard_map/all_to_all | solution.py:25
  192.0 3.9 %reduce-scatter.2.cloned.1.call-done = bf16[64,2560]{1,0:T(8,128)(2,1)} async-done(((bf16[256,2560]{1,0:T(8,128)(2,1)}), bf16[64,2560]{1,0:T(8,128)(2,1)}) %reduce-scatter.2.cloned.1.call-update) | async-done | bytes 327696 | tf_op jit(solution)/shard_map/reduce_scatter | solution.py:108
  196.0 9.7 %all-to-all-done.5 = bf16[4,8,1792]{2,1,0:T(8,128)(2,1)S(1)} async-done(((bf16[4,8,1792]{2,1,0:T(8,128)(2,1)}), bf16[4,8,1792]{2,1,0:T(8,128)(2,1)S(1)}, u32[]{:S(2)}, u32[]{:S(2)}) %all-to-all-start.5) | async-done | bytes 114720 | tf_op jit(solution)/shard_map/all_to_all | solution.py:25
  205.8 8.9 %all_to_all.41 = bf16[4,8,1792]{2,1,0:T(8,128)(2,1)S(1)} all-to-all(bf16[4,8,1792]{2,1,0:T(8,128)(2,1)S(1)} %broadcast_in_dim.18), channel_id=1, replica_groups={{0,32,64,96},{128,160,192,224},{256,288,320,352},{384,416,448,480},{1,3..., dimensions={0} | all-to-all | bytes 229376 | tf_op jit(solution)/shard_map/all_to_all | solution.py:25
  215.7 3.6 %all-to-all-start.7 = ((bf16[8,32,1792]{2,1,0:T(8,128)(2,1)}), bf16[8,32,1792]{2,1,0:T(8,128)(2,1)S(1)}, u32[]{:S(2)}, u32[]{:S(2)}) async-start(bf16[8,32,1792]{2,1,0:T(8,128)(2,1)} %broadcast_in_dim.20), calls=%async_computation.8 | async-start | bytes 1835008 | tf_op jit(solution)/shard_map/all_to_all | solution.py:25
  220.0 21.1 %all-to-all-done.7 = bf16[8,32,1792]{2,1,0:T(8,128)(2,1)S(1)} async-done(((bf16[8,32,1792]{2,1,0:T(8,128)(2,1)}), bf16[8,32,1792]{2,1,0:T(8,128)(2,1)S(1)}, u32[]{:S(2)}, u32[]{:S(2)}) %all-to-all-start.7) | async-done | bytes 917536 | tf_op jit(solution)/shard_map/all_to_all | solution.py:25
  242.0 2.5 copy.31
  (84 shorter events, 18.6 us)
Async XLA Ops:
  7.2 131.3 %copy-start = (bf16[256,2560]{1,0:T(8,128)(2,1)S(1)}, bf16[256,2560]{1,0:T(8,128)(2,1)}, u32[]{:S(2)}) copy-start(bf16[256,2560]{1,0:T(8,128)(2,1)} %param.6) | copy-start | bytes 3932164
  7.2 21.0 %slice-start.2 = ((bf16[20,1792]{1,0:T(8,128)(2,1)}), bf16[20,640]{1,0:T(8,128)(2,1)S(1)}, s32[]{:S(2)}) async-start(bf16[20,1792]{1,0:T(8,128)(2,1)} %param.8), calls=%async_computation.14 | async-start | bytes 61440 | tf_op jit(solution)/shard_map/slice | solution.py:67
  7.2 24.9 %copy-start.11 = (f32[2,1792]{1,0:T(2,128)S(1)}, f32[2,1792]{1,0:T(2,128)}, u32[]{:S(2)}) copy-start(f32[2,1792]{1,0:T(2,128)} %param.11) | copy-start | bytes 43012
  7.2 24.9 %copy-start.12 = (f32[2,1792]{1,0:T(2,128)S(1)}, f32[2,1792]{1,0:T(2,128)}, u32[]{:S(2)}) copy-start(f32[2,1792]{1,0:T(2,128)} %param.10) | copy-start | bytes 43012
  7.2 132.5 %all-gather.3.cloned.1.call-start = ((), (), s32[]{:S(2)}) async-start(), calls=%async_computation.9 | async-start | bytes 6963200 | tf_op jit(solution)/shard_map/all_gather | solution.py:66
  28.1 99.9 %slice-start = ((bf16[256,1792]{1,0:T(8,128)(2,1)}), bf16[256,640]{1,0:T(8,128)(2,1)S(1)}, s32[]{:S(2)}) async-start(bf16[256,1792]{1,0:T(8,128)(2,1)} %param.7), calls=%async_computation.12 | async-start | bytes 655360 | tf_op jit(solution)/shard_map/slice | solution.py:93
  28.8 8.9 %all-to-all-start.1 = ((bf16[2,20,640]{2,1,0:T(8,128)(2,1)}), bf16[2,20,640]{2,1,0:T(8,128)(2,1)S(1)}, u32[]{:S(2)}, u32[]{:S(2)}) async-start(bf16[2,20,640]{2,1,0:T(8,128)(2,1)} %broadcast_in_dim.15), calls=%async_computation.1 | async-start | bytes 122880 | tf_op jit(solution)/shard_map/all_to_all | solution.py:25
  32.1 97.9 %copy-start.9 = (f32[2,2,1792]{2,1,0:T(2,128)}, f32[2,2,1792]{2,1,0:T(2,128)S(1)}, u32[]{:S(2)}) copy-start(f32[2,2,1792]{2,1,0:T(2,128)S(1)} %pad_maximum_fusion.6) | copy-start | bytes 86020
  32.1 96.8 %slice-start.1 = ((bf16[256,1792]{1,0:T(8,128)(2,1)}), bf16[256,1152]{1,0:T(8,128)(2,1)S(1)}, s32[]{:S(2)}) async-start(bf16[256,1792]{1,0:T(8,128)(2,1)} %param.7), calls=%async_computation.13 | async-start | bytes 1179648 | tf_op jit(solution)/shard_map/slice | solution.py:87
  84.9 16.2 %collective-permute-start.1 = (bf16[16,40,640]{2,1,0:T(8,128)(2,1)S(1)}, bf16[16,40,640]{2,1,0:T(8,128)(2,1)S(1)}, u32[]{:S(2)}, u32[]{:S(2)}) collective-permute-start(bf16[16,40,640]{2,1,0:T(8,128)(2,1)S(1)} %all_gather.9), channel_id=1, source_target_pairs={{0,8},{4,12},{8,16},{12,20},{16,24},{20,28},{24,0},{28,4},{1,9},{5... | collective-permute-start | bytes 2457608 | tf_op jit(solution)/shard_map/ppermute | solution.py:32
  86.8 16.2 %collective-permute-start = (bf16[16,40,640]{2,1,0:T(8,128)(2,1)S(1)}, bf16[16,40,640]{2,1,0:T(8,128)(2,1)S(1)}, u32[]{:S(2)}, u32[]{:S(2)}) collective-permute-start(bf16[16,40,640]{2,1,0:T(8,128)(2,1)S(1)} %all_gather.9), channel_id=1, source_target_pairs={{8,0},{12,4},{16,8},{20,12},{24,16},{28,20},{0,24},{4,28},{9,1},{1... | collective-permute-start | bytes 2457608 | tf_op jit(solution)/shard_map/ppermute | solution.py:32
  101.0 2.0 copy-start.3
  103.0 1.0 copy-start.4
  104.0 29.0 %collective-permute-start.3 = (bf16[8,40,640]{2,1,0:T(8,128)(2,1)}, bf16[8,40,640]{2,1,0:T(8,128)(2,1)}, u32[]{:S(2)}, u32[]{:S(2)}) collective-permute-start(bf16[8,40,640]{2,1,0:T(8,128)(2,1)} %slice.33), channel_id=1, source_target_pairs={{0,8},{4,12},{8,16},{12,20},{16,24},{20,28},{24,0},{28,4},{1,9},{5... | collective-permute-start | bytes 1228808 | tf_op jit(solution)/shard_map/ppermute | solution.py:32
  105.9 27.1 %collective-permute-start.2 = (bf16[8,40,640]{2,1,0:T(8,128)(2,1)S(1)}, bf16[8,40,640]{2,1,0:T(8,128)(2,1)}, u32[]{:S(2)}, u32[]{:S(2)}) collective-permute-start(bf16[8,40,640]{2,1,0:T(8,128)(2,1)S(1)} %slice.32), channel_id=1, source_target_pairs={{8,0},{12,4},{16,8},{20,12},{24,16},{28,20},{0,24},{4,28},{9,1},{1... | collective-permute-start | bytes 1228808 | tf_op jit(solution)/shard_map/ppermute | solution.py:32
  111.5 18.5 %collective-permute-start.6 = (f32[2,2,1792]{2,1,0:T(2,128)S(1)}, f32[2,2,1792]{2,1,0:T(2,128)}, u32[]{:S(2)}, u32[]{:S(2)}) collective-permute-start(f32[2,2,1792]{2,1,0:T(2,128)S(1)} %pad_maximum_fusion.6), channel_id=1, source_target_pairs={{384,0},{416,32},{448,64},{480,96},{0,128},{32,160},{64,192},{96,2... | collective-permute-start | bytes 86024 | tf_op jit(solution)/shard_map/ppermute | solution.py:32
  113.7 16.4 %collective-permute-start.5 = (f32[2,2,1792]{2,1,0:T(2,128)S(1)}, f32[2,2,1792]{2,1,0:T(2,128)}, u32[]{:S(2)}, u32[]{:S(2)}) collective-permute-start(f32[2,2,1792]{2,1,0:T(2,128)S(1)} %pad_maximum_fusion.6), channel_id=1, source_target_pairs={{256,0},{288,32},{320,64},{352,96},{384,128},{416,160},{448,192},{... | collective-permute-start | bytes 86024 | tf_op jit(solution)/shard_map/ppermute | solution.py:32
  122.9 10.1 %collective-permute-start.4 = (f32[2,2,1792]{2,1,0:T(2,128)S(1)}, f32[2,2,1792]{2,1,0:T(2,128)}, u32[]{:S(2)}, u32[]{:S(2)}) collective-permute-start(f32[2,2,1792]{2,1,0:T(2,128)S(1)} %pad_maximum_fusion.6), channel_id=1, source_target_pairs={{128,0},{160,32},{192,64},{224,96},{256,128},{288,160},{320,192},{... | collective-permute-start | bytes 86024 | tf_op jit(solution)/shard_map/ppermute | solution.py:32
  136.2 2.3 copy-start.8
  136.7 1.8 copy-start.1
  138.5 6.8 %copy-start.5 = (bf16[256,1152]{0,1:T(8,128)(2,1)S(1)}, bf16[256,1152]{0,1:T(8,128)(2,1)}, u32[]{:S(2)}) copy-start(bf16[256,1152]{0,1:T(8,128)(2,1)} %copy.28) | copy-start | bytes 1769476
  142.0 8.8 %all-to-all-start.2 = ((bf16[4,64,256]{2,1,0:T(8,128)(2,1)}), bf16[4,64,256]{2,1,0:T(8,128)(2,1)S(1)}, u32[]{:S(2)}, u32[]{:S(2)}) async-start(bf16[4,64,256]{2,1,0:T(8,128)(2,1)} %broadcast_in_dim.16), calls=%async_computation.2 | async-start | bytes 262144 | tf_op jit(solution)/shard_map/all_to_all | solution.py:25
  150.8 7.0 %copy-start.6 = (bf16[256,1152]{0,1:T(8,128)(2,1)S(1)}, bf16[256,1152]{0,1:T(8,128)(2,1)}, u32[]{:S(2)}) copy-start(bf16[256,1152]{0,1:T(8,128)(2,1)} %multiply_convert_fusion) | copy-start | bytes 1769476
  153.6 20.6 %all-to-all-start.3 = ((bf16[8,32,1792]{2,1,0:T(8,128)(2,1)}), bf16[8,32,1792]{2,1,0:T(8,128)(2,1)S(1)}, u32[]{:S(2)}, u32[]{:S(2)}) async-start(bf16[8,32,1792]{2,1,0:T(8,128)(2,1)} %bitcast.21), calls=%async_computation.3 | async-start | bytes 1835008 | tf_op jit(solution)/shard_map/all_to_all | solution.py:106
  157.8 38.2 %reduce-scatter.2.cloned.1.call-start = ((), (), s32[]{:S(2)}) async-start(), calls=%async_computation.10 | async-start | bytes 1638400 | tf_op jit(solution)/shard_map/reduce_scatter | solution.py:108
  157.8 4.7 %copy-start.2 = (bf16[16,4,40,640]{3,2,1,0:T(8,128)(2,1)S(1)}, bf16[16,4,40,640]{3,2,1,0:T(8,128)(2,1)}, u32[]{:S(2)}) copy-start(bf16[16,4,40,640]{3,2,1,0:T(8,128)(2,1)} %copy-done.1) | copy-start | bytes 9830404
  162.6 11.7 %copy-start.10 = (f32[2,2,1792]{2,1,0:T(2,128)S(1)}, f32[2,2,1792]{2,1,0:T(2,128)}, u32[]{:S(2)}) copy-start(f32[2,2,1792]{2,1,0:T(2,128)} %copy-done.9) | copy-start | bytes 86020
  175.9 9.9 %all-to-all-start.4 = ((bf16[4,8,1792]{2,1,0:T(8,128)(2,1)}), bf16[4,8,1792]{2,1,0:T(8,128)(2,1)S(1)}, u32[]{:S(2)}, u32[]{:S(2)}) async-start(bf16[4,8,1792]{2,1,0:T(8,128)(2,1)} %bitcast.22), calls=%async_computation.5 | async-start | bytes 229376 | tf_op jit(solution)/shard_map/all_to_all | solution.py:111
  185.8 55.3 %copy-start.7 = (bf16[20,1792]{1,0:T(8,128)(2,1)S(1)}, bf16[20,1792]{1,0:T(8,128)(2,1)}, u32[]{:S(2)}) copy-start(bf16[20,1792]{1,0:T(8,128)(2,1)} %param.8) | copy-start | bytes 215044
  186.5 19.2 %all-to-all-start.5 = ((bf16[4,8,1792]{2,1,0:T(8,128)(2,1)}), bf16[4,8,1792]{2,1,0:T(8,128)(2,1)S(1)}, u32[]{:S(2)}, u32[]{:S(2)}) async-start(bf16[4,8,1792]{2,1,0:T(8,128)(2,1)} %broadcast_in_dim.17), calls=%async_computation.6 | async-start | bytes 229376 | tf_op jit(solution)/shard_map/all_to_all | solution.py:25
  191.8 50.2 %all-gather.5.cloned.1.call-start = ((), (), s32[]{:S(2)}) async-start(), calls=%async_computation.11 | async-start | bytes 1638400 | tf_op jit(solution)/shard_map/all_gather | solution.py:116
  215.7 25.4 %all-to-all-start.7 = ((bf16[8,32,1792]{2,1,0:T(8,128)(2,1)}), bf16[8,32,1792]{2,1,0:T(8,128)(2,1)S(1)}, u32[]{:S(2)}, u32[]{:S(2)}) async-start(bf16[8,32,1792]{2,1,0:T(8,128)(2,1)} %broadcast_in_dim.20), calls=%async_computation.8 | async-start | bytes 1835008 | tf_op jit(solution)/shard_map/all_to_all | solution.py:25
Sparse Core Ops, SparseCore 0:
  28.3 98.0 all-gather.2
  174.3 21.5 reduce-scatter.1
  198.1 38.2 all-gather.4

commit v8 on v7

--- a/solution.py
+++ b/solution.py
@@ -11,6 +11,7 @@
 EPSILON = 1e-08
 LEARN_RATE = 0.01
 RING = 4
+LANES = 128
 PAIR = 2
 
 
@@ -63,31 +64,28 @@
     half = width * 9 // 14
     first = jnp.concatenate([weight[:, :half], basis_part], axis=1)
     plane = spread(first, "fsdp").reshape(inner * rows, half + part)
+    spare = -(half + part) % LANES
+    moments = jnp.concatenate([first_moment, second_moment]).astype(bf16).reshape(-1, spare)
+    moments = jnp.pad(moments, ((0, inner * rows - moments.shape[0]), (0, 0)))
+    plane = jnp.concatenate([plane, moments], axis=1)
     full_a = lax.all_gather(plane, "dp", axis=0, tiled=True)
     plane, second = lax.optimization_barrier((plane, weight[:, half:]))
     second = spread(second, "fsdp", pairs).reshape(pair_rows, width - half)
     line = lax.all_gather(second, "dp", axis=0)
-    moments = jnp.stack([first_moment, second_moment])
-    line, moments = lax.optimization_barrier((line, moments))
     from_ahead, from_behind = ring_permutes("fsdp", PAIR)
     ahead, behind = from_ahead(line), from_behind(line)
-    carried = [moments] + [ring_permutes("dp", RING * j)[0](moments) for j in range(1, far)]
-    ahead, behind = lax.optimization_barrier((ahead, behind))
     across = from_ahead(ahead[: outer // 2]), from_behind(behind[outer // 2 :])
 
     def grad_of_preact(side, wanted):
         preact = jnp.dot(tokens, side, preferred_element_type=f32)
         return (wanted.astype(f32) * silu_slope(preact)).astype(bf16)
 
-    weight_a, full_basis = full_a[:, :half], full_a[:, half:]
+    weight_a, full_basis = full_a[:, :half], full_a[:, half : half + part]
     projected_part = lax.dot_general(
         full_basis, tokens, (((0,), (1,)), ((), ())), preferred_element_type=f32
     ).astype(bf16)
     projected = spread(projected_part, "tensor").reshape(rank, tokens.shape[0])
     grad_pre_a = grad_of_preact(weight_a, cotangent[:, :half])
-    across, carried = lax.optimization_barrier((across, carried))
-    moments = jnp.stack(by_class(carried, lax.axis_index("dp") // RING))
-
     blocks = by_class([line, ahead, jnp.concatenate(across), behind], lax.axis_index("fsdp") // PAIR)
     weight_b = jnp.stack(blocks, axis=1).reshape(depth, width - half)
     grad_pre_b = grad_of_preact(weight_b, cotangent[:, half:])
@@ -111,10 +109,13 @@
     landed = lax.all_to_all(blocks, "dp", 0, 0, tiled=True, axis_index_groups=fours)
     blocks = jnp.sum(landed.astype(f32), axis=0).astype(bf16)
     landed = spread(blocks, "dp", strides)
-    old_first, old_second = (moments[:, i].reshape(far * share, width) for i in range(2))
+    old = full_a[:, half + part :].reshape(far, RING, inner * rows, spare)
+    old = lax.dynamic_index_in_dim(old, lax.rem(lax.axis_index("dp"), RING), 1, keepdims=False)
+    old = old[:, : 2 * share * width // spare].reshape(far, 2, share, width).astype(f32)
+    old_first, old_second = old[:, 0], old[:, 1]
     old_first, token_rows = lax.optimization_barrier((BETA_ONE * old_first, token_rows))
     token_grad = lax.all_gather(token_rows, "tensor", axis=0, tiled=True)
-    reduced = jnp.sum(landed.astype(f32), axis=0)
+    reduced = jnp.sum(landed.astype(f32), axis=0).reshape(far, share, width)
 
     token_count = tokens.shape[0] * outer * inner
     grad_low = reduced / float(token_count)
@@ -123,14 +124,19 @@
     first_hat = new_first / (1.0 - BETA_ONE**ADAM_STEP)
     second_hat = new_second / (1.0 - BETA_TWO**ADAM_STEP)
     direction = (first_hat / (jnp.sqrt(second_hat) + EPSILON)).astype(bf16)
-    own = lax.axis_index("dp") // RING
-    new_first_moment, new_second_moment = (
-        lax.dynamic_index_in_dim(m.reshape(far, share, width), own, 0, keepdims=False)
-        for m in (new_first, new_second)
+    own = lax.dynamic_index_in_dim(grad_low, lax.axis_index("dp") // RING, 0, keepdims=False)
+    new_first_moment = BETA_ONE * first_moment + (1.0 - BETA_ONE) * own
+    new_second_moment = BETA_TWO * second_moment + (1.0 - BETA_TWO) * own * own
+    column = spread(direction.reshape(far * share, width), "fsdp", pairs)
+    column = spread(column.reshape(PAIR * far * share, width), "dp", fours)
+    column = column.reshape(PAIR * outer * share, width)
+    full_direction = spread(column, "fsdp", columns).reshape(rank, width)
+    basis_last = (
+        basis.reshape(rows, far, RING, RING, PAIR, share)
+        .transpose(0, 3, 2, 4, 1, 5)
+        .reshape(rows, rank)
     )
-    column = spread(direction, "dp", fours).reshape(outer * share, width)
-    full_direction = spread(column, "fsdp").reshape(rank, width)
-    update = jnp.dot(basis_perm, full_direction, preferred_element_type=f32)
+    update = jnp.dot(basis_last, full_direction, preferred_element_type=f32)
     new_weight = (weight.astype(f32) - LEARN_RATE * update).astype(bf16)
     return (token_grad, new_weight, new_first_moment, new_second_moment)
 

time: 253 us -> 240 us (0.949)
  the two profiles are of different devices: /device:TPU:32 before, /device:TPU:2 now
where the time goes in v8:
time: 240 us; the launch traced here: 239 us
  blocking collectives  74.5 us (31%)
  waiting for transfers between devices  62.7 us (26%)
  starting transfers between devices  46.1 us (19%)
  matrix products  18.1 us (8%)
  local copies, waits for them, and re-layouts  14.7 us (6%)
  between operations  14.2 us (6%)
  other arithmetic  8.4 us (4%)
    all_gather x1, blocking collectives, local(): line = lax.all_gather(second, 'dp', axis=0)  48.2 us
    all_to_all x4, waiting for transfers between devices, spread(): lax.all_to_all(copies, axis, 0, 0, tiled=True, axis_index_groups=groups)  32.3 us
    all_to_all x3, blocking collectives, spread(): lax.all_to_all(copies, axis, 0, 0, tiled=True, axis_index_groups=groups)  26.3 us
    all_to_all x4, starting transfers between devices, spread(): lax.all_to_all(copies, axis, 0, 0, tiled=True, axis_index_groups=groups)  24.4 us
    ppermute x2, waiting for transfers between devices, ring_permutes(): lax.ppermute(x, axis, behind)  12.5 us
    ppermute x2, starting transfers between devices, ring_permutes(): lax.ppermute(x, axis, ahead)  10.1 us
    all_to_all x1, waiting for transfers between devices, local(): lax.all_to_all(grad_part.reshape(inner, outer * share, width), 'fsdp', 0,...  8.96 us
    dot_general x2, matrix products, local(): lax.dot_general(g, w, (((1,), (1,)), ((), ())), preferred_element_type=f32)  7.07 us
  transfers between devices with their start and end apart: 13, of which 9 were waited for; matrix products, arithmetic and copies ran while one was open for 12% of the time, Pallas kernels for 0%

profile of v8, /device:TPU:2, one launch (start us, length us, event | category | flops | bytes accessed | tf_op | source)
XLA Modules:
  0.0 238.7 jit_solution(12254290402955795284)
XLA Ops:
  10.0 6.0 %all-to-all-start = ((bf16[8,20,1216]{2,1,0:T(8,128)(2,1)}), bf16[8,20,1216]{2,1,0:T(8,128)(2,1)S(1)}, u32[]{:S(2)}, u32[]{:S(2)}) async-start(bf16[8,20,1216]{2,1,0:T(8,128)(2,1)} %broadcast_in_dim.20), calls=%async_computation | async-start | bytes 983040 | tf_op jit(solution)/shard_map/all_to_all | solution.py:26
  17.6 9.6 %all-to-all-done = bf16[8,20,1216]{2,1,0:T(8,128)(2,1)S(1)} async-done(((bf16[8,20,1216]{2,1,0:T(8,128)(2,1)}), bf16[8,20,1216]{2,1,0:T(8,128)(2,1)S(1)}, u32[]{:S(2)}, u32[]{:S(2)}) %all-to-all-start) | async-done | bytes 389152 | tf_op jit(solution)/shard_map/all_to_all | solution.py:26
  28.3 8.1 %all_to_all.45 = bf16[2,20,640]{2,1,0:T(8,128)(2,1)S(1)} all-to-all(bf16[2,20,640]{2,1,0:T(8,128)(2,1)S(1)} %broadcast_in_dim.22), channel_id=1, replica_groups={{0,4},{8,12},{16,20},{24,28},{1,5},{9,13},{17,21},{25,29},{2,6},{10,14}..., dimensions={0} | all-to-all | bytes 102400 | tf_op jit(solution)/shard_map/all_to_all | solution.py:26
  36.4 48.2 %all_gather.10 = bf16[16,40,640]{2,1,0:T(8,128)(2,1)S(1)} all-gather(bf16[1,40,640]{2,1,0:T(8,128)(2,1)S(1)} %all_gather_reshape.3), channel_id=1, replica_groups=mesh['dp'=16,'fsdp'=8,'tensor'=4] {'dp'}, dimensions={0}, use_global_device_ids=true | all-gather | bytes 870400 | tf_op jit(solution)/shard_map/all_gather | solution.py:74
  84.6 2.1 collective-permute-start.2
  86.7 4.9 %collective-permute-start = (bf16[16,40,640]{2,1,0:T(8,128)(2,1)S(1)}, bf16[16,40,640]{2,1,0:T(8,128)(2,1)S(1)}, u32[]{:S(2)}, u32[]{:S(2)}) collective-permute-start(bf16[16,40,640]{2,1,0:T(8,128)(2,1)S(1)} %all_gather.10), channel_id=1, source_target_pairs={{8,0},{12,4},{16,8},{20,12},{24,16},{28,20},{0,24},{4,28},{9,1},{1... | collective-permute-start | bytes 2457608 | tf_op jit(solution)/shard_map/ppermute | solution.py:33
  91.7 10.5 %collective-permute-done.2 = bf16[16,40,640]{2,1,0:T(8,128)(2,1)S(1)} collective-permute-done((bf16[16,40,640]{2,1,0:T(8,128)(2,1)S(1)}, bf16[16,40,640]{2,1,0:T(8,128)(2,1)S(1)}, u32[]{:S(2)}, u32[]{:S(2)}) %collective-permute-start.2) | collective-permute-done | bytes 819232 | tf_op jit(solution)/shard_map/ppermute | solution.py:33
  103.1 1.9 collective-permute-start.3
  106.0 5.1 %collective-permute-start.1 = (bf16[8,40,640]{2,1,0:T(8,128)(2,1)}, bf16[8,40,640]{2,1,0:T(8,128)(2,1)}, u32[]{:S(2)}, u32[]{:S(2)}) collective-permute-start(bf16[8,40,640]{2,1,0:T(8,128)(2,1)} %slice.53), channel_id=1, source_target_pairs={{8,0},{12,4},{16,8},{20,12},{24,16},{28,20},{0,24},{4,28},{9,1},{1... | collective-permute-start | bytes 1228808 | tf_op jit(solution)/shard_map/ppermute | solution.py:33
  112.5 1.9 collective-permute-done.3
  114.5 2.5 %collective-permute-done.1 = bf16[8,40,640]{2,1,0:T(8,128)(2,1)} collective-permute-done((bf16[8,40,640]{2,1,0:T(8,128)(2,1)}, bf16[8,40,640]{2,1,0:T(8,128)(2,1)}, u32[]{:S(2)}, u32[]{:S(2)}) %collective-permute-start.1) | collective-permute-done | bytes 409632 | tf_op jit(solution)/shard_map/ppermute | solution.py:33
  116.9 1.2 maximum_bitcast_fusion
  118.2 1.7 pad_maximum_fusion
  120.7 1.7 copy-done.1
  124.4 1.6 convolution_convert_fusion.2
  126.7 4.6 %all-to-all-start.1 = ((bf16[4,64,256]{2,1,0:T(8,128)(2,1)}), bf16[4,64,256]{2,1,0:T(8,128)(2,1)S(1)}, u32[]{:S(2)}, u32[]{:S(2)}) async-start(bf16[4,64,256]{2,1,0:T(8,128)(2,1)} %broadcast_in_dim.21), calls=%async_computation.1 | async-start | bytes 262144 | tf_op jit(solution)/shard_map/all_to_all | solution.py:26
  131.3 5.5 %multiply_convert_fusion = bf16[256,1152]{0,1:T(8,128)(2,1)} fusion(bf16[256,2560]{1,0:T(8,128)(2,1)S(1)} %copy-done, bf16[2560,1280]{1,0:T(8,128)(2,1)} %all-gather.3.cloned.1.call-done, bf16[256,1152]{0,1:T(8,128)(2,1)S(1)} %copy-done.5), kind=kOutput, calls=%fused_computation.16 | convolution fusion | flops 1512898560 | bytes 8388608 | tf_op jit(solution)/shard_map/dot_general | solution.py:80
  136.7 1.5 convolution_convert_fusion
  139.5 4.3 %all-to-all-start.3 = ((bf16[8,32,1792]{2,1,0:T(8,128)(2,1)}), bf16[8,32,1792]{2,1,0:T(8,128)(2,1)S(1)}, u32[]{:S(2)}, u32[]{:S(2)}) async-start(bf16[8,32,1792]{2,1,0:T(8,128)(2,1)} %bitcast.18), calls=%async_computation.3 | async-start | bytes 1835008 | tf_op jit(solution)/shard_map/all_to_all | solution.py:104
  143.9 4.7 %fusion = f32[256,2560]{1,0:T(8,128)S(1)} fusion(bf16[256,1152]{0,1:T(8,128)(2,1)S(1)} %copy-done.6, bf16[2560,1280]{1,0:T(8,128)(2,1)} %all-gather.3.cloned.1.call-done), kind=kOutput, calls=%fused_computation | convolution fusion | flops 1509949440 | bytes 9109504 | tf_op jit(solution)/shard_map/dot_general | solution.py:100
  148.6 2.3 fusion.4
  151.0 9.0 %all-to-all-done.3 = bf16[8,32,1792]{2,1,0:T(8,128)(2,1)S(1)} async-done(((bf16[8,32,1792]{2,1,0:T(8,128)(2,1)}), bf16[8,32,1792]{2,1,0:T(8,128)(2,1)S(1)}, u32[]{:S(2)}, u32[]{:S(2)}) %all-to-all-start.3) | async-done | bytes 917536 | tf_op jit(solution)/shard_map/all_to_all | solution.py:104
  160.0 1.4 slice.48
  162.1 3.3 %all-to-all-start.4 = ((bf16[4,8,1792]{2,1,0:T(8,128)(2,1)}), bf16[4,8,1792]{2,1,0:T(8,128)(2,1)S(1)}, u32[]{:S(2)}, u32[]{:S(2)}) async-start(bf16[4,8,1792]{2,1,0:T(8,128)(2,1)} %bitcast.19), calls=%async_computation.5 | async-start | bytes 229376 | tf_op jit(solution)/shard_map/all_to_all | solution.py:109
  165.6 5.6 %all-to-all-done.4 = bf16[4,8,1792]{2,1,0:T(8,128)(2,1)S(1)} async-done(((bf16[4,8,1792]{2,1,0:T(8,128)(2,1)}), bf16[4,8,1792]{2,1,0:T(8,128)(2,1)S(1)}, u32[]{:S(2)}, u32[]{:S(2)}) %all-to-all-start.4) | async-done | bytes 114720 | tf_op jit(solution)/shard_map/all_to_all | solution.py:109
  171.9 10.2 %all-to-all-start.5 = ((bf16[4,8,1792]{2,1,0:T(8,128)(2,1)}), bf16[4,8,1792]{2,1,0:T(8,128)(2,1)S(1)}, u32[]{:S(2)}, u32[]{:S(2)}) async-start(bf16[4,8,1792]{2,1,0:T(8,128)(2,1)} %broadcast_in_dim.23), calls=%async_computation.6 | async-start | bytes 229376 | tf_op jit(solution)/shard_map/all_to_all | solution.py:26
  182.2 13.2 %all-to-all-done.5 = bf16[4,8,1792]{2,1,0:T(8,128)(2,1)S(1)} async-done(((bf16[4,8,1792]{2,1,0:T(8,128)(2,1)}), bf16[4,8,1792]{2,1,0:T(8,128)(2,1)S(1)}, u32[]{:S(2)}, u32[]{:S(2)}) %all-to-all-start.5) | async-done | bytes 114720 | tf_op jit(solution)/shard_map/all_to_all | solution.py:26
  195.9 8.0 %all_to_all.46 = bf16[2,8,1792]{2,1,0:T(8,128)(2,1)S(1)} all-to-all(bf16[2,8,1792]{2,1,0:T(8,128)(2,1)S(1)} %broadcast_in_dim.50), channel_id=1, replica_groups={{0,4},{8,12},{16,20},{24,28},{1,5},{9,13},{17,21},{25,29},{2,6},{10,14}..., dimensions={0} | all-to-all | bytes 114688 | tf_op jit(solution)/shard_map/all_to_all | solution.py:26
  203.9 10.2 %all_to_all.47 = bf16[4,16,1792]{2,1,0:T(8,128)(2,1)S(1)} all-to-all(bf16[4,16,1792]{2,1,0:T(8,128)(2,1)S(1)} %broadcast_in_dim.52), channel_id=1, replica_groups={{0,32,64,96},{128,160,192,224},{256,288,320,352},{384,416,448,480},{1,3..., dimensions={0} | all-to-all | bytes 458752 | tf_op jit(solution)/shard_map/all_to_all | solution.py:26
  215.1 3.5 %all-to-all-start.8 = ((bf16[4,64,1792]{2,1,0:T(8,128)(2,1)}), bf16[4,64,1792]{2,1,0:T(8,128)(2,1)S(1)}, u32[]{:S(2)}, u32[]{:S(2)}) async-start(bf16[4,64,1792]{2,1,0:T(8,128)(2,1)} %broadcast_in_dim.54), calls=%async_computation.9 | async-start | bytes 1835008 | tf_op jit(solution)/shard_map/all_to_all | solution.py:26
  219.3 9.4 %all-to-all-done.8 = bf16[4,64,1792]{2,1,0:T(8,128)(2,1)S(1)} async-done(((bf16[4,64,1792]{2,1,0:T(8,128)(2,1)}), bf16[4,64,1792]{2,1,0:T(8,128)(2,1)S(1)}, u32[]{:S(2)}, u32[]{:S(2)}) %all-to-all-start.8) | async-done | bytes 917536 | tf_op jit(solution)/shard_map/all_to_all | solution.py:26
  229.7 2.5 %copy.41 = bf16[256,2560]{1,0:T(8,128)(2,1)} copy(bf16[256,2560]{1,0:T(8,128)(2,1)} %all-gather.5.cloned.1.call-done) | data formatting | bytes 2621440
  (81 shorter events, 18.0 us)
Async XLA Ops:
  7.2 115.3 %copy-start = (bf16[256,2560]{1,0:T(8,128)(2,1)S(1)}, bf16[256,2560]{1,0:T(8,128)(2,1)}, u32[]{:S(2)}) copy-start(bf16[256,2560]{1,0:T(8,128)(2,1)} %param.6) | copy-start | bytes 3932164
  7.2 21.1 %slice-start.2 = ((bf16[20,1792]{1,0:T(8,128)(2,1)}), bf16[20,640]{1,0:T(8,128)(2,1)S(1)}, s32[]{:S(2)}) async-start(bf16[20,1792]{1,0:T(8,128)(2,1)} %param.8), calls=%async_computation.15 | async-start | bytes 61440 | tf_op jit(solution)/shard_map/slice | solution.py:72
  10.0 17.3 %all-to-all-start = ((bf16[8,20,1216]{2,1,0:T(8,128)(2,1)}), bf16[8,20,1216]{2,1,0:T(8,128)(2,1)S(1)}, u32[]{:S(2)}, u32[]{:S(2)}) async-start(bf16[8,20,1216]{2,1,0:T(8,128)(2,1)} %broadcast_in_dim.20), calls=%async_computation | async-start | bytes 983040 | tf_op jit(solution)/shard_map/all_to_all | solution.py:26
  16.0 108.4 %all-gather.3.cloned.1.call-start = ((), (), s32[]{:S(2)}) async-start(), calls=%async_computation.10 | async-start | bytes 6963200 | tf_op jit(solution)/shard_map/all_gather | solution.py:71
  28.2 83.0 %slice-start = ((bf16[256,1792]{1,0:T(8,128)(2,1)}), bf16[256,640]{1,0:T(8,128)(2,1)S(1)}, s32[]{:S(2)}) async-start(bf16[256,1792]{1,0:T(8,128)(2,1)} %param.7), calls=%async_computation.13 | async-start | bytes 655360 | tf_op jit(solution)/shard_map/slice | solution.py:91
  36.4 75.0 %slice-start.1 = ((bf16[256,1792]{1,0:T(8,128)(2,1)}), bf16[256,1152]{1,0:T(8,128)(2,1)S(1)}, s32[]{:S(2)}) async-start(bf16[256,1792]{1,0:T(8,128)(2,1)} %param.7), calls=%async_computation.14 | async-start | bytes 1179648 | tf_op jit(solution)/shard_map/slice | solution.py:88
  84.6 17.6 %collective-permute-start.2 = (bf16[16,40,640]{2,1,0:T(8,128)(2,1)S(1)}, bf16[16,40,640]{2,1,0:T(8,128)(2,1)S(1)}, u32[]{:S(2)}, u32[]{:S(2)}) collective-permute-start(bf16[16,40,640]{2,1,0:T(8,128)(2,1)S(1)} %all_gather.10), channel_id=1, source_target_pairs={{0,8},{4,12},{8,16},{12,20},{16,24},{20,28},{24,0},{28,4},{1,9},{5... | collective-permute-start | bytes 2457608 | tf_op jit(solution)/shard_map/ppermute | solution.py:33
  86.7 18.3 %collective-permute-start = (bf16[16,40,640]{2,1,0:T(8,128)(2,1)S(1)}, bf16[16,40,640]{2,1,0:T(8,128)(2,1)S(1)}, u32[]{:S(2)}, u32[]{:S(2)}) collective-permute-start(bf16[16,40,640]{2,1,0:T(8,128)(2,1)S(1)} %all_gather.10), channel_id=1, source_target_pairs={{8,0},{12,4},{16,8},{20,12},{24,16},{28,20},{0,24},{4,28},{9,1},{1... | collective-permute-start | bytes 2457608 | tf_op jit(solution)/shard_map/ppermute | solution.py:33
  102.2 2.8 %copy-start.3 = (bf16[16,40,640]{2,1,0:T(8,128)(2,1)}, bf16[16,40,640]{2,1,0:T(8,128)(2,1)S(1)}, u32[]{:S(2)}) copy-start(bf16[16,40,640]{2,1,0:T(8,128)(2,1)S(1)} %collective-permute-done.2) | copy-start | bytes 2457604
  103.1 11.4 %collective-permute-start.3 = (bf16[8,40,640]{2,1,0:T(8,128)(2,1)}, bf16[8,40,640]{2,1,0:T(8,128)(2,1)}, u32[]{:S(2)}, u32[]{:S(2)}) collective-permute-start(bf16[8,40,640]{2,1,0:T(8,128)(2,1)} %slice.54), channel_id=1, source_target_pairs={{0,8},{4,12},{8,16},{12,20},{16,24},{20,28},{24,0},{28,4},{1,9},{5... | collective-permute-start | bytes 1228808 | tf_op jit(solution)/shard_map/ppermute | solution.py:33
  105.0 1.0 copy-start.4
  106.0 10.9 %collective-permute-start.1 = (bf16[8,40,640]{2,1,0:T(8,128)(2,1)}, bf16[8,40,640]{2,1,0:T(8,128)(2,1)}, u32[]{:S(2)}, u32[]{:S(2)}) collective-permute-start(bf16[8,40,640]{2,1,0:T(8,128)(2,1)} %slice.53), channel_id=1, source_target_pairs={{8,0},{12,4},{16,8},{20,12},{24,16},{28,20},{0,24},{4,28},{9,1},{1... | collective-permute-start | bytes 1228808 | tf_op jit(solution)/shard_map/ppermute | solution.py:33
  120.7 1.7 copy-start.1
  122.4 8.8 %copy-start.5 = (bf16[256,1152]{0,1:T(8,128)(2,1)S(1)}, bf16[256,1152]{0,1:T(8,128)(2,1)}, u32[]{:S(2)}) copy-start(bf16[256,1152]{0,1:T(8,128)(2,1)} %copy.38) | copy-start | bytes 1769476
  126.7 10.1 %all-to-all-start.1 = ((bf16[4,64,256]{2,1,0:T(8,128)(2,1)}), bf16[4,64,256]{2,1,0:T(8,128)(2,1)S(1)}, u32[]{:S(2)}, u32[]{:S(2)}) async-start(bf16[4,64,256]{2,1,0:T(8,128)(2,1)} %broadcast_in_dim.21), calls=%async_computation.1 | async-start | bytes 262144 | tf_op jit(solution)/shard_map/all_to_all | solution.py:26
  136.7 7.1 %copy-start.6 = (bf16[256,1152]{0,1:T(8,128)(2,1)S(1)}, bf16[256,1152]{0,1:T(8,128)(2,1)}, u32[]{:S(2)}) copy-start(bf16[256,1152]{0,1:T(8,128)(2,1)} %multiply_convert_fusion) | copy-start | bytes 1769476
  139.5 20.4 %all-to-all-start.3 = ((bf16[8,32,1792]{2,1,0:T(8,128)(2,1)}), bf16[8,32,1792]{2,1,0:T(8,128)(2,1)S(1)}, u32[]{:S(2)}, u32[]{:S(2)}) async-start(bf16[8,32,1792]{2,1,0:T(8,128)(2,1)} %bitcast.18), calls=%async_computation.3 | async-start | bytes 1835008 | tf_op jit(solution)/shard_map/all_to_all | solution.py:104
  143.8 51.9 %reduce-scatter.2.cloned.1.call-start = ((), (), s32[]{:S(2)}) async-start(), calls=%async_computation.11 | async-start | bytes 1638400 | tf_op jit(solution)/shard_map/reduce_scatter | solution.py:106
  143.9 4.7 %copy-start.2 = (bf16[16,4,40,640]{3,2,1,0:T(8,128)(2,1)S(1)}, bf16[16,4,40,640]{3,2,1,0:T(8,128)(2,1)}, u32[]{:S(2)}) copy-start(bf16[16,4,40,640]{3,2,1,0:T(8,128)(2,1)} %copy-done.1) | copy-start | bytes 9830404
  162.1 9.2 %all-to-all-start.4 = ((bf16[4,8,1792]{2,1,0:T(8,128)(2,1)}), bf16[4,8,1792]{2,1,0:T(8,128)(2,1)S(1)}, u32[]{:S(2)}, u32[]{:S(2)}) async-start(bf16[4,8,1792]{2,1,0:T(8,128)(2,1)} %bitcast.19), calls=%async_computation.5 | async-start | bytes 229376 | tf_op jit(solution)/shard_map/all_to_all | solution.py:109
  171.9 23.5 %all-to-all-start.5 = ((bf16[4,8,1792]{2,1,0:T(8,128)(2,1)}), bf16[4,8,1792]{2,1,0:T(8,128)(2,1)S(1)}, u32[]{:S(2)}, u32[]{:S(2)}) async-start(bf16[4,8,1792]{2,1,0:T(8,128)(2,1)} %broadcast_in_dim.23), calls=%async_computation.6 | async-start | bytes 229376 | tf_op jit(solution)/shard_map/all_to_all | solution.py:26
  182.2 47.5 %all-gather.5.cloned.1.call-start = ((), (), s32[]{:S(2)}) async-start(), calls=%async_computation.12 | async-start | bytes 1638400 | tf_op jit(solution)/shard_map/all_gather | solution.py:117
  195.5 23.2 %copy-start.8 = (f32[2,1792]{1,0:T(2,128)S(1)}, f32[2,1792]{1,0:T(2,128)}, u32[]{:S(2)}) copy-start(f32[2,1792]{1,0:T(2,128)} %param.11) | copy-start | bytes 43012
  195.5 23.2 %copy-start.9 = (f32[2,1792]{1,0:T(2,128)S(1)}, f32[2,1792]{1,0:T(2,128)}, u32[]{:S(2)}) copy-start(f32[2,1792]{1,0:T(2,128)} %param.10) | copy-start | bytes 43012
  195.5 33.2 %copy-start.7 = (bf16[20,1792]{1,0:T(8,128)(2,1)S(1)}, bf16[20,1792]{1,0:T(8,128)(2,1)}, u32[]{:S(2)}) copy-start(bf16[20,1792]{1,0:T(8,128)(2,1)} %param.8) | copy-start | bytes 215044
  215.1 13.7 %all-to-all-start.8 = ((bf16[4,64,1792]{2,1,0:T(8,128)(2,1)}), bf16[4,64,1792]{2,1,0:T(8,128)(2,1)S(1)}, u32[]{:S(2)}, u32[]{:S(2)}) async-start(bf16[4,64,1792]{2,1,0:T(8,128)(2,1)} %broadcast_in_dim.54), calls=%async_computation.9 | async-start | bytes 1835008 | tf_op jit(solution)/shard_map/all_to_all | solution.py:26
Sparse Core Ops, SparseCore 0:
  28.4 95.9 all-gather.2
  160.1 24.8 reduce-scatter.1
  195.8 22.2 all-gather.4

commit v9 on v8

--- a/solution.py
+++ b/solution.py
@@ -1,6 +1,8 @@
 import jax
 import jax.numpy as jnp
 from jax import lax
+from jax.experimental import pallas as pl
+from jax.experimental.pallas import tpu as pltpu
 from jax.sharding import PartitionSpec as P
 
 ADAM_STEP = 10
@@ -18,6 +20,34 @@
 def silu_slope(preact):
     logistic = jax.nn.sigmoid(preact)
     return logistic * (1.0 + preact * (1.0 - logistic))
+
+
+def slope_kernel(tokens_ref, weight_ref, cotangent_ref, out_ref):
+    preact = jnp.dot(tokens_ref[...], weight_ref[...], preferred_element_type=jnp.float32)
+    wanted = cotangent_ref[...].astype(jnp.float32)
+    out_ref[...] = (wanted * silu_slope(preact)).astype(out_ref.dtype)
+
+
+def grad_of_first(tokens, weight, cotangent, width):
+    count, depth = tokens.shape
+    block = 3 * LANES
+    return pl.pallas_call(
+        slope_kernel,
+        grid=(width // block,),
+        in_specs=[
+            pl.BlockSpec((count, depth), lambda i: (0, 0)),
+            pl.BlockSpec((depth, block), lambda i: (0, i)),
+            pl.BlockSpec((count, block), lambda i: (0, i)),
+        ],
+        out_specs=pl.BlockSpec((count, block), lambda i: (0, i)),
+        out_shape=jax.ShapeDtypeStruct((count, width), jnp.bfloat16),
+        compiler_params=pltpu.CompilerParams(vmem_limit_bytes=16 * 1024 * 1024),
+        cost_estimate=pl.CostEstimate(
+            flops=2 * count * depth * width,
+            bytes_accessed=2 * (depth * width + count * (depth + 2 * width)),
+            transcendentals=count * width,
+        ),
+    )(tokens, weight, cotangent)
 
 
 def spread(block, axis, groups=None):
@@ -85,7 +115,7 @@
         full_basis, tokens, (((0,), (1,)), ((), ())), preferred_element_type=f32
     ).astype(bf16)
     projected = spread(projected_part, "tensor").reshape(rank, tokens.shape[0])
-    grad_pre_a = grad_of_preact(weight_a, cotangent[:, :half])
+    grad_pre_a = grad_of_first(tokens, full_a, cotangent, half)
     blocks = by_class([line, ahead, jnp.concatenate(across), behind], lax.axis_index("fsdp") // PAIR)
     weight_b = jnp.stack(blocks, axis=1).reshape(depth, width - half)
     grad_pre_b = grad_of_preact(weight_b, cotangent[:, half:])
@@ -131,6 +161,8 @@
     column = spread(column.reshape(PAIR * far * share, width), "dp", fours)
     column = column.reshape(PAIR * outer * share, width)
     full_direction = spread(column, "fsdp", columns).reshape(rank, width)
+    token_grad = token_grad * lax.optimization_barrier(jnp.ones((), bf16))
+    full_direction, token_grad = lax.optimization_barrier((full_direction, token_grad))
     basis_last = (
         basis.reshape(rows, far, RING, RING, PAIR, share)
         .transpose(0, 3, 2, 4, 1, 5)

time: 240 us -> 236 us (0.983)
  blocking collectives: 74.5 us -> 63.1 us
  waiting for transfers between devices: 62.7 us -> 69.8 us
  matrix products: 18.1 us -> 11.4 us
  Pallas kernels: 0 us -> 3.78 us
    all_to_all x3 -> x2, blocking collectives: 26.3 us -> 15.9 us  [spread(): lax.all_to_all(copies, axis, 0, 0, tiled=True, axis_index_groups=groups)]
    dot_general x2 -> x1, matrix products: 6.61 us -> 1.15 us  [grad_of_preact(): preact = jnp.dot(tokens, side, preferred_element_type=f32)]
    pallas_call x0 -> x1, Pallas kernels: none -> 3.78 us  [grad_of_first(): pl.pallas_call(slope_kernel, grid=(width // block,), in_specs=[pl.BlockSp...]
    reduce_scatter x1, waiting for transfers between devices: 0.02 us -> 2.77 us  [local(): lax.psum_scatter(partial_rows, 'tensor', scatter_dimension=0, tiled=True)]
    all_gather x1, waiting for transfers between devices: 0.77 us -> 3.5 us  [local(): full_a = lax.all_gather(plane, 'dp', axis=0, tiled=True)]
    mul x0 -> x1, other arithmetic: none -> 2.46 us  [local(): token_grad = token_grad * lax.optimization_barrier(jnp.ones((), bf16))]
    all_to_all x4 -> x5, starting transfers between devices: 24.4 us -> 25.9 us  [spread(): lax.all_to_all(copies, axis, 0, 0, tiled=True, axis_index_groups=groups)]
    all_to_all x4 -> x5, waiting for transfers between devices: 32.3 us -> 33.6 us  [spread(): lax.all_to_all(copies, axis, 0, 0, tiled=True, axis_index_groups=groups)]
  transfers between devices with their start and end apart: 13 -> 14, of which waited for: 9 -> 11; matrix products, arithmetic and copies ran while one was open for 12% -> 10% of each run, Pallas kernels for 0% -> 2%
where the time goes in v9:
time: 236 us; the launch traced here: 235 us
  waiting for transfers between devices  69.8 us (30%)
  blocking collectives  63.1 us (27%)
  starting transfers between devices  47.9 us (20%)
  local copies, waits for them, and re-layouts  15 us (6%)
  between operations  14.2 us (6%)
  matrix products  11.4 us (5%)
  other arithmetic  9.7 us (4%)
  Pallas kernels  3.78 us (2%)
    all_gather x1, blocking collectives, local(): line = lax.all_gather(second, 'dp', axis=0)  47.2 us
    all_to_all x5, waiting for transfers between devices, spread(): lax.all_to_all(copies, axis, 0, 0, tiled=True, axis_index_groups=groups)  33.6 us
    all_to_all x5, starting transfers between devices, spread(): lax.all_to_all(copies, axis, 0, 0, tiled=True, axis_index_groups=groups)  25.9 us
    all_to_all x2, blocking collectives, spread(): lax.all_to_all(copies, axis, 0, 0, tiled=True, axis_index_groups=groups)  15.9 us
    ppermute x2, waiting for transfers between devices, ring_permutes(): lax.ppermute(x, axis, behind)  13 us
    ppermute x2, starting transfers between devices, ring_permutes(): lax.ppermute(x, axis, ahead)  9.84 us
    all_to_all x1, waiting for transfers between devices, local(): lax.all_to_all(grad_part.reshape(inner, outer * share, width), 'fsdp', 0,...  8.99 us
    dot_general x2, matrix products, local(): lax.dot_general(g, w, (((1,), (1,)), ((), ())), preferred_element_type=f32)  7.05 us
  transfers between devices with their start and end apart: 14, of which 11 were waited for; matrix products, arithmetic and copies ran while one was open for 10% of the time, Pallas kernels for 2%

profile of v9, /device:TPU:2, one launch (start us, length us, event | category | flops | bytes accessed | tf_op | source)
XLA Modules:
  0.0 234.9 jit_solution(10123458314226344480)
XLA Ops:
  9.8 6.2 %all-to-all-start = ((bf16[8,20,1216]{2,1,0:T(8,128)(2,1)}), bf16[8,20,1216]{2,1,0:T(8,128)(2,1)S(1)}, u32[]{:S(2)}, u32[]{:S(2)}) async-start(bf16[8,20,1216]{2,1,0:T(8,128)(2,1)} %broadcast_in_dim.20), calls=%async_computation | async-start | bytes 983040 | tf_op jit(solution)/shard_map/all_to_all | solution.py:56
  17.6 9.6 %all-to-all-done = bf16[8,20,1216]{2,1,0:T(8,128)(2,1)S(1)} async-done(((bf16[8,20,1216]{2,1,0:T(8,128)(2,1)}), bf16[8,20,1216]{2,1,0:T(8,128)(2,1)S(1)}, u32[]{:S(2)}, u32[]{:S(2)}) %all-to-all-start) | async-done | bytes 389152 | tf_op jit(solution)/shard_map/all_to_all | solution.py:56
  28.3 8.0 %all_to_all.45 = bf16[2,20,640]{2,1,0:T(8,128)(2,1)S(1)} all-to-all(bf16[2,20,640]{2,1,0:T(8,128)(2,1)S(1)} %broadcast_in_dim.22), channel_id=1, replica_groups={{0,4},{8,12},{16,20},{24,28},{1,5},{9,13},{17,21},{25,29},{2,6},{10,14}..., dimensions={0} | all-to-all | bytes 102400 | tf_op jit(solution)/shard_map/all_to_all | solution.py:56
  36.3 47.2 %all_gather.10 = bf16[16,40,640]{2,1,0:T(8,128)(2,1)S(1)} all-gather(bf16[1,40,640]{2,1,0:T(8,128)(2,1)S(1)} %all_gather_reshape.3), channel_id=1, replica_groups=mesh['dp'=16,'fsdp'=8,'tensor'=4] {'dp'}, dimensions={0}, use_global_device_ids=true | all-gather | bytes 870400 | tf_op jit(solution)/shard_map/all_gather | solution.py:104
  83.4 2.3 collective-permute-start.2
  85.8 4.7 %collective-permute-start = (bf16[16,40,640]{2,1,0:T(8,128)(2,1)S(1)}, bf16[16,40,640]{2,1,0:T(8,128)(2,1)S(1)}, u32[]{:S(2)}, u32[]{:S(2)}) collective-permute-start(bf16[16,40,640]{2,1,0:T(8,128)(2,1)S(1)} %all_gather.10), channel_id=1, source_target_pairs={{8,0},{12,4},{16,8},{20,12},{24,16},{28,20},{0,24},{4,28},{9,1},{1... | collective-permute-start | bytes 2457608 | tf_op jit(solution)/shard_map/ppermute | solution.py:63
  90.5 10.5 %collective-permute-done.2 = bf16[16,40,640]{2,1,0:T(8,128)(2,1)S(1)} collective-permute-done((bf16[16,40,640]{2,1,0:T(8,128)(2,1)S(1)}, bf16[16,40,640]{2,1,0:T(8,128)(2,1)S(1)}, u32[]{:S(2)}, u32[]{:S(2)}) %collective-permute-start.2) | collective-permute-done | bytes 819232 | tf_op jit(solution)/shard_map/ppermute | solution.py:63
  101.8 1.9 collective-permute-start.3
  104.5 5.1 %collective-permute-start.1 = (bf16[8,40,640]{2,1,0:T(8,128)(2,1)}, bf16[8,40,640]{2,1,0:T(8,128)(2,1)}, u32[]{:S(2)}, u32[]{:S(2)}) collective-permute-start(bf16[8,40,640]{2,1,0:T(8,128)(2,1)} %slice.48), channel_id=1, source_target_pairs={{8,0},{12,4},{16,8},{20,12},{24,16},{28,20},{0,24},{4,28},{9,1},{1... | collective-permute-start | bytes 1228808 | tf_op jit(solution)/shard_map/ppermute | solution.py:63
  110.6 2.5 %collective-permute-done.3 = bf16[8,40,640]{2,1,0:T(8,128)(2,1)} collective-permute-done((bf16[8,40,640]{2,1,0:T(8,128)(2,1)}, bf16[8,40,640]{2,1,0:T(8,128)(2,1)}, u32[]{:S(2)}, u32[]{:S(2)}) %collective-permute-start.3) | collective-permute-done | bytes 409632 | tf_op jit(solution)/shard_map/ppermute | solution.py:63
  113.1 2.3 collective-permute-done.1
  118.0 1.7 copy-done.3
  120.9 3.5 %all-gather.3.cloned.1.call-done.weight_ref = bf16[2560,1280]{1,0:T(8,128)(2,1)} async-done(((bf16[160,1280]{1,0:T(8,128)(2,1)}), bf16[2560,1280]{1,0:T(8,128)(2,1)}) %all-gather.3.cloned.1.call-update) | async-done | bytes 6553616 | tf_op jit(solution)/shard_map/all_gather | solution.py:101
  124.4 1.6 convolution_convert_fusion.2
  126.7 4.2 %all-to-all-start.1 = ((bf16[4,64,256]{2,1,0:T(8,128)(2,1)}), bf16[4,64,256]{2,1,0:T(8,128)(2,1)S(1)}, u32[]{:S(2)}, u32[]{:S(2)}) async-start(bf16[4,64,256]{2,1,0:T(8,128)(2,1)} %broadcast_in_dim.21), calls=%async_computation.1 | async-start | bytes 262144 | tf_op jit(solution)/shard_map/all_to_all | solution.py:56
  131.0 2.9 %copy-done = bf16[2560,1280]{1,0:T(8,128)(2,1)S(1)} copy-done((bf16[2560,1280]{1,0:T(8,128)(2,1)S(1)}, bf16[2560,1280]{1,0:T(8,128)(2,1)}, u32[]{:S(2)}) %copy-start) | copy-done | bytes 6553624
  133.8 3.8 %shard_map.93 = bf16[256,1152]{1,0:T(8,128)(2,1)S(1)} custom-call(bf16[256,2560]{1,0:T(8,128)(2,1)S(1)} %copy-done.1, bf16[2560,1280]{1,0:T(8,128)(2,1)S(1)} %copy-done, bf16[256,1792]{1,0:T(8,128)(2,1)S(1)} %copy-done.2), custom_call_target="tpu_custom_call" | custom-call | flops 1509949440 | bytes 8388608 | tf_op jit(solution)/shard_map/pallas_call | solution.py:34
  139.3 4.5 %all-to-all-start.3 = ((bf16[8,32,1792]{2,1,0:T(8,128)(2,1)}), bf16[8,32,1792]{2,1,0:T(8,128)(2,1)S(1)}, u32[]{:S(2)}, u32[]{:S(2)}) async-start(bf16[8,32,1792]{2,1,0:T(8,128)(2,1)} %bitcast.17), calls=%async_computation.3 | async-start | bytes 1835008 | tf_op jit(solution)/shard_map/all_to_all | solution.py:134
  143.9 4.7 %fusion = f32[256,2560]{1,0:T(8,128)S(1)} fusion(bf16[256,1152]{1,0:T(8,128)(2,1)S(1)} %shard_map.93, bf16[2560,1280]{1,0:T(8,128)(2,1)} %all-gather.3.cloned.1.call-done.weight_ref), kind=kOutput, calls=%fused_computation | convolution fusion | flops 1509949440 | bytes 9109504 | tf_op jit(solution)/shard_map/dot_general | solution.py:130
  148.6 2.3 fusion.2
  150.9 9.0 %all-to-all-done.3 = bf16[8,32,1792]{2,1,0:T(8,128)(2,1)S(1)} async-done(((bf16[8,32,1792]{2,1,0:T(8,128)(2,1)}), bf16[8,32,1792]{2,1,0:T(8,128)(2,1)S(1)}, u32[]{:S(2)}, u32[]{:S(2)}) %all-to-all-start.3) | async-done | bytes 917536 | tf_op jit(solution)/shard_map/all_to_all | solution.py:134
  162.1 3.3 %all-to-all-start.4 = ((bf16[4,8,1792]{2,1,0:T(8,128)(2,1)}), bf16[4,8,1792]{2,1,0:T(8,128)(2,1)S(1)}, u32[]{:S(2)}, u32[]{:S(2)}) async-start(bf16[4,8,1792]{2,1,0:T(8,128)(2,1)} %bitcast.18), calls=%async_computation.5 | async-start | bytes 229376 | tf_op jit(solution)/shard_map/all_to_all | solution.py:139
  165.6 5.6 %all-to-all-done.4 = bf16[4,8,1792]{2,1,0:T(8,128)(2,1)S(1)} async-done(((bf16[4,8,1792]{2,1,0:T(8,128)(2,1)}), bf16[4,8,1792]{2,1,0:T(8,128)(2,1)S(1)}, u32[]{:S(2)}, u32[]{:S(2)}) %all-to-all-start.4) | async-done | bytes 114720 | tf_op jit(solution)/shard_map/all_to_all | solution.py:139
  171.9 8.5 %all-to-all-start.5 = ((bf16[4,8,1792]{2,1,0:T(8,128)(2,1)}), bf16[4,8,1792]{2,1,0:T(8,128)(2,1)S(1)}, u32[]{:S(2)}, u32[]{:S(2)}) async-start(bf16[4,8,1792]{2,1,0:T(8,128)(2,1)} %broadcast_in_dim.23), calls=%async_computation.6 | async-start | bytes 229376 | tf_op jit(solution)/shard_map/all_to_all | solution.py:56
  180.4 2.8 %reduce-scatter.2.cloned.1.call-done = bf16[64,2560]{1,0:T(8,128)(2,1)} async-done(((bf16[256,2560]{1,0:T(8,128)(2,1)}), bf16[64,2560]{1,0:T(8,128)(2,1)}) %reduce-scatter.2.cloned.1.call-update) | async-done | bytes 327696 | tf_op jit(solution)/shard_map/reduce_scatter | solution.py:136
  183.2 10.5 %all-to-all-done.5 = bf16[4,8,1792]{2,1,0:T(8,128)(2,1)S(1)} async-done(((bf16[4,8,1792]{2,1,0:T(8,128)(2,1)}), bf16[4,8,1792]{2,1,0:T(8,128)(2,1)S(1)}, u32[]{:S(2)}, u32[]{:S(2)}) %all-to-all-start.5) | async-done | bytes 114720 | tf_op jit(solution)/shard_map/all_to_all | solution.py:56
  194.0 8.0 %all_to_all.46 = bf16[2,8,1792]{2,1,0:T(8,128)(2,1)S(1)} all-to-all(bf16[2,8,1792]{2,1,0:T(8,128)(2,1)S(1)} %broadcast_in_dim.50), channel_id=1, replica_groups={{0,4},{8,12},{16,20},{24,28},{1,5},{9,13},{17,21},{25,29},{2,6},{10,14}..., dimensions={0} | all-to-all | bytes 114688 | tf_op jit(solution)/shard_map/all_to_all | solution.py:56
  202.7 3.5 %all-to-all-start.7 = ((bf16[4,16,1792]{2,1,0:T(8,128)(2,1)}), bf16[4,16,1792]{2,1,0:T(8,128)(2,1)S(1)}, u32[]{:S(2)}, u32[]{:S(2)}) async-start(bf16[4,16,1792]{2,1,0:T(8,128)(2,1)} %broadcast_in_dim.52), calls=%async_computation.8 | async-start | bytes 458752 | tf_op jit(solution)/shard_map/all_to_all | solution.py:56
  206.9 5.8 %all-to-all-done.7 = bf16[4,16,1792]{2,1,0:T(8,128)(2,1)S(1)} async-done(((bf16[4,16,1792]{2,1,0:T(8,128)(2,1)}), bf16[4,16,1792]{2,1,0:T(8,128)(2,1)S(1)}, u32[]{:S(2)}, u32[]{:S(2)}) %all-to-all-start.7) | async-done | bytes 229408 | tf_op jit(solution)/shard_map/all_to_all | solution.py:56
  213.7 3.5 %all-to-all-start.8 = ((bf16[4,64,1792]{2,1,0:T(8,128)(2,1)}), bf16[4,64,1792]{2,1,0:T(8,128)(2,1)S(1)}, u32[]{:S(2)}, u32[]{:S(2)}) async-start(bf16[4,64,1792]{2,1,0:T(8,128)(2,1)} %broadcast_in_dim.54), calls=%async_computation.9 | async-start | bytes 1835008 | tf_op jit(solution)/shard_map/all_to_all | solution.py:56
  217.3 2.5 %broadcast_multiply_fusion = bf16[256,2560]{1,0:T(8,128)(2,1)} fusion(bf16[256,2560]{1,0:T(8,128)(2,1)} %all-gather.5.cloned.1.call-done, bf16[]{:T(256)} %constant.114.clone.1), kind=kLoop, calls=%fused_computation.23 | loop fusion | flops 655360 | bytes 2621442 | tf_op jit(solution)/shard_map/mul | solution.py:164
  219.7 7.7 %all-to-all-done.8 = bf16[4,64,1792]{2,1,0:T(8,128)(2,1)S(1)} async-done(((bf16[4,64,1792]{2,1,0:T(8,128)(2,1)}), bf16[4,64,1792]{2,1,0:T(8,128)(2,1)S(1)}, u32[]{:S(2)}, u32[]{:S(2)}) %all-to-all-start.8) | async-done | bytes 917536 | tf_op jit(solution)/shard_map/all_to_all | solution.py:56
  (77 shorter events, 20.6 us)
Async XLA Ops:
  7.2 21.1 %slice-start.1 = ((bf16[20,1792]{1,0:T(8,128)(2,1)}), bf16[20,640]{1,0:T(8,128)(2,1)S(1)}, s32[]{:S(2)}) async-start(bf16[20,1792]{1,0:T(8,128)(2,1)} %param.8), calls=%async_computation.14 | async-start | bytes 61440 | tf_op jit(solution)/shard_map/slice | solution.py:102
  9.8 99.9 %slice-start = ((bf16[256,1792]{1,0:T(8,128)(2,1)}), bf16[256,640]{1,0:T(8,128)(2,1)S(1)}, s32[]{:S(2)}) async-start(bf16[256,1792]{1,0:T(8,128)(2,1)} %cotangent_ref.1), calls=%async_computation.13 | async-start | bytes 655360 | tf_op jit(solution)/shard_map/slice | solution.py:121
  9.8 17.4 %all-to-all-start = ((bf16[8,20,1216]{2,1,0:T(8,128)(2,1)}), bf16[8,20,1216]{2,1,0:T(8,128)(2,1)S(1)}, u32[]{:S(2)}, u32[]{:S(2)}) async-start(bf16[8,20,1216]{2,1,0:T(8,128)(2,1)} %broadcast_in_dim.20), calls=%async_computation | async-start | bytes 983040 | tf_op jit(solution)/shard_map/all_to_all | solution.py:56
  16.0 108.4 %all-gather.3.cloned.1.call-start = ((), (), s32[]{:S(2)}) async-start(), calls=%async_computation.10 | async-start | bytes 6963200 | tf_op jit(solution)/shard_map/all_gather | solution.py:101
  83.4 17.6 %collective-permute-start.2 = (bf16[16,40,640]{2,1,0:T(8,128)(2,1)S(1)}, bf16[16,40,640]{2,1,0:T(8,128)(2,1)S(1)}, u32[]{:S(2)}, u32[]{:S(2)}) collective-permute-start(bf16[16,40,640]{2,1,0:T(8,128)(2,1)S(1)} %all_gather.10), channel_id=1, source_target_pairs={{0,8},{4,12},{8,16},{12,20},{16,24},{20,28},{24,0},{28,4},{1,9},{5... | collective-permute-start | bytes 2457608 | tf_op jit(solution)/shard_map/ppermute | solution.py:63
  85.8 17.9 %collective-permute-start = (bf16[16,40,640]{2,1,0:T(8,128)(2,1)S(1)}, bf16[16,40,640]{2,1,0:T(8,128)(2,1)S(1)}, u32[]{:S(2)}, u32[]{:S(2)}) collective-permute-start(bf16[16,40,640]{2,1,0:T(8,128)(2,1)S(1)} %all_gather.10), channel_id=1, source_target_pairs={{8,0},{12,4},{16,8},{20,12},{24,16},{28,20},{0,24},{4,28},{9,1},{1... | collective-permute-start | bytes 2457608 | tf_op jit(solution)/shard_map/ppermute | solution.py:63
  101.8 11.4 %collective-permute-start.3 = (bf16[8,40,640]{2,1,0:T(8,128)(2,1)}, bf16[8,40,640]{2,1,0:T(8,128)(2,1)}, u32[]{:S(2)}, u32[]{:S(2)}) collective-permute-start(bf16[8,40,640]{2,1,0:T(8,128)(2,1)} %slice.49), channel_id=1, source_target_pairs={{0,8},{4,12},{8,16},{12,20},{16,24},{20,28},{24,0},{28,4},{1,9},{5... | collective-permute-start | bytes 1228808 | tf_op jit(solution)/shard_map/ppermute | solution.py:63
  104.5 10.9 %collective-permute-start.1 = (bf16[8,40,640]{2,1,0:T(8,128)(2,1)}, bf16[8,40,640]{2,1,0:T(8,128)(2,1)}, u32[]{:S(2)}, u32[]{:S(2)}) collective-permute-start(bf16[8,40,640]{2,1,0:T(8,128)(2,1)} %slice.48), channel_id=1, source_target_pairs={{8,0},{12,4},{16,8},{20,12},{24,16},{28,20},{0,24},{4,28},{9,1},{1... | collective-permute-start | bytes 1228808 | tf_op jit(solution)/shard_map/ppermute | solution.py:63
  117.5 2.3 copy-start.1
  117.5 2.3 copy-start.6
  118.0 1.7 copy-start.3
  119.8 11.2 %copy-start.2 = (bf16[256,1792]{1,0:T(8,128)(2,1)S(1)}, bf16[256,1792]{1,0:T(8,128)(2,1)}, u32[]{:S(2)}) copy-start(bf16[256,1792]{1,0:T(8,128)(2,1)} %cotangent_ref.1) | copy-start | bytes 2752516
  126.7 10.9 %all-to-all-start.1 = ((bf16[4,64,256]{2,1,0:T(8,128)(2,1)}), bf16[4,64,256]{2,1,0:T(8,128)(2,1)S(1)}, u32[]{:S(2)}, u32[]{:S(2)}) async-start(bf16[4,64,256]{2,1,0:T(8,128)(2,1)} %broadcast_in_dim.21), calls=%async_computation.1 | async-start | bytes 262144 | tf_op jit(solution)/shard_map/all_to_all | solution.py:56
  131.0 2.9 %copy-start = (bf16[2560,1280]{1,0:T(8,128)(2,1)S(1)}, bf16[2560,1280]{1,0:T(8,128)(2,1)}, u32[]{:S(2)}) copy-start(bf16[2560,1280]{1,0:T(8,128)(2,1)} %all-gather.3.cloned.1.call-done.weight_ref) | copy-start | bytes 19660804
  139.3 20.6 %all-to-all-start.3 = ((bf16[8,32,1792]{2,1,0:T(8,128)(2,1)}), bf16[8,32,1792]{2,1,0:T(8,128)(2,1)S(1)}, u32[]{:S(2)}, u32[]{:S(2)}) async-start(bf16[8,32,1792]{2,1,0:T(8,128)(2,1)} %bitcast.17), calls=%async_computation.3 | async-start | bytes 1835008 | tf_op jit(solution)/shard_map/all_to_all | solution.py:134
  143.8 39.4 %reduce-scatter.2.cloned.1.call-start = ((), (), s32[]{:S(2)}) async-start(), calls=%async_computation.11 | async-start | bytes 1638400 | tf_op jit(solution)/shard_map/reduce_scatter | solution.py:136
  143.8 4.7 %copy-start.4 = (bf16[16,4,40,640]{3,2,1,0:T(8,128)(2,1)S(1)}, bf16[16,4,40,640]{3,2,1,0:T(8,128)(2,1)}, u32[]{:S(2)}) copy-start(bf16[16,4,40,640]{3,2,1,0:T(8,128)(2,1)} %copy-done.3) | copy-start | bytes 9830404
  160.0 46.3 %copy-start.7 = (f32[2,1792]{1,0:T(2,128)S(1)}, f32[2,1792]{1,0:T(2,128)}, u32[]{:S(2)}) copy-start(f32[2,1792]{1,0:T(2,128)} %param.11) | copy-start | bytes 43012
  160.0 46.3 %copy-start.8 = (f32[2,1792]{1,0:T(2,128)S(1)}, f32[2,1792]{1,0:T(2,128)}, u32[]{:S(2)}) copy-start(f32[2,1792]{1,0:T(2,128)} %param.10) | copy-start | bytes 43012
  162.1 9.2 %all-to-all-start.4 = ((bf16[4,8,1792]{2,1,0:T(8,128)(2,1)}), bf16[4,8,1792]{2,1,0:T(8,128)(2,1)S(1)}, u32[]{:S(2)}, u32[]{:S(2)}) async-start(bf16[4,8,1792]{2,1,0:T(8,128)(2,1)} %bitcast.18), calls=%async_computation.5 | async-start | bytes 229376 | tf_op jit(solution)/shard_map/all_to_all | solution.py:139
  171.9 21.7 %all-to-all-start.5 = ((bf16[4,8,1792]{2,1,0:T(8,128)(2,1)}), bf16[4,8,1792]{2,1,0:T(8,128)(2,1)S(1)}, u32[]{:S(2)}, u32[]{:S(2)}) async-start(bf16[4,8,1792]{2,1,0:T(8,128)(2,1)} %broadcast_in_dim.23), calls=%async_computation.6 | async-start | bytes 229376 | tf_op jit(solution)/shard_map/all_to_all | solution.py:56
  180.4 36.9 %all-gather.5.cloned.1.call-start = ((), (), s32[]{:S(2)}) async-start(), calls=%async_computation.12 | async-start | bytes 1638400 | tf_op jit(solution)/shard_map/all_gather | solution.py:147
  202.0 25.4 %copy-start.5 = (bf16[20,1792]{1,0:T(8,128)(2,1)S(1)}, bf16[20,1792]{1,0:T(8,128)(2,1)}, u32[]{:S(2)}) copy-start(bf16[20,1792]{1,0:T(8,128)(2,1)} %param.8) | copy-start | bytes 215044
  202.7 10.1 %all-to-all-start.7 = ((bf16[4,16,1792]{2,1,0:T(8,128)(2,1)}), bf16[4,16,1792]{2,1,0:T(8,128)(2,1)S(1)}, u32[]{:S(2)}, u32[]{:S(2)}) async-start(bf16[4,16,1792]{2,1,0:T(8,128)(2,1)} %broadcast_in_dim.52), calls=%async_computation.8 | async-start | bytes 458752 | tf_op jit(solution)/shard_map/all_to_all | solution.py:56
  213.7 13.7 %all-to-all-start.8 = ((bf16[4,64,1792]{2,1,0:T(8,128)(2,1)}), bf16[4,64,1792]{2,1,0:T(8,128)(2,1)S(1)}, u32[]{:S(2)}, u32[]{:S(2)}) async-start(bf16[4,64,1792]{2,1,0:T(8,128)(2,1)} %broadcast_in_dim.54), calls=%async_computation.9 | async-start | bytes 1835008 | tf_op jit(solution)/shard_map/all_to_all | solution.py:56
Sparse Core Ops, SparseCore 0:
  28.4 96.0 all-gather.2
  160.1 23.0 reduce-scatter.1
  185.3 31.0 all-gather.4

commit v10 on v9

--- a/solution.py
+++ b/solution.py
@@ -41,7 +41,7 @@
         ],
         out_specs=pl.BlockSpec((count, block), lambda i: (0, i)),
         out_shape=jax.ShapeDtypeStruct((count, width), jnp.bfloat16),
-        compiler_params=pltpu.CompilerParams(vmem_limit_bytes=16 * 1024 * 1024),
+        compiler_params=pltpu.CompilerParams(vmem_limit_bytes=56 * 1024 * 1024),
         cost_estimate=pl.CostEstimate(
             flops=2 * count * depth * width,
             bytes_accessed=2 * (depth * width + count * (depth + 2 * width)),

time: 236 us -> 239 us (1.013)
  the two profiles are of different devices: /device:TPU:2 before, /device:TPU:32 now
where the time goes in v10:
time: 239 us; the launch traced here: 238 us
  waiting for transfers between devices  68.8 us (29%)
  blocking collectives  61.7 us (26%)
  starting transfers between devices  50.2 us (21%)
  matrix products  14.7 us (6%)
  between operations  14.1 us (6%)
  local copies, waits for them, and re-layouts  11.3 us (5%)
  other arithmetic  10.9 us (5%)
  Pallas kernels  6.14 us (3%)
    all_gather x1, blocking collectives, local(): line = lax.all_gather(second, 'dp', axis=0)  45.7 us
    all_to_all x5, waiting for transfers between devices, spread(): lax.all_to_all(copies, axis, 0, 0, tiled=True, axis_index_groups=groups)  34 us
    all_to_all x5, starting transfers between devices, spread(): lax.all_to_all(copies, axis, 0, 0, tiled=True, axis_index_groups=groups)  25.9 us
    all_to_all x2, blocking collectives, spread(): lax.all_to_all(copies, axis, 0, 0, tiled=True, axis_index_groups=groups)  15.9 us
    ppermute x2, waiting for transfers between devices, ring_permutes(): lax.ppermute(x, axis, behind)  13.3 us
    ppermute x2, starting transfers between devices, ring_permutes(): lax.ppermute(x, axis, ahead)  10.3 us
    all_to_all x1, waiting for transfers between devices, local(): lax.all_to_all(grad_part.reshape(inner, outer * share, width), 'fsdp', 0,...  9.29 us
    dot_general x2, matrix products, local(): lax.dot_general(g, w, (((1,), (1,)), ((), ())), preferred_element_type=f32)  7.15 us
  transfers between devices with their start and end apart: 14, of which 11 were waited for; matrix products, arithmetic and copies ran while one was open for 11% of the time, Pallas kernels for 3%

profile of v10, /device:TPU:32, one launch (start us, length us, event | category | flops | bytes accessed | tf_op | source)
XLA Modules:
  0.0 237.9 jit_solution(3747855815496672941)
XLA Ops:
  9.8 7.1 %all-to-all-start = ((bf16[8,20,1216]{2,1,0:T(8,128)(2,1)}), bf16[8,20,1216]{2,1,0:T(8,128)(2,1)S(1)}, u32[]{:S(2)}, u32[]{:S(2)}) async-start(bf16[8,20,1216]{2,1,0:T(8,128)(2,1)} %broadcast_in_dim.20), calls=%async_computation | async-start | bytes 983040 | tf_op jit(solution)/shard_map/all_to_all | solution.py:56
  18.5 9.6 %all-to-all-done = bf16[8,20,1216]{2,1,0:T(8,128)(2,1)S(1)} async-done(((bf16[8,20,1216]{2,1,0:T(8,128)(2,1)}), bf16[8,20,1216]{2,1,0:T(8,128)(2,1)S(1)}, u32[]{:S(2)}, u32[]{:S(2)}) %all-to-all-start) | async-done | bytes 389152 | tf_op jit(solution)/shard_map/all_to_all | solution.py:56
  29.2 8.0 %all_to_all.45 = bf16[2,20,640]{2,1,0:T(8,128)(2,1)S(1)} all-to-all(bf16[2,20,640]{2,1,0:T(8,128)(2,1)S(1)} %broadcast_in_dim.22), channel_id=1, replica_groups={{0,4},{8,12},{16,20},{24,28},{1,5},{9,13},{17,21},{25,29},{2,6},{10,14}..., dimensions={0} | all-to-all | bytes 102400 | tf_op jit(solution)/shard_map/all_to_all | solution.py:56
  37.2 45.7 %all_gather.10 = bf16[16,40,640]{2,1,0:T(8,128)(2,1)S(1)} all-gather(bf16[1,40,640]{2,1,0:T(8,128)(2,1)S(1)} %all_gather_reshape.3), channel_id=1, replica_groups=mesh['dp'=16,'fsdp'=8,'tensor'=4] {'dp'}, dimensions={0}, use_global_device_ids=true | all-gather | bytes 870400 | tf_op jit(solution)/shard_map/all_gather | solution.py:104
  82.9 1.9 collective-permute-start.2
  84.8 5.1 %collective-permute-start = (bf16[16,40,640]{2,1,0:T(8,128)(2,1)S(1)}, bf16[16,40,640]{2,1,0:T(8,128)(2,1)S(1)}, u32[]{:S(2)}, u32[]{:S(2)}) collective-permute-start(bf16[16,40,640]{2,1,0:T(8,128)(2,1)S(1)} %all_gather.10), channel_id=1, source_target_pairs={{8,0},{12,4},{16,8},{20,12},{24,16},{28,20},{0,24},{4,28},{9,1},{1... | collective-permute-start | bytes 2457608 | tf_op jit(solution)/shard_map/ppermute | solution.py:63
  90.0 10.9 %collective-permute-done.2 = bf16[16,40,640]{2,1,0:T(8,128)(2,1)S(1)} collective-permute-done((bf16[16,40,640]{2,1,0:T(8,128)(2,1)S(1)}, bf16[16,40,640]{2,1,0:T(8,128)(2,1)S(1)}, u32[]{:S(2)}, u32[]{:S(2)}) %collective-permute-start.2) | collective-permute-done | bytes 819232 | tf_op jit(solution)/shard_map/ppermute | solution.py:63
  101.7 1.9 collective-permute-start.3
  104.4 5.1 %collective-permute-start.1 = (bf16[8,40,640]{2,1,0:T(8,128)(2,1)}, bf16[8,40,640]{2,1,0:T(8,128)(2,1)}, u32[]{:S(2)}, u32[]{:S(2)}) collective-permute-start(bf16[8,40,640]{2,1,0:T(8,128)(2,1)} %slice.48), channel_id=1, source_target_pairs={{8,0},{12,4},{16,8},{20,12},{24,16},{28,20},{0,24},{4,28},{9,1},{1... | collective-permute-start | bytes 1228808 | tf_op jit(solution)/shard_map/ppermute | solution.py:63
  110.6 2.4 collective-permute-done.3
  112.9 2.4 collective-permute-done.1
  118.6 1.9 multiply_convert_fusion
  120.5 2.6 %all-gather.3.cloned.1.call-done.weight_ref = bf16[2560,1280]{1,0:T(8,128)(2,1)} async-done(((bf16[160,1280]{1,0:T(8,128)(2,1)}), bf16[2560,1280]{1,0:T(8,128)(2,1)}) %all-gather.3.cloned.1.call-update) | async-done | bytes 6553616 | tf_op jit(solution)/shard_map/all_gather | solution.py:101
  123.2 2.1 convolution_convert_fusion.2
  125.9 3.3 %all-to-all-start.1 = ((bf16[4,64,256]{2,1,0:T(8,128)(2,1)}), bf16[4,64,256]{2,1,0:T(8,128)(2,1)S(1)}, u32[]{:S(2)}, u32[]{:S(2)}) async-start(bf16[4,64,256]{2,1,0:T(8,128)(2,1)} %broadcast_in_dim.21), calls=%async_computation.1 | async-start | bytes 262144 | tf_op jit(solution)/shard_map/all_to_all | solution.py:56
  129.2 6.1 %shard_map.93 = bf16[256,1152]{1,0:T(8,128)(2,1)} custom-call(bf16[256,2560]{1,0:T(8,128)(2,1)} %tokens_ref.1, bf16[2560,1280]{1,0:T(8,128)(2,1)} %all-gather.3.cloned.1.call-done.weight_ref, bf16[256,1792]{1,0:T(8,128)(2,1)} %cotangent_ref.1), custom_call_target="tpu_custom_call" | custom-call | flops 1509949440 | bytes 8388608 | tf_op jit(solution)/shard_map/pallas_call | solution.py:34
  139.1 5.6 %all-to-all-start.3 = ((bf16[8,32,1792]{2,1,0:T(8,128)(2,1)}), bf16[8,32,1792]{2,1,0:T(8,128)(2,1)}, u32[]{:S(2)}, u32[]{:S(2)}) async-start(bf16[8,32,1792]{2,1,0:T(8,128)(2,1)} %bitcast.81), calls=%async_computation.3 | async-start | bytes 1835008 | tf_op jit(solution)/shard_map/all_to_all | solution.py:134
  144.8 4.8 %fusion = f32[256,2560]{1,0:T(8,128)S(1)} fusion(bf16[256,1152]{1,0:T(8,128)(2,1)} %shard_map.93, bf16[2560,1280]{1,0:T(8,128)(2,1)} %all-gather.3.cloned.1.call-done.weight_ref), kind=kOutput, calls=%fused_computation | convolution fusion | flops 1509949440 | bytes 9109504 | tf_op jit(solution)/shard_map/dot_general | solution.py:130
  149.6 2.4 fusion.2
  151.9 9.3 %all-to-all-done.3 = bf16[8,32,1792]{2,1,0:T(8,128)(2,1)} async-done(((bf16[8,32,1792]{2,1,0:T(8,128)(2,1)}), bf16[8,32,1792]{2,1,0:T(8,128)(2,1)}, u32[]{:S(2)}, u32[]{:S(2)}) %all-to-all-start.3) | async-done | bytes 917536 | tf_op jit(solution)/shard_map/all_to_all | solution.py:134
  162.6 2.0 reduce_sum.33
  164.6 4.7 %all-to-all-start.4 = ((bf16[4,8,1792]{2,1,0:T(8,128)(2,1)}), bf16[4,8,1792]{2,1,0:T(8,128)(2,1)S(1)}, u32[]{:S(2)}, u32[]{:S(2)}) async-start(bf16[4,8,1792]{2,1,0:T(8,128)(2,1)} %bitcast.18), calls=%async_computation.5 | async-start | bytes 229376 | tf_op jit(solution)/shard_map/all_to_all | solution.py:139
  169.5 4.8 %all-to-all-done.4 = bf16[4,8,1792]{2,1,0:T(8,128)(2,1)S(1)} async-done(((bf16[4,8,1792]{2,1,0:T(8,128)(2,1)}), bf16[4,8,1792]{2,1,0:T(8,128)(2,1)S(1)}, u32[]{:S(2)}, u32[]{:S(2)}) %all-to-all-start.4) | async-done | bytes 114720 | tf_op jit(solution)/shard_map/all_to_all | solution.py:139
  175.0 7.9 %all-to-all-start.5 = ((bf16[4,8,1792]{2,1,0:T(8,128)(2,1)}), bf16[4,8,1792]{2,1,0:T(8,128)(2,1)S(1)}, u32[]{:S(2)}, u32[]{:S(2)}) async-start(bf16[4,8,1792]{2,1,0:T(8,128)(2,1)} %broadcast_in_dim.23), calls=%async_computation.6 | async-start | bytes 229376 | tf_op jit(solution)/shard_map/all_to_all | solution.py:56
  182.9 2.4 reduce-scatter.2.cloned.1.call-done
  185.3 11.5 %all-to-all-done.5 = bf16[4,8,1792]{2,1,0:T(8,128)(2,1)S(1)} async-done(((bf16[4,8,1792]{2,1,0:T(8,128)(2,1)}), bf16[4,8,1792]{2,1,0:T(8,128)(2,1)S(1)}, u32[]{:S(2)}, u32[]{:S(2)}) %all-to-all-start.5) | async-done | bytes 114720 | tf_op jit(solution)/shard_map/all_to_all | solution.py:56
  197.1 8.0 %all_to_all.46 = bf16[2,8,1792]{2,1,0:T(8,128)(2,1)S(1)} all-to-all(bf16[2,8,1792]{2,1,0:T(8,128)(2,1)S(1)} %broadcast_in_dim.50), channel_id=1, replica_groups={{0,4},{8,12},{16,20},{24,28},{1,5},{9,13},{17,21},{25,29},{2,6},{10,14}..., dimensions={0} | all-to-all | bytes 114688 | tf_op jit(solution)/shard_map/all_to_all | solution.py:56
  205.8 4.1 %all-to-all-start.7 = ((bf16[4,16,1792]{2,1,0:T(8,128)(2,1)}), bf16[4,16,1792]{2,1,0:T(8,128)(2,1)S(1)}, u32[]{:S(2)}, u32[]{:S(2)}) async-start(bf16[4,16,1792]{2,1,0:T(8,128)(2,1)} %broadcast_in_dim.52), calls=%async_computation.8 | async-start | bytes 458752 | tf_op jit(solution)/shard_map/all_to_all | solution.py:56
  210.6 5.2 %all-to-all-done.7 = bf16[4,16,1792]{2,1,0:T(8,128)(2,1)S(1)} async-done(((bf16[4,16,1792]{2,1,0:T(8,128)(2,1)}), bf16[4,16,1792]{2,1,0:T(8,128)(2,1)S(1)}, u32[]{:S(2)}, u32[]{:S(2)}) %all-to-all-start.7) | async-done | bytes 229408 | tf_op jit(solution)/shard_map/all_to_all | solution.py:56
  216.8 3.5 %all-to-all-start.8 = ((bf16[4,64,1792]{2,1,0:T(8,128)(2,1)}), bf16[4,64,1792]{2,1,0:T(8,128)(2,1)S(1)}, u32[]{:S(2)}, u32[]{:S(2)}) async-start(bf16[4,64,1792]{2,1,0:T(8,128)(2,1)} %broadcast_in_dim.54), calls=%async_computation.9 | async-start | bytes 1835008 | tf_op jit(solution)/shard_map/all_to_all | solution.py:56
  220.3 2.5 %broadcast_multiply_fusion = bf16[256,2560]{1,0:T(8,128)(2,1)} fusion(bf16[256,2560]{1,0:T(8,128)(2,1)} %all-gather.5.cloned.1.call-done, bf16[]{:T(256)} %constant.114.clone.1), kind=kLoop, calls=%fused_computation.23 | loop fusion | flops 655360 | bytes 2621442 | tf_op jit(solution)/shard_map/mul | solution.py:164
  222.8 7.7 %all-to-all-done.8 = bf16[4,64,1792]{2,1,0:T(8,128)(2,1)S(1)} async-done(((bf16[4,64,1792]{2,1,0:T(8,128)(2,1)}), bf16[4,64,1792]{2,1,0:T(8,128)(2,1)S(1)}, u32[]{:S(2)}, u32[]{:S(2)}) %all-to-all-start.8) | async-done | bytes 917536 | tf_op jit(solution)/shard_map/all_to_all | solution.py:56
  (71 shorter events, 21.5 us)
Async XLA Ops:
  7.2 22.0 %slice-start.1 = ((bf16[20,1792]{1,0:T(8,128)(2,1)}), bf16[20,640]{1,0:T(8,128)(2,1)S(1)}, s32[]{:S(2)}) async-start(bf16[20,1792]{1,0:T(8,128)(2,1)} %param.8), calls=%async_computation.14 | async-start | bytes 61440 | tf_op jit(solution)/shard_map/slice | solution.py:102
  9.8 99.7 %slice-start = ((bf16[256,1792]{1,0:T(8,128)(2,1)}), bf16[256,640]{1,0:T(8,128)(2,1)S(1)}, s32[]{:S(2)}) async-start(bf16[256,1792]{1,0:T(8,128)(2,1)} %cotangent_ref.1), calls=%async_computation.13 | async-start | bytes 655360 | tf_op jit(solution)/shard_map/slice | solution.py:121
  9.8 18.3 %all-to-all-start = ((bf16[8,20,1216]{2,1,0:T(8,128)(2,1)}), bf16[8,20,1216]{2,1,0:T(8,128)(2,1)S(1)}, u32[]{:S(2)}, u32[]{:S(2)}) async-start(bf16[8,20,1216]{2,1,0:T(8,128)(2,1)} %broadcast_in_dim.20), calls=%async_computation | async-start | bytes 983040 | tf_op jit(solution)/shard_map/all_to_all | solution.py:56
  16.9 106.2 %all-gather.3.cloned.1.call-start = ((), (), s32[]{:S(2)}) async-start(), calls=%async_computation.10 | async-start | bytes 6963200 | tf_op jit(solution)/shard_map/all_gather | solution.py:101
  82.9 18.0 %collective-permute-start.2 = (bf16[16,40,640]{2,1,0:T(8,128)(2,1)S(1)}, bf16[16,40,640]{2,1,0:T(8,128)(2,1)S(1)}, u32[]{:S(2)}, u32[]{:S(2)}) collective-permute-start(bf16[16,40,640]{2,1,0:T(8,128)(2,1)S(1)} %all_gather.10), channel_id=1, source_target_pairs={{0,8},{4,12},{8,16},{12,20},{16,24},{20,28},{24,0},{28,4},{1,9},{5... | collective-permute-start | bytes 2457608 | tf_op jit(solution)/shard_map/ppermute | solution.py:63
  84.8 18.8 %collective-permute-start = (bf16[16,40,640]{2,1,0:T(8,128)(2,1)S(1)}, bf16[16,40,640]{2,1,0:T(8,128)(2,1)S(1)}, u32[]{:S(2)}, u32[]{:S(2)}) collective-permute-start(bf16[16,40,640]{2,1,0:T(8,128)(2,1)S(1)} %all_gather.10), channel_id=1, source_target_pairs={{8,0},{12,4},{16,8},{20,12},{24,16},{28,20},{0,24},{4,28},{9,1},{1... | collective-permute-start | bytes 2457608 | tf_op jit(solution)/shard_map/ppermute | solution.py:63
  101.7 11.3 %collective-permute-start.3 = (bf16[8,40,640]{2,1,0:T(8,128)(2,1)}, bf16[8,40,640]{2,1,0:T(8,128)(2,1)S(1)}, u32[]{:S(2)}, u32[]{:S(2)}) collective-permute-start(bf16[8,40,640]{2,1,0:T(8,128)(2,1)} %slice.49), channel_id=1, source_target_pairs={{0,8},{4,12},{8,16},{12,20},{16,24},{20,28},{24,0},{28,4},{1,9},{5... | collective-permute-start | bytes 1228808 | tf_op jit(solution)/shard_map/ppermute | solution.py:63
  104.4 10.9 %collective-permute-start.1 = (bf16[8,40,640]{2,1,0:T(8,128)(2,1)}, bf16[8,40,640]{2,1,0:T(8,128)(2,1)}, u32[]{:S(2)}, u32[]{:S(2)}) collective-permute-start(bf16[8,40,640]{2,1,0:T(8,128)(2,1)} %slice.48), channel_id=1, source_target_pairs={{8,0},{12,4},{16,8},{20,12},{24,16},{28,20},{0,24},{4,28},{9,1},{1... | collective-permute-start | bytes 1228808 | tf_op jit(solution)/shard_map/ppermute | solution.py:63
  117.2 1.3 copy-start
  117.2 1.4 copy-start.3
  125.9 9.5 %all-to-all-start.1 = ((bf16[4,64,256]{2,1,0:T(8,128)(2,1)}), bf16[4,64,256]{2,1,0:T(8,128)(2,1)S(1)}, u32[]{:S(2)}, u32[]{:S(2)}) async-start(bf16[4,64,256]{2,1,0:T(8,128)(2,1)} %broadcast_in_dim.21), calls=%async_computation.1 | async-start | bytes 262144 | tf_op jit(solution)/shard_map/all_to_all | solution.py:56
  139.1 22.1 %all-to-all-start.3 = ((bf16[8,32,1792]{2,1,0:T(8,128)(2,1)}), bf16[8,32,1792]{2,1,0:T(8,128)(2,1)}, u32[]{:S(2)}, u32[]{:S(2)}) async-start(bf16[8,32,1792]{2,1,0:T(8,128)(2,1)} %bitcast.81), calls=%async_computation.3 | async-start | bytes 1835008 | tf_op jit(solution)/shard_map/all_to_all | solution.py:134
  144.7 40.5 %reduce-scatter.2.cloned.1.call-start = ((), (), s32[]{:S(2)}) async-start(), calls=%async_computation.11 | async-start | bytes 1638400 | tf_op jit(solution)/shard_map/reduce_scatter | solution.py:136
  144.8 4.8 %copy-start.1 = (bf16[256,640]{0,1:T(8,128)(2,1)S(1)}, bf16[256,640]{0,1:T(8,128)(2,1)}, u32[]{:S(2)}) copy-start(bf16[256,640]{0,1:T(8,128)(2,1)} %multiply_convert_fusion) | copy-start | bytes 983044
  161.3 48.6 %copy-start.4 = (f32[2,1792]{1,0:T(2,128)S(1)}, f32[2,1792]{1,0:T(2,128)}, u32[]{:S(2)}) copy-start(f32[2,1792]{1,0:T(2,128)} %param.11) | copy-start | bytes 43012
  161.3 48.6 %copy-start.5 = (f32[2,1792]{1,0:T(2,128)S(1)}, f32[2,1792]{1,0:T(2,128)}, u32[]{:S(2)}) copy-start(f32[2,1792]{1,0:T(2,128)} %param.10) | copy-start | bytes 43012
  164.6 9.7 %all-to-all-start.4 = ((bf16[4,8,1792]{2,1,0:T(8,128)(2,1)}), bf16[4,8,1792]{2,1,0:T(8,128)(2,1)S(1)}, u32[]{:S(2)}, u32[]{:S(2)}) async-start(bf16[4,8,1792]{2,1,0:T(8,128)(2,1)} %bitcast.18), calls=%async_computation.5 | async-start | bytes 229376 | tf_op jit(solution)/shard_map/all_to_all | solution.py:139
  175.0 21.8 %all-to-all-start.5 = ((bf16[4,8,1792]{2,1,0:T(8,128)(2,1)}), bf16[4,8,1792]{2,1,0:T(8,128)(2,1)S(1)}, u32[]{:S(2)}, u32[]{:S(2)}) async-start(bf16[4,8,1792]{2,1,0:T(8,128)(2,1)} %broadcast_in_dim.23), calls=%async_computation.6 | async-start | bytes 229376 | tf_op jit(solution)/shard_map/all_to_all | solution.py:56
  182.9 37.4 %all-gather.5.cloned.1.call-start = ((), (), s32[]{:S(2)}) async-start(), calls=%async_computation.12 | async-start | bytes 1638400 | tf_op jit(solution)/shard_map/all_gather | solution.py:147
  205.1 25.4 %copy-start.2 = (bf16[20,1792]{1,0:T(8,128)(2,1)S(1)}, bf16[20,1792]{1,0:T(8,128)(2,1)}, u32[]{:S(2)}) copy-start(bf16[20,1792]{1,0:T(8,128)(2,1)} %param.8) | copy-start | bytes 215044
  205.8 10.0 %all-to-all-start.7 = ((bf16[4,16,1792]{2,1,0:T(8,128)(2,1)}), bf16[4,16,1792]{2,1,0:T(8,128)(2,1)S(1)}, u32[]{:S(2)}, u32[]{:S(2)}) async-start(bf16[4,16,1792]{2,1,0:T(8,128)(2,1)} %broadcast_in_dim.52), calls=%async_computation.8 | async-start | bytes 458752 | tf_op jit(solution)/shard_map/all_to_all | solution.py:56
  216.8 13.7 %all-to-all-start.8 = ((bf16[4,64,1792]{2,1,0:T(8,128)(2,1)}), bf16[4,64,1792]{2,1,0:T(8,128)(2,1)S(1)}, u32[]{:S(2)}, u32[]{:S(2)}) async-start(bf16[4,64,1792]{2,1,0:T(8,128)(2,1)} %broadcast_in_dim.54), calls=%async_computation.9 | async-start | bytes 1835008 | tf_op jit(solution)/shard_map/all_to_all | solution.py:56
Sparse Core Ops, SparseCore 0:
  29.3 93.8 all-gather.2
  161.4 23.8 reduce-scatter.1
  187.4 31.2 all-gather.4
